TPU v7x, 32 devices: a whole 2x2x4 slice. The times are simulated.
32 devices in a mesh: dp: 4 (over z), freq: 8 (over y, x, core).
Axes of the slice: x: 2, y: 2, z: 4, core: 2. Of those that a mesh axis runs over, the one named last changes fastest.
Arguments:
- tokens: bfloat16 [8, 2048, 768], P('dp', 'freq'), may hold values from -6 to 6
- offsets: int32 [8], P('dp'), may hold values from 0 to 1023, as said below
- kernel_lengths: int32 [768], replicated, may hold values from 512 to 2048, as said below
- norm1_gain: float32 [768], replicated, may hold values from 0.5 to 1.5
- norm1_bias: float32 [768], replicated, may hold values from -3 to 3
- input_projection_weight: bfloat16 [768, 2304], replicated, may hold values from -0.21875 to 0.21875
- in_bias: float32 [2304], replicated, may hold values from -2 to 2
- kernel_taps: float32 [768, 2048], P(None, 'freq'), may hold values from -0.25 to 0.25
- skip_gain: float32 [768], P('freq'), may hold values from -3 to 3
- out_weight: bfloat16 [768, 768], replicated, may hold values from -0.21875 to 0.21875
- out_bias: float32 [768], replicated, may hold values from -2 to 2
- norm2_gain: float32 [768], replicated, may hold values from 0.5 to 1.5
- norm2_bias: float32 [768], replicated, may hold values from -3 to 3
- up_projection_weight: bfloat16 [768, 3072], replicated, may hold values from -0.21875 to 0.21875
- fc1_bias: float32 [3072], replicated, may hold values from -2 to 2
- down_projection_weight: bfloat16 [3072, 768], replicated, may hold values from -0.109375 to 0.109375
- fc2_bias: float32 [768], replicated, may hold values from -2 to 2
- cotangent: bfloat16 [8, 2048, 768], P('dp', 'freq'), may hold values from -6 to 6
Outputs:
- block_out: bfloat16 [8, 2048, 768], P('dp', 'freq')
- input_grad: bfloat16 [8, 2048, 768], P('dp', 'freq')
- norm1_gain_grad: float32 [768], P('freq')
- norm1_bias_grad: float32 [768], P('freq')
- in_weight_grad: float32 [768, 2304], P('dp', 'freq')
- in_bias_grad: float32 [2304], P('freq')
- kernel_taps_grad: float32 [768, 2048], P(None, 'freq')
- skip_grad: float32 [768], P('freq')
- out_weight_grad: float32 [768, 768], P('dp', 'freq')
- out_bias_grad: float32 [768], P('freq')
- norm2_gain_grad: float32 [768], P('freq')
- norm2_bias_grad: float32 [768], P('freq')
- fc1_weight_grad: float32 [768, 3072], P('dp', 'freq')
- fc1_bias_grad: float32 [3072], P('freq')
- fc2_weight_grad: float32 [3072, 768], P('dp', 'freq')
- fc2_bias_grad: float32 [768], P('freq')
Inputs may be any that keep to these rules, and one draw needn't show every extreme that they name: `offsets`: in every run of 2 consecutive sequences (those of one index of dp) at least one has offset 0; some sequence has offset 2048 / 2 - 1. `kernel_lengths`: at least one channel's kernel has all 2048 taps.
All inputs are finite; a program needn't handle non-finite values.
Results may differ from a plain program's by a relative error of at most 0.018.
Values may be sent and summed in bfloat16 or wider, within the bound.
No kernel may reach another device: no remote copies, remote signals or barrier semaphores. Data moves between devices by JAX's collectives and lax.ppermute only.
A program may use at most 192 MiB of HBM per device.

v0:
```python
import functools

import jax
import jax.numpy as jnp
import numpy as np
from jax import lax
from jax.experimental import pallas as pl
from jax.experimental.pallas import tpu as pltpu
from jax.sharding import PartitionSpec as P

NORM_EPS = 1e-05
SHRINK = 0.003
GELU_C = 0.7978845608028654
GELU_A = 0.044715
F32 = jnp.float32
BF16 = jnp.bfloat16
MIB = 1 << 20

NN = (((1,), (0,)), ((), ()))
NT = (((1,), (1,)), ((), ()))


def mm(left, right, dims=NN):
    return lax.dot_general(left, right, dims, preferred_element_type=F32)


def whole(dims):
    return pl.BlockSpec(tuple(dims), lambda i: (0,) * len(dims))


def anywhere():
    return pl.BlockSpec(memory_space=pl.ANY)


def smem():
    return pl.BlockSpec(memory_space=pltpu.SMEM)


def shape(dims, dtype):
    return jax.ShapeDtypeStruct(dims, dtype)


def launch(kernel, grid, ins, in_specs, outs, out_specs, scratch, estimate, name, after=(), carry=()):
    count, extra, given = len(ins), len(after) + len(carry), len(outs)

    def run(*refs):
        made = refs[count + extra : count + extra + given]
        kernel(*refs[:count], *made, *refs[count + extra + given + len(carry) :])

    first = count + len(after)
    results = pl.pallas_call(
        run,
        grid=grid,
        out_shape=tuple(outs) + tuple(shape(v.shape, v.dtype) for v in carry),
        in_specs=list(in_specs) + [anywhere()] * extra,
        out_specs=tuple(out_specs) + (anywhere(),) * len(carry),
        scratch_shapes=scratch,
        input_output_aliases={first + k: given + k for k in range(len(carry))},
        compiler_params=pltpu.CompilerParams(vmem_limit_bytes=60 * MIB, dimension_semantics=("arbitrary",)),
        cost_estimate=estimate,
        name=name,
    )(*ins, *after, *carry)
    made = results[0] if given == 1 else results[:given]
    return (made, results[given:]) if carry else made


def cost(flops, moved, special=0):
    return pl.CostEstimate(flops=int(flops) * 64, bytes_accessed=int(moved) * 64, transcendentals=0)


def split16(table):
    high = np.asarray(table, np.float32).astype(jnp.bfloat16)
    low = (np.asarray(table, np.float64) - high.astype(np.float64)).astype(np.float32).astype(jnp.bfloat16)
    return high, low


@functools.lru_cache(maxsize=None)
def tables(width):
    order = np.concatenate([np.arange(0, width, 2), np.arange(1, width, 2)])
    turns = (2 * order[None, :] + 1) * np.arange(width)[:, None] % (4 * width)
    angle = np.pi * turns / (2 * width)
    forward = np.concatenate([np.cos(angle), -np.sin(angle)], axis=1)
    inverse = forward.T / width
    return split16(forward) + split16(inverse)


def split_value(value):
    high = value.astype(BF16)
    return high, (value - high.astype(F32)).astype(BF16)


def spectrum_of(block, fhi, flo):
    return mm(block, fhi) + mm(block, flo)


def signal_of(spec, ghi, glo):
    high, low = split_value(spec)
    return mm(high, ghi) + (mm(low, ghi) + mm(high, glo))


def each(count, step, unroll):
    if unroll:
        for i in range(count):
            step(i)
    else:
        lax.fori_loop(0, count, lambda i, c: (step(i), c)[1], 0)


def blocks_to_spectra(x_ref, spec_ref, fhi, flo, batch, width):
    count, chans = x_ref.shape[0], x_ref.shape[1]
    for b in range(batch):
        lanes = slice(b * width, (b + 1) * width)
        if chans % 16 == 0:
            rows = x_ref[:, :, lanes].reshape(count * chans, width)
            spec_ref[b] = spectrum_of(rows, fhi[...], flo[...]).reshape(count, chans, 2 * width)
        else:

            def step(j, b=b, lanes=lanes):
                spec_ref[b, j] = spectrum_of(x_ref[j, :, lanes], fhi[...], flo[...])

            each(count, step, False)


def tiles(chans, width, step):
    lane_tiles = width // 128

    def rows_step(rt):
        start = rt * 8 if isinstance(rt, int) else pl.multiple_of(rt * 8, 8)
        for lane in range(lane_tiles):
            step(pl.ds(start, 8), lane)

    each(chans // 8, rows_step, False)


def pair(ref, lead, rows, lane, width):
    return (
        ref[lead + (rows, slice(lane * 128, (lane + 1) * 128))],
        ref[lead + (rows, slice(width + lane * 128, width + (lane + 1) * 128))],
    )


def put_pair(ref, lead, rows, lane, width, value):
    ref[lead + (rows, slice(lane * 128, (lane + 1) * 128))] = value[0]
    ref[lead + (rows, slice(width + lane * 128, width + (lane + 1) * 128))] = value[1]


def times(a, k):
    return a[0] * k[0] - a[1] * k[1], a[0] * k[1] + a[1] * k[0]


def times_conj(a, k):
    return a[0] * k[0] + a[1] * k[1], a[1] * k[0] - a[0] * k[1]


def plus(a, b):
    return b if a is None else (a[0] + b[0], a[1] + b[1])


def quarter(now, before, sign):
    if before is None:
        return now
    if sign > 0:
        return now[0] - before[1], now[1] + before[0]
    return now[0] + before[1], now[1] - before[0]


def wide_quarter(now, before, width):
    lane = lax.broadcasted_iota(jnp.int32, (1, width), 1)
    sign = jnp.where(lane < width // 2, 1.0, -1.0)
    return jnp.concatenate(
        [now[:, :width] - sign * before[:, width:], now[:, width:] + sign * before[:, :width]], axis=1
    )


def wide_times(a, k, width, conj):
    ar, ai, kr, ki = a[:, :width], a[:, width:], k[:, :width], k[:, width:]
    if conj:
        return jnp.concatenate([ar * kr + ai * ki, ai * kr - ar * ki], axis=1)
    return jnp.concatenate([ar * kr - ai * ki, ar * ki + ai * kr], axis=1)


UNROLLED = 8


def small(count, chans, width):
    return count <= UNROLLED and chans % 16 == 0 and width % 256 == 0


def conv_products(spec_ref, k_ref, z_ref, batch, width, adjoint):
    reach, chans = k_ref.shape[0], k_ref.shape[1]
    count = spec_ref.shape[1]
    if small(count, chans, width):

        def step(rows, lane):
            k = [pair(k_ref, (d,), rows, lane, width) for d in range(reach)]
            for b in range(batch):
                x = [pair(spec_ref, (b, j), rows, lane, width) for j in range(count)]
                for i in range(count):
                    total = None
                    if adjoint:
                        for d in range(min(count - i, reach)):
                            total = plus(total, times_conj(x[i + d], k[d]))
                    else:
                        for d in range(min(i + 1, reach)):
                            total = plus(total, times(x[i - d], k[d]))
                    put_pair(z_ref, (b, i), rows, lane, width, total)

        tiles(chans, width, step)
        return
    for b in range(batch):

        def row(i, b=b):
            def term(d, total):
                src = i + d if adjoint else i - d
                return total + wide_times(spec_ref[b, src], k_ref[d], width, adjoint)

            terms = jnp.minimum(count - i if adjoint else i + 1, reach)
            z_ref[b, i] = lax.fori_loop(0, terms, term, jnp.zeros((chans, 2 * width), F32))

        each(count, row, False)


def conv_body(adjoint, batch, x_ref, k_ref, skip_ref, fhi, flo, ghi, glo, out_ref, spec_ref, z_ref):
    count, chans = x_ref.shape[:2]
    width = fhi.shape[0]
    blocks_to_spectra(x_ref, spec_ref, fhi, flo, batch, width)
    conv_products(spec_ref, k_ref, z_ref, batch, width, adjoint)
    for b in range(batch):
        cut = slice(b * width, (b + 1) * width)
        if chans % 16 == 0:
            y = signal_of(z_ref[b].reshape(count * chans, 2 * width), ghi[...], glo[...])
            y = y.reshape(count, chans, width) + skip_ref[...][None] * x_ref[:, :, cut].astype(F32)
            out_ref[:, :, cut] = y.astype(BF16)
        else:

            def step(j, b=b, cut=cut):
                y = signal_of(z_ref[b, j], ghi[...], glo[...])
                out_ref[j, :, cut] = (y + skip_ref[...] * x_ref[j, :, cut].astype(F32)).astype(BF16)

            each(count, step, False)


def forward_kernel(batch, x_ref, s_ref, len_ref, skip_ref, fhi, flo, ghi, glo, out_ref, k_ref, spec_ref, z_ref, raw_ref):
    taps_spectra(s_ref, s_ref.shape[2] - fhi.shape[0], len_ref, fhi, flo, k_ref, raw_ref)
    conv_body(False, batch, x_ref, k_ref, skip_ref, fhi, flo, ghi, glo, out_ref, spec_ref, z_ref)


def forward_call(x, batch, width, taps, lens, skip, after=(), carry=()):
    count, chans = x.shape[:2]
    reach = taps.shape[0]
    tabs = tables(width)
    spec = pltpu.VMEM((batch, count, chans, 2 * width), F32)
    span = min(reach + 1, count)
    same = taps is x
    args = (x,) if same else (x, taps)

    def kernel(*refs):
        forward_kernel(batch, refs[0], *(refs if same else refs[1:]))

    return launch(
        kernel,
        (1,),
        (*args, lens, skip, *tabs),
        [whole(v.shape) for v in (*args, lens, skip, *tabs)],
        (shape((count, chans, batch * width), BF16), shape((span, chans, 2 * width), F32)),
        (whole((count, chans, batch * width)), whole((span, chans, 2 * width))),
        [spec, spec, pltpu.VMEM((reach, chans, 2 * width), F32)],
        cost(x.size * width * 20, x.size * 8 + 4 * width * width * 4),
        "conv_forward",
        after,
        carry,
    )


def adjoint_kernel(batch, *refs):
    conv_body(True, batch, *refs)


def adjoint_call(x, batch, k_spec, skip, after=(), carry=()):
    count, chans, lanes = x.shape
    width = k_spec.shape[2] // 2
    tabs = tables(width)
    spec = pltpu.VMEM((batch, count, chans, 2 * width), F32)
    return launch(
        functools.partial(adjoint_kernel, batch),
        (1,),
        (x, k_spec, skip, *tabs),
        [whole(v.shape) for v in (x, k_spec, skip, *tabs)],
        (shape(x.shape, BF16),),
        (whole(x.shape),),
        [spec, spec],
        cost(x.size * width * 20, x.size * 4 + k_spec.size * 4 + 4 * width * width * 4),
        "conv_adjoint",
        after,
        carry,
    )


def pooled_rows(full):
    span = full.shape[1]
    place = lax.broadcasted_iota(jnp.int32, (1, span), 1)
    before = jnp.where(place == 0, 0.0, pltpu.roll(full, 1, 1))
    after = jnp.where(place == span - 1, 0.0, pltpu.roll(full, span - 1, 1))
    return (before + full + after) / 3.0


def taps_spectra(s_ref, start, len_ref, fhi, flo, out_ref, raw_ref):
    count, chans = s_ref.shape[:2]
    width = fhi.shape[0]
    full = jnp.concatenate([s_ref[d, :, start : start + width].astype(F32) for d in range(count)], axis=1)
    place = lax.broadcasted_iota(jnp.int32, (1, count * width), 1)
    kernel = jnp.where(place < len_ref[...], pooled_rows(full), 0.0)
    for d in range(count):
        high, low = split_value(kernel[:, d * width : (d + 1) * width])
        raw_ref[d] = mm(high, fhi[...]) + (mm(low, fhi[...]) + mm(high, flo[...]))
    out_ref[0] = raw_ref[0]
    for d in range(1, count):
        out_ref[d] = wide_quarter(raw_ref[d], raw_ref[d - 1], width)
    if out_ref.shape[0] > count:
        out_ref[count] = wide_quarter(jnp.zeros((chans, 2 * width), F32), raw_ref[count - 1], width)


def taps_grad_kernel(x_ref, g_ref, len_ref, fhi, flo, ghi, glo, out_ref, skip_ref, xs_ref, gs_ref, z_ref):
    count, chans, lanes = g_ref.shape
    reach = out_ref.shape[0]
    width = fhi.shape[0]
    batch = lanes // width
    blocks_to_spectra(x_ref, xs_ref, fhi, flo, batch, width)
    blocks_to_spectra(g_ref, gs_ref, fhi, flo, batch, width)
    if small(count, chans, width):

        def step(rows, lane):
            sign = 1 if lane < width // 256 else -1
            total = [None] * reach
            for b in range(batch):
                x = [pair(xs_ref, (b, j), rows, lane, width) for j in range(count)]
                x = [quarter(x[j], x[j - 1] if j else None, sign) for j in range(count)]
                for i in range(count):
                    g = pair(gs_ref, (b, i), rows, lane, width)
                    for d in range(min(i + 1, reach)):
                        total[d] = plus(total[d], times_conj(g, x[i - d]))
            for d in range(reach):
                put_pair(z_ref, (d,), rows, lane, width, total[d])

        tiles(chans, width, step)
        rows = signal_of(z_ref[...].reshape(reach * chans, 2 * width), ghi[...], glo[...])
        rows = rows.reshape(reach, chans, width)
        pieces = [rows[d] for d in range(reach)]
    else:

        def shift(t, c):
            j = count - 1 - t
            for b in range(batch):
                xs_ref[b, j] = wide_quarter(xs_ref[b, j], xs_ref[b, j - 1], width)
            return c

        lax.fori_loop(0, count - 1, shift, 0)

        def lag(d):
            total = jnp.zeros((chans, 2 * width), F32)
            for b in range(batch):

                def term(i, acc, b=b):
                    return acc + wide_times(gs_ref[b, i], xs_ref[b, i - d], width, True)

                total = lax.fori_loop(d, count, term, total)
            z_ref[d] = total

        each(reach, lag, False)
        pieces = [signal_of(z_ref[d], ghi[...], glo[...]) for d in range(reach)]
    full = jnp.concatenate(pieces, axis=1)
    place = lax.broadcasted_iota(jnp.int32, (1, reach * width), 1)
    full = pooled_rows(jnp.where(place < len_ref[...], full, 0.0))
    for d in range(reach):
        out_ref[d] = full[:, d * width : (d + 1) * width].astype(BF16)
    dot = jnp.zeros((chans, lanes), F32)
    for j in range(count):
        dot = dot + x_ref[j, :, :lanes].astype(F32) * g_ref[j].astype(F32)
    skip_ref[...] = jnp.sum(dot, axis=1, keepdims=True)


def taps_grad_call(x, g, lens, width, reach, after=(), carry=()):
    count, chans, lanes = g.shape
    batch = lanes // width
    tabs = tables(width)
    spec = pltpu.VMEM((batch, count, chans, 2 * width), F32)
    return launch(
        taps_grad_kernel,
        (1,),
        (x, g, lens, *tabs,),
        [whole(v.shape) for v in (x, g, lens, *tabs)],
        (shape((reach, chans, width), BF16), shape((chans, 1), F32)),
        (whole((reach, chans, width)), whole((chans, 1))),
        [spec, spec, pltpu.VMEM((reach, chans, 2 * width), F32)],
        cost(x.size * width * 20, x.size * 6),
        "taps_gradient",
        after,
        carry,
    )


def normalized(values):
    centred = values - jnp.mean(values, axis=-1, keepdims=True)
    rate = lax.rsqrt(jnp.mean(centred * centred, axis=-1, keepdims=True) + NORM_EPS)
    return centred * rate, rate


def live_rows(offs_ref, batch, tok_rows, rows):
    row = lax.broadcasted_iota(jnp.int32, (rows, 1), 0)
    limit = jnp.zeros((rows, 1), jnp.int32)
    base = lax.axis_index("freq") * tok_rows
    position = base + row
    for b in range(batch):
        inside = jnp.logical_and(row >= b * tok_rows, row < (b + 1) * tok_rows)
        limit = jnp.where(inside, offs_ref[b] + b * tok_rows, limit)
    return position >= limit


def front_kernel(batch, tok_rows, offs_ref, tok, gain, bias, wv, wg, ws, bv, bg, bs, taps, normed, mixed, value, gate, second):
    rows = tok.shape[0]

    @pl.when(pl.program_id(0) == 0)
    def _():
        n, _ = normalized(tok[...].astype(F32))
        normed[...] = (n * gain[...].reshape(1, -1) + bias[...].reshape(1, -1)).astype(BF16)

    x = normed[...]
    v = mm(x, wv[...]) + bv[...]
    g = mm(x, wg[...]) + bg[...]
    live = live_rows(offs_ref, batch, tok_rows, rows)
    mixed[:, :rows] = jnp.where(live, g * v, 0.0).T.astype(BF16)
    t = taps[...]
    mixed[:, rows:] = (t - SHRINK * jnp.tanh(t / SHRINK)).astype(BF16)
    value[...] = jnp.where(live, v, 0.0).astype(BF16)
    gate[...] = jnp.where(live, g, 0.0).astype(BF16)
    second[...] = (mm(x, ws[...]) + bs[...]).astype(BF16)


def front_call(tok, offsets, gain, bias, weight, in_bias, taps, batch, tok_rows):
    rows, width = tok.shape
    span = rows + taps.shape[1]
    cut = 256
    per = width // cut

    def full(i):
        return (0, 0)

    def col(part):
        return lambda i: (0, part * per + i)

    act = shape((rows, width), BF16)
    return launch(
        functools.partial(front_kernel, batch, tok_rows),
        (per,),
        (offsets, tok, gain, bias, weight, weight, weight, in_bias, in_bias, in_bias, taps),
        [smem(), pl.BlockSpec((rows, width), full), whole((width,)), whole((width,))]
        + [pl.BlockSpec((width, cut), col(k)) for k in range(3)]
        + [pl.BlockSpec((1, cut), col(k)) for k in range(3)]
        + [pl.BlockSpec((cut, taps.shape[1]), lambda i: (i, 0))],
        (act, shape((width, span), BF16), act, act, act),
        (
            pl.BlockSpec((rows, width), full),
            pl.BlockSpec((cut, span), lambda i: (i, 0)),
            pl.BlockSpec((rows, cut), lambda i: (0, i)),
            pl.BlockSpec((rows, cut), lambda i: (0, i)),
            pl.BlockSpec((rows, cut), lambda i: (0, i)),
        ),
        [],
        cost(2 * rows * width * 3 * width, weight.size * 2 + rows * width * 12),
        "norm_project",
            )


def active_grad_kernel(freq_parts, cot, wdown, out, b2g, mine, other):
    @pl.when(pl.program_id(0) == 0)
    def _():
        c = cot[...].astype(F32)
        b2g[...] = jnp.sum(c, axis=0, keepdims=True)
        put_halves(c.T.astype(BF16), mine, other, 0, lax.rem(lax.axis_index("freq"), 2), freq_parts)

    out[...] = mm(cot[...], wdown[...], NT).astype(BF16)


def active_grad_call(cot, wdown, cut, freq_parts, after=(), carry=()):
    rows, width = cot.shape
    ff = wdown.shape[0]
    half = shape((width // 2, rows), BF16)
    return launch(
        functools.partial(active_grad_kernel, freq_parts),
        (ff // cut,),
        (cot, wdown),
        [pl.BlockSpec((rows, width), lambda i: (0, 0)), pl.BlockSpec((cut, width), lambda i: (i, 0))],
        (shape((rows, ff), BF16), shape((1, width), F32), half, half),
        (pl.BlockSpec((rows, cut), lambda i: (0, i)), whole((1, width)), whole(half.shape), whole(half.shape)),
        [],
        cost(2 * rows * width * ff, wdown.size * 2 + rows * ff * 2),
        "active_grad",
        after,
        carry,
    )


def gelu_parts(h):
    square = h * h
    t = jnp.tanh(GELU_C * h * (1.0 + GELU_A * square))
    half = 0.5 + 0.5 * t
    slope = half + (0.5 * GELU_C) * h * (1.0 - t * t) * (1.0 + (3.0 * GELU_A) * square)
    return h * half, slope


def mlp_kernel(paired, freq_parts, tok, convt, second, wo, ob, gain, bias, wup, b1, ag_ref, cot, pack, res, b1g, rgrad, convgt, sgrad, mine_t, other_t, vecs, *rest):
    mine, (n2, gn, conv, acc) = rest[:-4], rest[-4:]
    step = pl.program_id(0)
    cut, part = wup.shape[1], gn.shape[2]
    core = lax.rem(lax.axis_index("freq"), 2)

    @pl.when(step == 0)
    def _():
        c = convt[...].astype(F32).T
        conv[...] = c.astype(BF16)
        g = (second[...].astype(F32) * c).astype(BF16)
        r = tok[...].astype(F32) + (mm(g, wo[...]) + ob[...])
        res[...] = r
        n, _ = normalized(r)
        m = (n * gain[...] + bias[...]).astype(BF16)
        n2[...] = m
        both = [g, m]
        for k in range(gn.shape[0]):
            start = k * part
            gn[k] = both[start // g.shape[1]][:, start % g.shape[1] : start % g.shape[1] + part]
        acc[...] = jnp.zeros_like(acc)

    h = mm(n2[...], wup[...]) + b1[...]
    a, slope = gelu_parts(h)
    pack[:, :cut] = a.astype(BF16)
    hg = (ag_ref[...].astype(F32) * slope).astype(BF16)
    acc[...] += mm(hg, wup[...], NT)
    b1g[...] = jnp.sum(hg.astype(F32), axis=0, keepdims=True)
    pack[:, pack.shape[1] - part :] = gn[step]
    if not paired:
        pack[:, cut : 2 * cut] = hg
    else:
        half = cut // 2

        @pl.when(core == 0)
        def _():
            mine[0][...] = hg[:, :half]
            pack[:, cut : cut + half] = hg[:, half:]

        @pl.when(core == 1)
        def _():
            mine[0][...] = hg[:, half:]
            pack[:, cut : cut + half] = hg[:, :half]

    @pl.when(step == pl.num_programs(0) - 1)
    def _():
        ng = acc[...]
        n, rate = normalized(res[...])
        e = ng * gain[...]
        pulled = e - jnp.mean(e, axis=-1, keepdims=True) - n * jnp.mean(e * n, axis=-1, keepdims=True)
        r = cot[...].astype(F32) + rate * pulled
        rgrad[...] = r
        br = r.astype(BF16)
        brf = br.astype(F32)
        gg = mm(br, wo[...], NT)
        convgt[...] = (gg * second[...].astype(F32)).T.astype(BF16)
        sg = (gg * conv[...].astype(F32)).astype(BF16)
        sgrad[...] = sg
        sgf = sg.astype(F32)
        vecs[0:1] = jnp.sum(ng * n, axis=0, keepdims=True)
        vecs[1:2] = jnp.sum(ng, axis=0, keepdims=True)
        vecs[2:3] = jnp.sum(brf, axis=0, keepdims=True)
        vecs[3:4] = jnp.sum(sgf, axis=0, keepdims=True)
        put_halves(brf.T.astype(BF16), mine_t, other_t, 0, core, freq_parts)
        put_halves(sgf.T.astype(BF16), mine_t, other_t, 1, core, freq_parts)


def mlp_call(tok, convt, second, wo, ob, gain, bias, wup, b1, active_grad, cot, cut, paired, freq_parts, after=(), carry=()):
    rows, width = tok.shape
    ff = wup.shape[1]
    steps = ff // cut
    part = 2 * width // steps
    span = cut + (cut // 2 if paired else cut) + part

    def full(i):
        return (0, 0)

    def along(i):
        return (0, i)

    token = pl.BlockSpec((rows, width), full)
    vec = pl.BlockSpec((1, width), full)
    act = shape((rows, width), BF16)
    mine = [shape((rows, ff // 2), BF16)] if paired else []
    turned, turned_spec = shape((width, rows), BF16), pl.BlockSpec((width, rows), full)
    wide = shape((rows, width), F32)
    return launch(
        functools.partial(mlp_kernel, paired, freq_parts),
        (steps,),
        (tok, convt, second, wo, ob, gain, bias, wup, b1, active_grad, cot),
        [
            token,
            turned_spec,
            token,
            pl.BlockSpec((width, width), full),
            vec,
            vec,
            vec,
            pl.BlockSpec((width, cut), along),
            pl.BlockSpec((1, cut), along),
            pl.BlockSpec((rows, cut), along),
            token,
        ],
        (shape((rows, span * steps), BF16), wide, shape((1, ff), F32), wide, turned, act, turned, turned, shape((8, width), F32), *mine),
        (
            pl.BlockSpec((rows, span), along),
            token,
            pl.BlockSpec((1, cut), along),
            token,
            turned_spec,
            token,
            turned_spec,
            turned_spec,
            pl.BlockSpec((8, width), full),
            *[pl.BlockSpec((rows, cut // 2), along) for _ in mine],
        ),
        [pltpu.VMEM((rows, width), BF16), pltpu.VMEM((steps, rows, part), BF16), pltpu.VMEM((rows, width), BF16), pltpu.VMEM((rows, width), F32)],
        cost(2 * rows * width * (2 * ff + width), wup.size * 4 + rows * ff * 4 + rows * width * 14, rows * ff),
        "mix_out_mlp",
        after,
        carry,
    )


def unpacked(pack, hidden, steps, cut):
    rows = pack.shape[0]
    blocks = pack.reshape(rows, steps, -1)
    tail = blocks[:, :, cut + hidden :].reshape(rows, -1)
    return blocks[:, :, :cut].reshape(rows, -1), blocks[:, :, cut : cut + hidden].reshape(rows, -1), tail[:, : tail.shape[1] // 2], tail[:, tail.shape[1] // 2 :]


def put_halves(value, mine, other, half, core, freq_parts):
    per = value.shape[0] // freq_parts
    even = [value[(2 * k) * per : (2 * k + 1) * per] for k in range(freq_parts // 2)]
    odd = [value[(2 * k + 1) * per : (2 * k + 2) * per] for k in range(freq_parts // 2)]

    base = half * per * (freq_parts // 2)

    def put(ref, blocks):
        for k, block in enumerate(blocks):
            ref[base + k * per : base + (k + 1) * per] = block

    @pl.when(core == 0)
    def _():
        put(mine, even)
        put(other, odd)

    @pl.when(core == 1)
    def _():
        put(mine, odd)
        put(other, even)


def block_out_kernel(act, wdown, res, b2, out, acc):
    step = pl.program_id(0)
    part = mm(act[...], wdown[...])

    @pl.when(step == 0)
    def _():
        acc[...] = res[...] + b2[...] + part

    @pl.when(step > 0)
    def _():
        acc[...] += part

    @pl.when(step == pl.num_programs(0) - 1)
    def _():
        out[...] = acc[...].astype(BF16)


def block_out_call(pack, wdown, res, b2, cut, after=(), carry=()):
    rows, width = res.shape
    ff = wdown.shape[0]
    step = pack.shape[1] // ff
    if step * ff != pack.shape[1]:
        pack, step = unpacked(pack, cut, ff // cut, cut)[0], 1

    def full(i):
        return (0, 0)

    token = pl.BlockSpec((rows, width), full)
    return launch(
        block_out_kernel,
        (ff // cut,),
        (pack, wdown, res, b2),
        [pl.BlockSpec((rows, cut), lambda i: (0, step * i)), pl.BlockSpec((cut, width), lambda i: (i, 0)), token, pl.BlockSpec((1, width), full)],
        (shape((rows, width), BF16),),
        (token,),
        [pltpu.VMEM((rows, width), F32)],
        cost(2 * rows * width * ff, wdown.size * 2 + rows * ff * 2 + rows * width * 8),
        "block_out",
        after,
        carry,
    )


def back_kernel(mgt, value, gate, sgrad, weight, tok, gain, rgrad, out, vecs, mg, acc):
    step = pl.program_id(0)

    @pl.when(step == 0)
    def _():
        mg[...] = mgt[...].astype(F32).T.astype(BF16)
        acc[...] = mm(sgrad[...], weight[...], NT)

    @pl.when(step == 1)
    def _():
        pv = (gate[...].astype(F32) * mg[...].astype(F32)).astype(BF16)
        acc[...] += mm(pv, weight[...], NT)
        vecs[2:3] = jnp.sum(pv.astype(F32), axis=0, keepdims=True)

    @pl.when(step == 2)
    def _():
        pg = (value[...].astype(F32) * mg[...].astype(F32)).astype(BF16)
        ng = acc[...] + mm(pg, weight[...], NT)
        vecs[3:4] = jnp.sum(pg.astype(F32), axis=0, keepdims=True)
        n, rate = normalized(tok[...].astype(F32))
        vecs[0:1] = jnp.sum(ng * n, axis=0, keepdims=True)
        vecs[1:2] = jnp.sum(ng, axis=0, keepdims=True)
        e = ng * gain[...]
        pulled = e - jnp.mean(e, axis=-1, keepdims=True) - n * jnp.mean(e * n, axis=-1, keepdims=True)
        out[...] = (rgrad[...] + rate * pulled).astype(BF16)


def back_call(mgt, value, gate, sgrad, weight, tok, gain, rgrad, after=(), carry=()):
    rows, width = tok.shape

    def full(i):
        return (0, 0)

    token = pl.BlockSpec((rows, width), full)
    return launch(
        back_kernel,
        (3,),
        (mgt, value, gate, sgrad, weight, tok, gain, rgrad,),
        [
            pl.BlockSpec((width, rows), full),
            token,
            token,
            token,
            pl.BlockSpec((width, width), lambda i: (0, lax.rem(i + 2, 3))),
            token,
            pl.BlockSpec((1, width), full),
            token,
        ],
        (shape((rows, width), BF16), shape((8, width), F32)),
        (token, pl.BlockSpec((8, width), full)),
        [pltpu.VMEM((rows, width), BF16), pltpu.VMEM((rows, width), F32)],
        cost(2048 * 2 * rows * width * width * 3, 2048 * (weight.size * 2 + rows * width * 16)),
        "project_back",
        after,
        carry,
    )


def owner_part(offs_ref, wt, bias, x, mg, source, batch, tok_rows):
    chans = wt.shape[0] // 2
    vg = mm(wt, x, NT) + bias
    lane = lax.broadcasted_iota(jnp.int32, (1, x.shape[0]), 1)
    limit = jnp.zeros_like(lane)
    for b in range(batch):
        inside = jnp.logical_and(lane >= b * tok_rows, lane < (b + 1) * tok_rows)
        limit = jnp.where(inside, offs_ref[b] + b * tok_rows, limit)
    m = jnp.where(source * tok_rows + lane >= limit, mg.astype(F32), 0.0)
    return jnp.concatenate([vg[chans:] * m, vg[:chans] * m], axis=0).astype(BF16)


def owner_list_kernel(batch, tok_rows, parts, offs_ref, wt, bias, mg, *refs):
    xs, out = refs[:parts], refs[parts]
    me = lax.axis_index("freq")
    total = None
    for r in range(parts):
        x = xs[r][...]
        source = me ^ r
        pg = owner_part(offs_ref, wt[...], bias[...], x, mg[source], source, batch, tok_rows)
        part = mm(pg, x)
        total = part if total is None else total + part
    out[...] = total.astype(BF16)


def owner_grid_kernel(batch, tok_rows, offs_ref, wt, bias, mg, x, out, acc):
    step = pl.program_id(0)

    @pl.when(step == 0)
    def _():
        acc[...] = jnp.zeros_like(acc)

    pg = owner_part(offs_ref, wt[...], bias[...], x[0], mg[0], step, batch, tok_rows)
    acc[...] += mm(pg, x[0])

    @pl.when(step == pl.num_programs(0) - 1)
    def _():
        out[...] = acc[...].astype(BF16)


def owner_call(offsets, wt, bias, mg, xs, batch, tok_rows, after=(), carry=()):
    chans, rows = mg.shape[1:]
    width = wt.shape[1]
    listed = isinstance(xs, list)
    count = mg.shape[0]
    if listed:
        kernel = functools.partial(owner_list_kernel, batch, tok_rows, count)
        grid, x_specs, scratch, mg_spec = (1,), [whole((rows, width))] * count, [], whole(mg.shape)
    else:
        kernel = functools.partial(owner_grid_kernel, batch, tok_rows)
        xs = [xs]
        grid, x_specs = (count,), [pl.BlockSpec((1, rows, width), lambda i: (i, 0, 0))]
        scratch = [pltpu.VMEM((2 * chans, width), F32)]
        mg_spec = pl.BlockSpec((1, chans, rows), lambda i: (i, 0, 0))
    return launch(
        kernel,
        grid,
        (offsets, wt, bias, mg, *xs,),
        [smem(), whole(wt.shape), whole(bias.shape), mg_spec] + x_specs,
        (shape((2 * chans, width), BF16),),
        (whole((2 * chans, width)),),
        scratch,
        cost(8 * count * rows * chans * width, count * rows * width * 2),
        "owner_gradients",
        after,
        carry,
    )


def once(value, after):
    def nothing(after_ref, value_ref, out_ref):
        pass

    return pl.pallas_call(
        nothing,
        out_shape=shape(value.shape, value.dtype),
        in_specs=[anywhere(), anywhere()],
        out_specs=anywhere(),
        input_output_aliases={1: 0},
        name="gate",
    )(after, value)


def bit_order(chips, low_first):
    bits = list(range(chips.bit_length() - 1))
    return bits if low_first else bits[::-1]


def place_of(rel, order):
    place = 0
    for level, bit in enumerate(order):
        digit = lax.shift_right_logical(rel, bit) & 1
        place = place + digit * (1 << (len(order) - 1 - level))
    return place


def store_slot(keep, send, place, index, block):
    half = keep.shape[0]

    @pl.when(place < half)
    def _():
        keep[(place,) + index] = block

    @pl.when(place >= half)
    def _():
        send[(place - half,) + index] = block


def rows_kernel(chips, per, chip_order, dp_order, cot, act, cot_p, act_p, keep, send):
    chip = lax.axis_index("freq") // 2
    quarter = pl.program_id(0) ^ lax.axis_index("dp")
    total = (mm(cot[...], act[...]) + mm(cot_p[...], act_p[...])).astype(BF16)
    for k in range(chips):
        place = place_of(jnp.int32(k) ^ chip, chip_order)
        store_slot(keep, send, place_of(quarter, dp_order), (place,), total[k * per : (k + 1) * per])


def rows_pair(own, partner, width, dp, chips, low_first, after=(), carry=()):
    half, inner = own[0].shape
    per = half // chips
    out = shape((dp // 2, chips, per, width), BF16)
    arrays, specs = [], []
    for cot, pack in (own, partner):
        arrays += [cot, pack]
        specs += [whole(cot.shape), pl.BlockSpec((inner, width), lambda i: (0, 2 * i))]
    return launch(
        functools.partial(rows_kernel, chips, per, bit_order(chips, low_first), bit_order(dp, True)),
        (dp,),
        tuple(arrays),
        specs,
        (out, out),
        (whole(out.shape), whole(out.shape)),
        [],
        cost(4 * dp * half * inner * width, dp * inner * width * 4),
        "fc2_gradient",
        after,
        carry,
    )


def rows_plain(cot, act, cot_p, act_p, dp, chips, low_first):
    total = (mm(cot, act) + mm(cot_p, act_p)).astype(BF16)
    blocks = total.reshape(chips, cot.shape[0] // chips, dp, -1).transpose(2, 0, 1, 3)
    blocks = jnp.concatenate(halves_of(blocks.transpose(1, 0, 2, 3), bit_order(chips, low_first)), axis=0).transpose(1, 0, 2, 3)
    return halves_of(blocks, bit_order(dp, True), lax.axis_index("dp"))


def mixer_kernel(chips, per, order, turned, ga, gb, normed, turned_p, ga_p, gb_p, normed_p, keep, send):
    step = pl.program_id(0)
    chip = lax.axis_index("freq") // 2

    def put(half, total):
        for k in range(chips):
            place = place_of(jnp.int32(k) ^ chip, order)
            store_slot(keep, send, place, (slice(half * per, (half + 1) * per), slice(None)), total[k * per : (k + 1) * per].astype(BF16))

    @pl.when(step == 0)
    def _():
        def out(t, a, b):
            return jnp.concatenate([mm(t[...], a[...]), mm(t[...], b[...])], axis=1)

        put(0, out(turned, ga, gb) + out(turned_p, ga_p, gb_p))

    @pl.when(step == 1)
    def _():
        put(1, mm(turned[...], normed[...]) + mm(turned_p[...], normed_p[...]))


def mixer_pair(own, partner, width, chips, low_first, after=(), carry=()):
    order = bit_order(chips, low_first)
    half = width // 2
    per = half // chips
    out = shape((chips // 2, 2 * per, width), BF16)
    arrays, specs = [], []
    for turned, pack, normed in (own, partner):
        inner = turned.shape[1]
        arrays += [turned, pack, pack, normed]
        specs += [
            pl.BlockSpec((half, inner), lambda i: (i, 0)),
            pl.BlockSpec((inner, half), lambda i: (0, 3)),
            pl.BlockSpec((inner, half), lambda i: (0, 7)),
            whole(normed.shape),
        ]
    return launch(
        functools.partial(mixer_kernel, chips, per, order),
        (2,),
        tuple(arrays),
        specs,
        (out, out),
        (whole(out.shape), whole(out.shape)),
        [],
        cost(8 * half * inner * width, 4 * inner * width * 4),
        "mixer_gradient",
        after,
        carry,
    )


def halves_of(blocks, order, chip=None):
    chips = blocks.shape[0]
    chip = lax.axis_index("freq") // 2 if chip is None else chip
    picks = np.zeros(chips, np.int32)
    for rel in range(chips):
        place = sum(((rel >> bit) & 1) << (len(order) - 1 - level) for level, bit in enumerate(order))
        picks[place] = rel
    moved = jnp.take(blocks, jnp.asarray(picks) ^ chip, axis=0)
    return moved[: chips // 2], moved[chips // 2 :]


def cols_kernel(order, la, lb, rt, lap, lbp, rtp, keep, send, left):
    step = pl.program_id(0)
    chip = lax.axis_index("freq") // 2
    half = la.shape[1]

    @pl.when(step == 0)
    def _():
        for k, ref in enumerate((la, lb, lap, lbp)):
            left[k // 2, (k % 2) * half : (k % 2 + 1) * half] = ref[...].astype(F32).T.astype(BF16)

    total = (mm(left[0], rt[...]) + mm(left[1], rtp[...])).astype(BF16)
    store_slot(keep, send, place_of(step ^ chip, order), (), total)


def cols_pair(mine, pack, pack_p, width, cut, chips, low_first, after=(), carry=()):
    order = bit_order(chips, low_first)
    rows = mine.shape[0]
    per = mine.shape[1] // chips
    last = pack.shape[1] // per - 1
    step = pack.shape[1] // chips // per
    out = shape((chips // 2, width, per), BF16)
    out_spec = pl.BlockSpec((chips // 2, width, per), lambda i: (0, 0, 0))

    def at(place):
        return pl.BlockSpec((rows, per), place)

    first, second = (lambda i: (0, last - step)), (lambda i: (0, last))
    return launch(
        functools.partial(cols_kernel, order),
        (chips,),
        (pack, pack, mine, pack_p, pack_p, pack_p),
        [at(first), at(second), at(lambda i: (0, i)), at(first), at(second), at(lambda i: (0, step * i + 2))],
        (out, out),
        (out_spec, out_spec),
        [pltpu.VMEM((2, width, rows), BF16)],
        cost(4 * width * rows * mine.shape[1], (width * rows + rows * mine.shape[1] * 2) * 4),
        "fc1_gradient",
        after,
        carry,
    )


def cols_plain(lt, rt, ltp, rtp, chips, low_first):
    total = (mm(lt.T, rt) + mm(ltp.T, rtp)).astype(BF16)
    return halves_of(total.reshape(lt.shape[1], chips, -1).transpose(1, 0, 2), bit_order(chips, low_first))


def flip(value, freq_parts, bit):
    return lax.ppermute(value, "freq", [(i, i ^ bit) for i in range(freq_parts)])


def begin(keep, send, axis, bit):
    count = lax.axis_size(axis)
    return keep, lax.ppermute(send, axis, [(i, i ^ bit) for i in range(count)])


def finish(pending):
    return pending[0].astype(F32) + pending[1].astype(F32)


def step_on(pending, axis, bits, level):
    if level == len(bits):
        return finish(pending)[0], None
    half = pending[0].shape[0] // 2
    send = finish([v[half:] for v in pending]).astype(BF16)
    keep = finish([v[:half] for v in pending]).astype(BF16)
    return begin(keep, send, axis, bits[level]), send


def across_first(blocks):
    blocks = blocks.astype(BF16)
    count = blocks.shape[0]
    me = lax.axis_index("dp")
    blocks = blocks.reshape((count // 2, 2) + blocks.shape[1:])
    send = lax.dynamic_index_in_dim(blocks, 1 - me % 2, 1, keepdims=False)
    keep = lax.dynamic_index_in_dim(blocks, me % 2, 1, keepdims=False)
    return begin(keep, send, "dp", 1), send


def across_next(pending):
    total = finish(pending)
    me, count = lax.axis_index("dp"), lax.axis_size("dp")
    step = count // total.shape[0]
    total = total.astype(BF16)
    total = total.reshape((total.shape[0] // 2, 2) + total.shape[1:])
    mine = me // step % 2
    send = lax.dynamic_index_in_dim(total, 1 - mine, 1, keepdims=False)
    keep = lax.dynamic_index_in_dim(total, mine, 1, keepdims=False)
    return begin(keep, send, "dp", step), send


def across_rest(pending):
    while pending[0].shape[0] > 1:
        pending, _ = across_next(pending)
    return finish(pending)[0]


def pack_kernel(chans, one, two, b2, b1, skip, out):
    dp, freq = out.shape[:2]
    me = lax.axis_index("freq")
    column = jnp.broadcast_to(skip[...], (chans, 128)).T[0:1, :]
    per = b1.shape[1] // (freq * chans)

    def put(f, start, value):
        for d in range(dp):
            out[d, f, start : start + value.shape[0]] = value

    for f in range(freq):
        cut = slice(f * chans, (f + 1) * chans)
        put(f, 0, one[0:2, cut])
        for r in range(3):
            group, chunk = divmod(3 * f + r, freq)
            source = (one[2:3], one[3:4], two[3:4])[group]
            put(f, 2 + r, source[:, chunk * chans : (chunk + 1) * chans])
        put(f, 5, two[0:3, cut])
        put(f, 8, b2[:, cut])
        for r in range(per):
            start = (f * per + r) * chans
            put(f, 9 + r, b1[:, start : start + chans])
        put(f, 9 + per, jnp.where(me == f, column, 0.0))
    for d in range(dp):
        for f in range(freq):
            out[d, f, 10 + per :] = jnp.zeros((out.shape[2] - 10 - per, chans), F32)


def packed_vectors(one, two, b2, b1, skip, dp, freq, after=(), carry=()):
    chans = one.shape[1] // freq
    lines = 16
    if freq == 8:
        return launch(
            functools.partial(pack_kernel, chans),
            (1,),
            (one, two, b2, b1, skip),
            [whole(v.shape) for v in (one, two, b2, b1, skip)],
            (shape((dp, freq, lines, chans), F32),),
            (whole((dp, freq, lines, chans)),),
            [],
            cost(1, 1),
            "pack_vectors",
            after,
            carry,
        )
    own = (jnp.arange(freq, dtype=jnp.int32) == lax.axis_index("freq")).astype(F32)[:, None, None] * skip.reshape(1, 1, chans)
    rows = jnp.concatenate([one[:2], two[:3], b2]).reshape(6, freq, chans).transpose(1, 0, 2)
    bias_in = jnp.concatenate([one[2:4], two[3:4]]).reshape(freq, 3, chans)
    rows = jnp.concatenate([rows[:, :2], bias_in, rows[:, 2:], b1.reshape(freq, -1, chans), own], axis=1)
    return jnp.broadcast_to(rows[None], (dp,) + rows.shape), carry


def to_all(block):
    dp, freq = lax.axis_size("dp"), lax.axis_size("freq")
    wide = block if block.ndim == 4 else jnp.broadcast_to(block[None], (dp,) + block.shape)
    wide = wide.reshape((dp * freq,) + wide.shape[2:])
    return lax.all_to_all(wide, ("dp", "freq"), split_axis=0, concat_axis=0, tiled=True)


def reblocked(blocks, count, width):
    if blocks.shape[0] == count and blocks.shape[2] == width:
        return blocks
    whole = blocks.transpose(1, 0, 2).reshape(blocks.shape[1], -1)
    need = count * width
    whole = jnp.pad(whole, ((0, 0), (0, max(0, need - whole.shape[1]))))[:, :need]
    return whole.reshape(-1, count, width).transpose(1, 0, 2)


def body(tokens, offsets, kernel_lengths, norm1_gain, norm1_bias, w_in, in_bias, kernel_taps, skip_gain, w_out, out_bias, norm2_gain, norm2_bias, w_up, fc1_bias, w_down, fc2_bias, cotangent):
    freq = lax.axis_size("freq")
    dp = lax.axis_size("dp")
    chips = freq // 2
    batch, tok_rows, width = tokens.shape
    rows = batch * tok_rows
    ff = w_up.shape[1]
    chans = width // freq
    me = lax.axis_index("freq")
    core = lax.rem(me, 2)

    def row(v):
        return v.reshape(1, -1)

    tok = tokens.reshape(rows, width)
    cot = cotangent.reshape(rows, width)
    tap_rows = kernel_taps.shape[1]
    reach = -(-freq * tap_rows // tok_rows)
    lens = lax.dynamic_slice_in_dim(kernel_lengths, me * chans, chans).reshape(chans, 1)
    skip = skip_gain.reshape(chans, 1)

    def swap(v):
        return flip(v, freq, 1)

    cut = 768
    normed, mixed_t, value, gate, gate_two = front_call(
        tok, offsets, norm1_gain, norm1_bias, w_in, row(in_bias), kernel_taps, batch, tok_rows
    )
    mixed = lax.all_to_all(mixed_t.reshape(freq, chans, -1), "freq", split_axis=0, concat_axis=0, tiled=True)
    taps = mixed if tap_rows == tok_rows else reblocked(mixed[:, :, rows:], reach, tok_rows)
    active_grad, b2g, cot_mine, cot_other = active_grad_call(cot, w_down, cut, freq, after=(mixed_t,))
    own_w = jnp.concatenate([lax.dynamic_slice_in_dim(w_in, k * width + me * chans, chans, axis=1) for k in range(2)], axis=1).T
    own_b = jnp.concatenate([lax.dynamic_slice_in_dim(in_bias, k * width + me * chans, chans) for k in range(2)]).reshape(-1, 1)
    (conv, k_spec), (cot_p, normed_p, normed) = forward_call(mixed, batch, tok_rows, taps, lens, skip, after=(active_grad, own_w, own_b), carry=(swap(cot_other), swap(normed), normed))
    conv_t = lax.all_to_all(conv, "freq", split_axis=0, concat_axis=0, tiled=True).reshape(width, rows)
    near = []
    if freq == 8:
        near = [flip(normed, freq, 2), flip(normed, freq, 4), flip(normed, freq, 6)]
    paired = freq == 8 and ff == 4 * cut
    pack, res, b1g, rgrad, convg_t, sgrad, turned, turned_other, vec_two, *mine = mlp_call(
        tok, conv_t, gate_two, w_out, row(out_bias), row(norm2_gain), row(norm2_bias), w_up, row(fc1_bias), active_grad, cot, cut, paired, freq
    )
    mine = mine[0] if paired else None
    block_out = block_out_call(pack, w_down, res, row(fc2_bias), cut)
    convg = lax.all_to_all(convg_t.reshape(freq, chans, rows), "freq", split_axis=0, concat_axis=0, tiled=True)
    half = width // 2
    if paired:
        pack_p, turned_p = swap(pack), swap(turned_other)
        fc2, near = rows_pair((cot_mine, pack), (cot_p, pack_p), width, dp, chips, True, after=(block_out,), carry=near)
        fc1 = cols_pair(mine, pack, pack_p, width, cut, chips, False, after=(fc2[1],))
        far = [swap(v) for v in near]
        mixed_grad = adjoint_call(convg, batch, k_spec, skip, after=(fc1[1],))
        mixer = mixer_pair((turned, pack, normed), (turned_p, pack_p, normed_p), width, chips, True, after=(mixed_grad,))
        normed_all = [v for pair_of in zip([normed, *near], [normed_p, *far]) for v in pair_of]
    else:
        normed_all = lax.all_gather(normed, "freq", axis=0, tiled=False)
        act, hg, gated, n2 = unpacked(pack, cut, ff // cut, cut)
        hg = hg.reshape(rows, chips, 2, ff // freq)
        hg_mine = jnp.take(hg, core, axis=2).reshape(rows, ff // 2)
        hg_other = jnp.take(hg, 1 - core, axis=2).reshape(rows, ff // 2)
        act_p, gated_p, n2_p, turned_p = swap(act), swap(gated), swap(n2), swap(turned_other)
        fc2 = rows_plain(cot_mine, act, cot_p, act_p, dp, chips, True)
        fc1 = cols_plain(n2, hg_mine, n2_p, swap(hg_other), chips, False)
        mixer = []
        for lt, rt, ltp, rtp in ((turned[:half], gated, turned_p[:half], gated_p), (turned[half:], normed, turned_p[half:], normed_p)):
            mixer.append((mm(lt, rt) + mm(ltp, rtp)).astype(BF16).reshape(chips, -1, width))
        mixer = halves_of(jnp.concatenate(mixer, axis=1), bit_order(chips, True))
        mixed_grad = adjoint_call(convg, batch, k_spec, skip)
    mixed_grad_t = lax.all_to_all(mixed_grad, "freq", split_axis=0, concat_axis=0, tiled=True).reshape(width, rows)
    low, high = ([2 << bit for bit in bit_order(chips, first)] for first in (True, False))
    deep = [1 << bit for bit in bit_order(dp, True)]
    fc2_sum, fc1_sum, mixer_sum = begin(*fc2, "dp", deep[0]), begin(*fc1, "freq", high[0]), begin(*mixer, "freq", low[0])
    owned, (keep, keep_m) = owner_call(
        offsets, own_w, own_b, mixed_grad, normed_all, batch, tok_rows, after=(mixer[1],), carry=(fc2_sum[0], mixer_sum[0])
    )
    fc2_sum, sent = step_on((keep, fc2_sum[1]), "dp", deep, 1)
    mixer_sum, sent_m = step_on((once(keep_m, sent), mixer_sum[1]), "freq", low, 1)
    (taps_g, skip_g), (keep, keep_1, keep_m) = taps_grad_call(
        mixed, convg, lens, tok_rows, reach, after=(owned, sent_m), carry=(fc2_sum[0], fc1_sum[0], mixer_sum[0])
    )
    fc2_sum = (keep, fc2_sum[1])
    taps_g = reblocked(taps_g, freq, tap_rows).reshape(freq, dp, chans // dp, tap_rows).transpose(1, 0, 2, 3).reshape(dp, width // dp, tap_rows)
    taps_sum, sent_t = across_first(taps_g)
    fc1_sum, sent_1 = step_on((once(keep_1, sent_t), fc1_sum[1]), "freq", high, 1)
    mixer_sum = (once(keep_m, sent_1), mixer_sum[1])
    for level in range(2, len(low) + 1):
        mixer_sum, _ = step_on(mixer_sum, "freq", low, level)
    mixer = mixer_sum.astype(BF16)
    parts = jnp.concatenate([owned, mixer[chans:]]).reshape(3, chans, width)
    pieces, moved = [], []
    for r in range(3):
        part = lax.rem((freq % 3) * (r - me + 3 * freq), 3)
        moved.append(lax.dynamic_index_in_dim(parts, part, 0, keepdims=False))
        pieces.append(lax.ppermute(moved[-1], "freq", [((3 * d + r) % freq, d) for d in range(freq)]))
    (input_grad, vec_one), (keep, keep_1, keep_t) = back_call(
        mixed_grad_t, value, gate, sgrad, w_in, tok, row(norm1_gain), rgrad,
        after=tuple(moved), carry=(fc2_sum[0], fc1_sum[0], taps_sum[0]),
    )
    fa = ff // freq
    fc1_sum = (keep_1, fc1_sum[1])
    for level in range(2, len(high) + 1):
        fc1_sum, _ = step_on(fc1_sum, "freq", high, level)
    first, sent_1 = across_first(fc1_sum.reshape(dp, width // dp, fa))
    vectors, (keep, keep_t) = packed_vectors(vec_one, vec_two, b2g, b1g, skip_g, dp, freq, after=(sent_1,), carry=(keep, keep_t))
    final = to_all(vectors)
    taps_sum, sent_t = across_next((keep_t, taps_sum[1]))
    second = jnp.concatenate(pieces + [once(mixer[:chans], sent_t)], axis=0).T.reshape(dp, width // dp, 4 * chans)
    second, sent = across_first(second)
    first = (once(first[0], sent), first[1])
    first, sent = across_next(first)
    fc2_sum = (once(keep, sent), fc2_sum[1])
    for level in range(2, len(deep)):
        fc2_sum, _ = step_on(fc2_sum, "dp", deep, level)
    half = chips // 2
    sent = finish([v[0, half:] for v in fc2_sum]).astype(BF16)
    fc2_sum = begin(finish([v[0, :half] for v in fc2_sum]).astype(BF16), sent, "freq", low[0])
    second, sent = across_next((once(second[0], sent), second[1]))
    quarter_sum = across_rest((once(taps_sum[0], sent), taps_sum[1])).astype(BF16).reshape(freq, chans // dp, tap_rows)
    spread = to_all(quarter_sum)
    for level in range(1, len(low) + 1):
        fc2_sum, _ = step_on(fc2_sum, "freq", low, level)
    first, second = across_rest(first), across_rest(second)
    fc1_final, in_final, out_final = first, second[:, : 3 * chans], second[:, 3 * chans :]
    fc2_final = fc2_sum.T
    spread = spread.reshape(dp, freq, chans // dp, tap_rows).transpose(1, 0, 2, 3).reshape(width, tap_rows)
    taps_final = spread.astype(F32) * jnp.square(jnp.tanh(kernel_taps / SHRINK))
    final = jnp.sum(final, axis=0)
    n1g, n1b = final[0], final[1]
    inb = final[2:5].reshape(-1)
    n2g, n2b, outb, b2f = (final[k] for k in range(5, 9))
    lines = ff // width
    b1f, skg = final[9 : 9 + lines].reshape(-1), final[9 + lines]
    return (
        block_out.reshape(tokens.shape),
        input_grad.reshape(tokens.shape),
        n1g,
        n1b,
        in_final,
        inb,
        taps_final,
        skg,
        out_final,
        outb,
        n2g,
        n2b,
        fc1_final,
        b1f,
        fc2_final,
        b2f,
    )


def solution(mesh):
    token, whole, lead = P("dp", "freq", None), P(), P("freq")
    both = P("dp", "freq")
    in_specs = (token, P("dp"), whole, whole, whole, whole, whole, P(None, "freq"), lead) + (whole,) * 8 + (token,)
    out_specs = (token, token, lead, lead, both, lead, P(None, "freq"), lead, both, lead, lead, lead, both, lead, both, lead)
    return jax.shard_map(body, mesh=mesh, in_specs=in_specs, out_specs=out_specs, check_vma=False)
```

profile of v0, /device:TPU:0, one launch (start us, length us, event | category | flops | bytes accessed | tf_op | source)
XLA Modules:
  0.0 229.6 jit_solution(1091285928340366250)
XLA Ops:
  0.7 1.3 reshape.156.refs_7_.refs_8_.refs_9_
  2.0 6.7 %norm_project.1 = (bf16[512,768]{1,0:T(8,128)(2,1)}, bf16[768,768]{1,0:T(8,128)(2,1)}, bf16[512,768]{1,0:T(8,128)(2,1)}, bf16[512,768]{1,0:T(8,128)(2,1)}, bf16[512,768]{1,0:T(8,128)(2,1)}) custom-call(s32[2]{0:T(128)} %refs_0_.3, bf16[512,768]{1,0:T(8,128)(2,1)} %bitcast.109, f32[768]{0:T(1024)} %refs_2_.1, f32[768]{0:T(1024)} %refs_3_.5, ...), custom_call_target="tpu_custom_call" | custom-call | flops 115964116992 | bytes 528482304 | tf_op jit(solution)/shard_map/norm_project/pallas_call | solution.py:51
  8.7 5.2 %all-to-all-start = ((bf16[8,96,768]{2,1,0:T(8,128)(2,1)}), bf16[8,96,768]{2,1,0:T(8,128)(2,1)}, u32[]{:S(2)}, u32[]{:S(2)}) async-start(bf16[8,96,768]{2,1,0:T(8,128)(2,1)} %bitcast.99), calls=%async_computation | async-start | bytes 2359296 | tf_op jit(solution)/shard_map/all_to_all | solution.py:1167
  14.4 6.9 %active_grad.1 = (bf16[512,3072]{1,0:T(8,128)(2,1)}, f32[1,768]{1,0:T(1,128)}, bf16[384,512]{1,0:T(8,128)(2,1)}, bf16[384,512]{1,0:T(8,128)(2,1)}) custom-call(bf16[512,768]{1,0:T(8,128)(2,1)} %bitcast.107, bf16[3072,768]{1,0:T(8,128)(2,1)} %refs_1_.3, bf16[768,768]{1,0:T(8,128)(2,1)} %get-tuple-element.65.refs_2_), custom_call_target="tpu_custom_call" | custom-call | flops 154618822656 | bytes 503316480 | tf_op jit(solution)/shard_map/active_grad/pallas_call | solution.py:51
  21.3 1.3 constant_dynamic-slice_fusion.5
  26.9 3.9 %all-to-all-done.refs_0_ = bf16[8,96,768]{2,1,0:T(8,128)(2,1)} async-done(((bf16[8,96,768]{2,1,0:T(8,128)(2,1)}), bf16[8,96,768]{2,1,0:T(8,128)(2,1)}, u32[]{:S(2)}, u32[]{:S(2)}) %all-to-all-start) | async-done | bytes 1179680 | tf_op jit(solution)/shard_map/all_to_all | solution.py:1167
  30.8 7.8 %conv_forward.1 = (bf16[8,96,512]{2,1,0:T(8,128)(2,1)}, f32[8,96,512]{2,1,0:T(8,128)}, bf16[384,512]{1,0:T(8,128)(2,1)}, bf16[512,768]{1,0:T(8,128)(2,1)}, bf16[512,768]{1,0:T(8,128)(2,1)}) custom-call(bf16[8,96,768]{2,1,0:T(8,128)(2,1)} %all-to-all-done.refs_0_, ...), custom_call_target="tpu_custom_call", output_to_operand_aliasing={{2}: (10, {}), {3}: (11, {}), {4}: (12, {})} | custom-call | flops 193273528320 | bytes 369098752 | tf_op jit(solution)/shard_map/conv_forward/pallas_call | solution.py:51
  38.7 3.9 %all-to-all-start.1 = ((bf16[8,96,512]{2,1,0:T(8,128)(2,1)}), bf16[8,96,512]{2,1,0:T(8,128)(2,1)S(1)}, u32[]{:S(2)}, u32[]{:S(2)}) async-start(bf16[8,96,512]{2,1,0:T(8,128)(2,1)} %get-tuple-element.69), calls=%async_computation.1 | async-start | bytes 1572864 | tf_op jit(solution)/shard_map/all_to_all | solution.py:1173
  45.5 1.7 collective-permute-start.3
  47.2 1.5 collective-permute-start.4
  49.0 6.4 %all-to-all-done.1 = bf16[8,96,512]{2,1,0:T(8,128)(2,1)S(1)} async-done(((bf16[8,96,512]{2,1,0:T(8,128)(2,1)}), bf16[8,96,512]{2,1,0:T(8,128)(2,1)S(1)}, u32[]{:S(2)}, u32[]{:S(2)}) %all-to-all-start.1) | async-done | bytes 786464 | tf_op jit(solution)/shard_map/all_to_all | solution.py:1173
  56.3 19.8 %mix_out_mlp.1 = (bf16[512,6144]{1,0:T(8,128)(2,1)}, f32[512,768]{1,0:T(8,128)}, f32[1,3072]{1,0:T(1,128)}, f32[512,768]{1,0:T(8,128)}, bf16[768,512]{1,0:T(8,12...) custom-call(bf16[512,768]{1,0:T(8,128)(2,1)} %bitcast.110, ...), custom_call_target="tpu_custom_call" | custom-call | flops 347892350976 | bytes 1358954496 | tf_op jit(solution)/shard_map/mix_out_mlp/pallas_call | solution.py:51
  76.2 4.4 %all-to-all-start.2 = ((bf16[8,96,512]{2,1,0:T(8,128)(2,1)}), bf16[8,96,512]{2,1,0:T(8,128)(2,1)}, u32[]{:S(2)}, u32[]{:S(2)}) async-start(bf16[8,96,512]{2,1,0:T(8,128)(2,1)} %bitcast.101), calls=%async_computation.2 | async-start | bytes 1572864 | tf_op jit(solution)/shard_map/all_to_all | solution.py:1183
  81.1 7.5 %block_out.1.refs_4_ = bf16[512,768]{1,0:T(8,128)(2,1)} custom-call(bf16[512,6144]{1,0:T(8,128)(2,1)} %get-tuple-element.71.refs_0_.refs_1_.refs_2_, bf16[3072,768]{1,0:T(8,128)(2,1)} %refs_1_.3, f32[512,768]{1,0:T(8,128)} %get-tuple-element.72.refs_2_, f32[1,768]{1,0:T(1,128)} %reshape.167.refs_3_), custom_call_target="tpu_custom_call" | custom-call | flops 154618822656 | bytes 704643072 | tf_op jit(solution)/shard_map/block_out/pallas_call | solution.py:51
  89.3 7.1 %fc2_gradient.1 = (bf16[2,4,96,768]{3,2,1,0:T(8,128)(2,1)}, bf16[2,4,96,768]{3,2,1,0:T(8,128)(2,1)}, bf16[512,768]{1,0:T(8,128)(2,1)}, bf16[512,768]{1,0:T(8,128)(2,1)}, bf16[512,768]{1,0:T(8,128)(2,1)}) custom-call(bf16[384,512]{1,0:T(8,128)(2,1)} %get-tuple-element.76.refs_0_, ...), custom_call_target="tpu_custom_call", output_to_operand_aliasing={{2}: (5, {}), {3}: (6, {}), {4}: (7, {})} | custom-call | flops 154618822656 | bytes 402653184 | tf_op jit(solution)/shard_map/fc2_gradient/pallas_call | solution.py:51
  96.9 2.0 collective-permute-start.10
  98.9 7.8 %fc1_gradient.1 = (bf16[2,768,384]{2,1,0:T(8,128)(2,1)}, bf16[2,768,384]{2,1,0:T(8,128)(2,1)}) custom-call(bf16[512,6144]{1,0:T(8,128)(2,1)} %get-tuple-element.71.refs_0_.refs_1_.refs_2_, bf16[512,6144]{1,0:T(8,128)(2,1)} %get-tuple-element.71.refs_0_.refs_1_.refs_2_, bf16[512,1536]{1,0:T(8,128)(2,1)} %get-tuple-element.75.refs_2_, ...), custom_call_target="tpu_custom_call" | custom-call | flops 154618822656 | bytes 503316480 | tf_op jit(solution)/shard_map/fc1_gradient/pallas_call | solution.py:51
  107.5 7.0 %conv_adjoint.1.refs_8_.refs_3_ = bf16[8,96,512]{2,1,0:T(8,128)(2,1)} custom-call(bf16[8,96,512]{2,1,0:T(8,128)(2,1)} %all-to-all-done.2.refs_0_.refs_1_, f32[8,96,512]{2,1,0:T(8,128)} %get-tuple-element.74.refs_1_, f32[96,1]{1,0:T(8,128)} %copy.87.refs_2_, bf16[256,512]{1,0:T(8,128)(2,1)} %constant.127.clone.refs_3_, ...), custom_call_target="tpu_custom_call" | custom-call | flops 128849018880 | bytes 268435456 | tf_op jit(solution)/shard_map/conv_adjoint/pallas_call | solution.py:51
  114.4 4.5 %all-to-all-start.3 = ((bf16[8,96,512]{2,1,0:T(8,128)(2,1)}), bf16[8,96,512]{2,1,0:T(8,128)(2,1)}, u32[]{:S(2)}, u32[]{:S(2)}) async-start(bf16[8,96,512]{2,1,0:T(8,128)(2,1)} %conv_adjoint.1.refs_8_.refs_3_), calls=%async_computation.3 | async-start | bytes 1572864 | tf_op jit(solution)/shard_map/all_to_all | solution.py:1207
  119.0 5.2 %mixer_gradient.1 = (bf16[2,192,768]{2,1,0:T(8,128)(2,1)}, bf16[2,192,768]{2,1,0:T(8,128)(2,1)}) custom-call(bf16[768,512]{1,0:T(8,128)(2,1)} %get-tuple-element.89.refs_0_, bf16[512,6144]{1,0:T(8,128)(2,1)} %get-tuple-element.71.refs_0_.refs_1_.refs_2_, bf16[512,6144]{1,0:T(8,128)(2,1)} %get-tuple-element.71.refs_0_.refs_1_.refs_2_, ...), custom_call_target="tpu_custom_call" | custom-call | flops 77309411328 | bytes 402653184 | tf_op jit(solution)/shard_map/mixer_gradient/pallas_call | solution.py:51
  124.2 1.7 collective-permute-start.11
  126.8 8.3 %owner_gradients.1 = (bf16[192,768]{1,0:T(8,128)(2,1)}, bf16[2,4,96,768]{3,2,1,0:T(8,128)(2,1)}, bf16[2,192,768]{2,1,0:T(8,128)(2,1)}) custom-call(s32[2]{0:T(128)} %refs_0_.3, bf16[192,768]{1,0:T(8,128)(2,1)} %maximum_bitcast_fusion.1.refs_8_.refs_1_, f32[192,1]{1,0:T(8,128)} %copy.88.refs_9_.refs_2_, ...), custom_call_target="tpu_custom_call", output_to_operand_aliasing={{1}: (13, {}), {2}: (14, {})} | custom-call | flops 154618822656 | bytes 402653184 | tf_op jit(solution)/shard_map/owner_gradients/pallas_call | solution.py:51
  135.2 2.9 %add_convert_fusion.3 = (bf16[1,4,96,768]{3,2,1,0:T(8,128)(2,1)}, bf16[1,4,96,768]{3,2,1,0:T(8,128)(2,1)}) fusion(bf16[2,4,96,768]{3,2,1,0:T(8,128)(2,1)} %collective-permute-done.10, bf16[2,4,96,768]{3,2,1,0:T(8,128)(2,1)} %get-tuple-element.95), kind=kLoop, calls=%fused_computation.3 | loop fusion | flops 2359296 | bytes 3538944 | tf_op jit(solution)/shard_map/convert_element_type | solution.py:1039
  138.1 2.6 %collective-permute-start.20 = (bf16[1,4,96,768]{3,2,1,0:T(8,128)(2,1)}, bf16[1,4,96,768]{3,2,1,0:T(8,128)(2,1)}, u32[]{:S(2)}, u32[]{:S(2)}) collective-permute-start(bf16[1,4,96,768]{3,2,1,0:T(8,128)(2,1)} %get-tuple-element.119.after_ref), channel_id=1, source_target_pairs={{0,16},{8,24},{16,0},{24,8},{1,17},{9,25},{17,1},{25,9},{2,18},{10... | collective-permute-start | bytes 1769480 | tf_op jit(solution)/shard_map/ppermute | solution.py:1027
  140.7 2.3 %collective-permute-done.11 = bf16[2,192,768]{2,1,0:T(8,128)(2,1)} collective-permute-done((bf16[2,192,768]{2,1,0:T(8,128)(2,1)}, bf16[2,192,768]{2,1,0:T(8,128)(2,1)}, u32[]{:S(2)}, u32[]{:S(2)}) %collective-permute-start.11) | collective-permute-done | bytes 589856 | tf_op jit(solution)/shard_map/ppermute | solution.py:1027
  143.0 2.2 add_convert_fusion.10
  145.2 1.5 collective-permute-start.13
  146.7 8.7 %taps_gradient.1 = (bf16[8,96,256]{2,1,0:T(8,128)(2,1)}, f32[96,1]{1,0:T(8,128)}, bf16[1,4,96,768]{3,2,1,0:T(8,128)(2,1)}, bf16[2,768,384]{2,1,0:T(8,128)(2,1)}, bf16[1,192,768]{2,1,0:T(8,128)(2,1)}) custom-call(bf16[8,96,768]{2,1,0:T(8,128)(2,1)} %all-to-all-done.refs_0_, ...), custom_call_target="tpu_custom_call", output_to_operand_aliasing={{2}: (9, {}), {3}: (10, {}), {4}: (11, {})} | custom-call | flops 193273528320 | bytes 226492416 | tf_op jit(solution)/shard_map/taps_gradient/pallas_call | solution.py:51
  157.2 2.9 %add_convert_fusion.1 = (bf16[1,768,384]{2,1,0:T(8,128)(2,1)}, bf16[1,768,384]{2,1,0:T(8,128)(2,1)}) fusion(bf16[2,768,384]{2,1,0:T(8,128)(2,1)} %collective-permute-done.12, bf16[2,768,384]{2,1,0:T(8,128)(2,1)} %gate.9), kind=kLoop, calls=%fused_computation.1 | loop fusion | flops 2359296 | bytes 3538944 | tf_op jit(solution)/shard_map/convert_element_type | solution.py:1039
  160.7 1.2 add_convert_fusion.9
  163.3 2.8 %collective-permute-start.15 = (bf16[96,768]{1,0:T(8,128)(2,1)}, bf16[96,768]{1,0:T(8,128)(2,1)}, u32[]{:S(2)}, u32[]{:S(2)}) collective-permute-start(bf16[96,768]{1,0:T(8,128)(2,1)} %get-tuple-element.130.refs_8_), channel_id=1, source_target_pairs={{0,0},{3,1},{6,2},{1,3},{4,4},{7,5},{2,6},{5,7},{8,8},{11,9},{14,1... | collective-permute-start | bytes 442376 | tf_op jit(solution)/shard_map/ppermute | solution.py:1232
  166.2 7.7 %project_back.1 = (bf16[512,768]{1,0:T(8,128)(2,1)}, f32[8,768]{1,0:T(8,128)}, bf16[1,4,96,768]{3,2,1,0:T(8,128)(2,1)}, bf16[1,768,384]{2,1,0:T(8,128)(2,1)}, bf16[2,192,256]{2,1,0:T(8,128)(2,1)}) custom-call(bf16[768,512]{1,0:T(8,128)(2,1)} %bitcast.11.refs_0_, ...), custom_call_target="tpu_custom_call", output_to_operand_aliasing={{2}: (11, {}), {3}: (12, {}), {4}: (13, {})} | custom-call | flops 237494511599616 | bytes 1288490188800 | tf_op jit(solution)/shard_map/project_back/pallas_call | solution.py:51
  173.9 2.7 %collective-permute-done.14 = bf16[1,768,384]{2,1,0:T(8,128)(2,1)} collective-permute-done((bf16[1,768,384]{2,1,0:T(8,128)(2,1)}, bf16[1,768,384]{2,1,0:T(8,128)(2,1)}, u32[]{:S(2)}, u32[]{:S(2)}) %collective-permute-start.14) | collective-permute-done | bytes 589856 | tf_op jit(solution)/shard_map/ppermute | solution.py:1027
  176.6 2.4 %collective-permute-start.17 = (bf16[96,768]{1,0:T(8,128)(2,1)S(1)}, bf16[96,768]{1,0:T(8,128)(2,1)S(1)}, u32[]{:S(2)}, u32[]{:S(2)}) collective-permute-start(bf16[96,768]{1,0:T(8,128)(2,1)S(1)} %copy-done.11), channel_id=1, source_target_pairs={{2,0},{5,1},{0,2},{3,3},{6,4},{1,5},{4,6},{7,7},{10,8},{13,9},{8,1... | collective-permute-start | bytes 442376 | tf_op jit(solution)/shard_map/ppermute | solution.py:1232
  179.1 1.4 add_convert_fusion
  181.3 1.8 pack_vectors.1
  183.2 1.7 collective-permute-start.19
  186.7 2.6 %collective-permute-start.23 = (bf16[1,192,256]{2,1,0:T(8,128)(2,1)}, bf16[1,192,256]{2,1,0:T(8,128)(2,1)S(1)}, u32[]{:S(2)}, u32[]{:S(2)}) collective-permute-start(bf16[1,192,256]{2,1,0:T(8,128)(2,1)} %get-tuple-element.136.after_ref), channel_id=1, source_target_pairs={{0,16},{8,24},{16,0},{24,8},{1,17},{9,25},{17,1},{25,9},{2,18},{10... | collective-permute-start | bytes 294920 | tf_op jit(solution)/shard_map/ppermute | solution.py:1027
  192.2 2.6 %all-to-all-start.4 = ((f32[32,16,96]{2,1,0:T(8,128)}), f32[32,16,96]{2,1,0:T(8,128)S(1)}, u32[]{:S(2)}, u32[]{:S(2)}) async-start(f32[32,16,96]{2,1,0:T(8,128)} %bitcast.26), calls=%async_computation.4 | async-start | bytes 524288 | tf_op jit(solution)/shard_map/all_to_all | solution.py:1127
  195.9 2.7 %collective-permute-start.24 = (bf16[1,192,384]{2,1,0:T(8,128)(2,1)S(1)}, bf16[1,192,384]{2,1,0:T(8,128)(2,1)S(1)}, u32[]{:S(2)}, u32[]{:S(2)}) collective-permute-start(bf16[1,192,384]{2,1,0:T(8,128)(2,1)S(1)} %constant_dynamic-slice_fusion.2.after_ref), channel_id=1, source_target_pairs={{0,16},{8,24},{16,0},{24,8},{1,17},{9,25},{17,1},{25,9},{2,18},{10... | collective-permute-start | bytes 442376 | tf_op jit(solution)/shard_map/ppermute | solution.py:1027
  198.7 1.4 add_convert_fusion.5
  200.0 1.5 collective-permute-start.25
  202.7 1.3 collective-permute-start.22
  204.9 7.0 %all-to-all-done.4 = f32[32,16,96]{2,1,0:T(8,128)S(1)} async-done(((f32[32,16,96]{2,1,0:T(8,128)}), f32[32,16,96]{2,1,0:T(8,128)S(1)}, u32[]{:S(2)}, u32[]{:S(2)}) %all-to-all-start.4) | async-done | bytes 196640 | tf_op jit(solution)/shard_map/all_to_all | solution.py:1127
  212.7 2.6 %all-to-all-start.5 = ((bf16[32,24,256]{2,1,0:T(8,128)(2,1)}), bf16[32,24,256]{2,1,0:T(8,128)(2,1)S(1)}, u32[]{:S(2)}, u32[]{:S(2)}) async-start(bf16[32,24,256]{2,1,0:T(8,128)(2,1)} %bitcast.38), calls=%async_computation.5 | async-start | bytes 786432 | tf_op jit(solution)/shard_map/all_to_all | solution.py:1127
  218.1 1.7 collective-permute-start.26
  220.5 5.2 %collective-permute-done.26 = bf16[1,96,768]{2,1,0:T(8,128)(2,1)S(1)} collective-permute-done((bf16[1,96,768]{2,1,0:T(8,128)(2,1)S(1)}, bf16[1,96,768]{2,1,0:T(8,128)(2,1)S(1)}, u32[]{:S(2)}, u32[]{:S(2)}) %collective-permute-start.26) | collective-permute-done | bytes 147488 | tf_op jit(solution)/shard_map/ppermute | solution.py:1027
  226.5 2.0 all-to-all-done.5
  (132 shorter events, 31.1 us)
Async XLA Ops:
  0.6 24.0 %copy-start = (s32[768]{0:T(1024)S(1)}, s32[768]{0:T(1024)}, u32[]{:S(2)}) copy-start(s32[768]{0:T(1024)} %param.24) | copy-start | bytes 9220
  8.7 22.1 %all-to-all-start = ((bf16[8,96,768]{2,1,0:T(8,128)(2,1)}), bf16[8,96,768]{2,1,0:T(8,128)(2,1)}, u32[]{:S(2)}, u32[]{:S(2)}) async-start(bf16[8,96,768]{2,1,0:T(8,128)(2,1)} %bitcast.99), calls=%async_computation | async-start | bytes 2359296 | tf_op jit(solution)/shard_map/all_to_all | solution.py:1167
  13.9 13.0 %collective-permute-start.1 = (bf16[512,768]{1,0:T(8,128)(2,1)}, bf16[512,768]{1,0:T(8,128)(2,1)}, u32[]{:S(2)}, u32[]{:S(2)}) collective-permute-start(bf16[512,768]{1,0:T(8,128)(2,1)} %get-tuple-element.68.refs_12_), channel_id=1, source_target_pairs={{0,1},{1,0},{2,3},{3,2},{4,5},{5,4},{6,7},{7,6},{8,9},{9,8},{10,11... | collective-permute-start | bytes 2359304 | tf_op jit(solution)/shard_map/ppermute | solution.py:1022
  21.3 4.1 %copy-start.17 = (f32[96]{0:T(128)S(1)}, f32[96]{0:T(128)}, u32[]{:S(2)}) copy-start(f32[96]{0:T(128)} %param.30) | copy-start | bytes 1156
  21.3 5.6 %collective-permute-start = (bf16[384,512]{1,0:T(8,128)(2,1)}, bf16[384,512]{1,0:T(8,128)(2,1)S(1)}, u32[]{:S(2)}, u32[]{:S(2)}) collective-permute-start(bf16[384,512]{1,0:T(8,128)(2,1)} %get-tuple-element.67), channel_id=1, source_target_pairs={{0,1},{1,0},{2,3},{3,2},{4,5},{5,4},{6,7},{7,6},{8,9},{9,8},{10,11... | collective-permute-start | bytes 1179656 | tf_op jit(solution)/shard_map/ppermute | solution.py:1022
  26.9 3.9 %copy-start.19 = (bf16[384,512]{1,0:T(8,128)(2,1)}, bf16[384,512]{1,0:T(8,128)(2,1)S(1)}, u32[]{:S(2)}) copy-start(bf16[384,512]{1,0:T(8,128)(2,1)S(1)} %collective-permute-done.refs_10_) | copy-start | bytes 1179652
  38.6 4.0 %copy-start.12 = (f32[768]{0:T(1024)S(1)}, f32[768]{0:T(1024)}, u32[]{:S(2)}) copy-start(f32[768]{0:T(1024)} %refs_2_.1) | copy-start | bytes 9220
  38.6 4.6 %copy-start.13 = (f32[768]{0:T(1024)S(1)}, f32[768]{0:T(1024)}, u32[]{:S(2)}) copy-start(f32[768]{0:T(1024)} %param.32) | copy-start | bytes 9220
  38.6 5.1 %copy-start.14 = (f32[768]{0:T(1024)S(1)}, f32[768]{0:T(1024)}, u32[]{:S(2)}) copy-start(f32[768]{0:T(1024)} %param.33) | copy-start | bytes 9220
  38.6 5.7 %copy-start.15 = (f32[768]{0:T(1024)S(1)}, f32[768]{0:T(1024)}, u32[]{:S(2)}) copy-start(f32[768]{0:T(1024)} %param.34) | copy-start | bytes 9220
  38.6 6.3 %copy-start.16 = (f32[768]{0:T(1024)S(1)}, f32[768]{0:T(1024)}, u32[]{:S(2)}) copy-start(f32[768]{0:T(1024)} %param.38) | copy-start | bytes 9220
  38.7 16.7 %all-to-all-start.1 = ((bf16[8,96,512]{2,1,0:T(8,128)(2,1)}), bf16[8,96,512]{2,1,0:T(8,128)(2,1)S(1)}, u32[]{:S(2)}, u32[]{:S(2)}) async-start(bf16[8,96,512]{2,1,0:T(8,128)(2,1)} %get-tuple-element.69), calls=%async_computation.1 | async-start | bytes 1572864 | tf_op jit(solution)/shard_map/all_to_all | solution.py:1173
  45.5 43.1 %collective-permute-start.3 = (bf16[512,768]{1,0:T(8,128)(2,1)}, bf16[512,768]{1,0:T(8,128)(2,1)}, u32[]{:S(2)}, u32[]{:S(2)}) collective-permute-start(bf16[512,768]{1,0:T(8,128)(2,1)} %get-tuple-element.78.refs_3_.refs_4_), channel_id=1, source_target_pairs={{0,2},{1,3},{2,0},{3,1},{4,6},{5,7},{6,4},{7,5},{8,10},{9,11},{10,... | collective-permute-start | bytes 2359304 | tf_op jit(solution)/shard_map/ppermute | solution.py:1022
  47.2 41.4 %collective-permute-start.4 = (bf16[512,768]{1,0:T(8,128)(2,1)}, bf16[512,768]{1,0:T(8,128)(2,1)}, u32[]{:S(2)}, u32[]{:S(2)}) collective-permute-start(bf16[512,768]{1,0:T(8,128)(2,1)} %get-tuple-element.78.refs_3_.refs_4_), channel_id=1, source_target_pairs={{0,4},{1,5},{2,6},{3,7},{4,0},{5,1},{6,2},{7,3},{8,12},{9,13},{10,... | collective-permute-start | bytes 2359304 | tf_op jit(solution)/shard_map/ppermute | solution.py:1022
  48.7 40.5 %collective-permute-start.5 = (bf16[512,768]{1,0:T(8,128)(2,1)}, bf16[512,768]{1,0:T(8,128)(2,1)}, u32[]{:S(2)}, u32[]{:S(2)}) collective-permute-start(bf16[512,768]{1,0:T(8,128)(2,1)} %get-tuple-element.78.refs_3_.refs_4_), channel_id=1, source_target_pairs={{0,6},{1,7},{2,4},{3,5},{4,2},{5,3},{6,0},{7,1},{8,14},{9,15},{10,... | collective-permute-start | bytes 2359304 | tf_op jit(solution)/shard_map/ppermute | solution.py:1022
  76.1 13.2 %collective-permute-start.2 = (bf16[512,6144]{1,0:T(8,128)(2,1)}, bf16[512,6144]{1,0:T(8,128)(2,1)}, u32[]{:S(2)}, u32[]{:S(2)}) collective-permute-start(bf16[512,6144]{1,0:T(8,128)(2,1)} %get-tuple-element.71.refs_0_.refs_1_.refs_2_), channel_id=1, source_target_pairs={{0,1},{1,0},{2,3},{3,2},{4,5},{5,4},{6,7},{7,6},{8,9},{9,8},{10,11... | collective-permute-start | bytes 18874376 | tf_op jit(solution)/shard_map/ppermute | solution.py:1022
  76.2 31.3 %all-to-all-start.2 = ((bf16[8,96,512]{2,1,0:T(8,128)(2,1)}), bf16[8,96,512]{2,1,0:T(8,128)(2,1)}, u32[]{:S(2)}, u32[]{:S(2)}) async-start(bf16[8,96,512]{2,1,0:T(8,128)(2,1)} %bitcast.101), calls=%async_computation.2 | async-start | bytes 1572864 | tf_op jit(solution)/shard_map/all_to_all | solution.py:1183
  80.6 38.3 %collective-permute-start.9 = (bf16[768,512]{1,0:T(8,128)(2,1)}, bf16[768,512]{1,0:T(8,128)(2,1)}, u32[]{:S(2)}, u32[]{:S(2)}) collective-permute-start(bf16[768,512]{1,0:T(8,128)(2,1)} %get-tuple-element.90), channel_id=1, source_target_pairs={{0,1},{1,0},{2,3},{3,2},{4,5},{5,4},{6,7},{7,6},{8,9},{9,8},{10,11... | collective-permute-start | bytes 2359304 | tf_op jit(solution)/shard_map/ppermute | solution.py:1022
  96.4 27.8 %collective-permute-start.6 = (bf16[512,768]{1,0:T(8,128)(2,1)}, bf16[512,768]{1,0:T(8,128)(2,1)}, u32[]{:S(2)}, u32[]{:S(2)}) collective-permute-start(bf16[512,768]{1,0:T(8,128)(2,1)} %get-tuple-element.86.refs_6_), channel_id=1, source_target_pairs={{0,1},{1,0},{2,3},{3,2},{4,5},{5,4},{6,7},{7,6},{8,9},{9,8},{10,11... | collective-permute-start | bytes 2359304 | tf_op jit(solution)/shard_map/ppermute | solution.py:1022
  96.4 29.6 %collective-permute-start.7 = (bf16[512,768]{1,0:T(8,128)(2,1)}, bf16[512,768]{1,0:T(8,128)(2,1)}, u32[]{:S(2)}, u32[]{:S(2)}) collective-permute-start(bf16[512,768]{1,0:T(8,128)(2,1)} %get-tuple-element.87.refs_8_), channel_id=1, source_target_pairs={{0,1},{1,0},{2,3},{3,2},{4,5},{5,4},{6,7},{7,6},{8,9},{9,8},{10,11... | collective-permute-start | bytes 2359304 | tf_op jit(solution)/shard_map/ppermute | solution.py:1022
  96.9 38.3 %collective-permute-start.10 = (bf16[2,4,96,768]{3,2,1,0:T(8,128)(2,1)}, bf16[2,4,96,768]{3,2,1,0:T(8,128)(2,1)}, u32[]{:S(2)}, u32[]{:S(2)}) collective-permute-start(bf16[2,4,96,768]{3,2,1,0:T(8,128)(2,1)} %get-tuple-element.79.refs_6_), channel_id=1, source_target_pairs={{0,8},{8,0},{16,24},{24,16},{1,9},{9,1},{17,25},{25,17},{2,10},{10... | collective-permute-start | bytes 3538952 | tf_op jit(solution)/shard_map/ppermute | solution.py:1027
  106.7 50.5 %collective-permute-start.12 = (bf16[2,768,384]{2,1,0:T(8,128)(2,1)}, bf16[2,768,384]{2,1,0:T(8,128)(2,1)}, u32[]{:S(2)}, u32[]{:S(2)}) collective-permute-start(bf16[2,768,384]{2,1,0:T(8,128)(2,1)} %get-tuple-element.80.refs_7_), channel_id=1, source_target_pairs={{0,4},{1,5},{2,6},{3,7},{4,0},{5,1},{6,2},{7,3},{8,12},{9,13},{10,... | collective-permute-start | bytes 3538952 | tf_op jit(solution)/shard_map/ppermute | solution.py:1027
  114.4 51.7 %all-to-all-start.3 = ((bf16[8,96,512]{2,1,0:T(8,128)(2,1)}), bf16[8,96,512]{2,1,0:T(8,128)(2,1)}, u32[]{:S(2)}, u32[]{:S(2)}) async-start(bf16[8,96,512]{2,1,0:T(8,128)(2,1)} %conv_adjoint.1.refs_8_.refs_3_), calls=%async_computation.3 | async-start | bytes 1572864 | tf_op jit(solution)/shard_map/all_to_all | solution.py:1207
  118.9 7.0 %collective-permute-start.8 = (bf16[512,768]{1,0:T(8,128)(2,1)}, bf16[512,768]{1,0:T(8,128)(2,1)S(1)}, u32[]{:S(2)}, u32[]{:S(2)}) collective-permute-start(bf16[512,768]{1,0:T(8,128)(2,1)} %get-tuple-element.88.refs_10_), channel_id=1, source_target_pairs={{0,1},{1,0},{2,3},{3,2},{4,5},{5,4},{6,7},{7,6},{8,9},{9,8},{10,11... | collective-permute-start | bytes 2359304 | tf_op jit(solution)/shard_map/ppermute | solution.py:1022
  124.2 18.8 %collective-permute-start.11 = (bf16[2,192,768]{2,1,0:T(8,128)(2,1)}, bf16[2,192,768]{2,1,0:T(8,128)(2,1)}, u32[]{:S(2)}, u32[]{:S(2)}) collective-permute-start(bf16[2,192,768]{2,1,0:T(8,128)(2,1)} %get-tuple-element.91.refs_12_), channel_id=1, source_target_pairs={{0,2},{1,3},{2,0},{3,1},{4,6},{5,7},{6,4},{7,5},{8,10},{9,11},{10,... | collective-permute-start | bytes 1769480 | tf_op jit(solution)/shard_map/ppermute | solution.py:1027
  138.1 60.6 %collective-permute-start.20 = (bf16[1,4,96,768]{3,2,1,0:T(8,128)(2,1)}, bf16[1,4,96,768]{3,2,1,0:T(8,128)(2,1)}, u32[]{:S(2)}, u32[]{:S(2)}) collective-permute-start(bf16[1,4,96,768]{3,2,1,0:T(8,128)(2,1)} %get-tuple-element.119.after_ref), channel_id=1, source_target_pairs={{0,16},{8,24},{16,0},{24,8},{1,17},{9,25},{17,1},{25,9},{2,18},{10... | collective-permute-start | bytes 1769480 | tf_op jit(solution)/shard_map/ppermute | solution.py:1027
  145.2 15.5 %collective-permute-start.13 = (bf16[1,192,768]{2,1,0:T(8,128)(2,1)}, bf16[1,192,768]{2,1,0:T(8,128)(2,1)}, u32[]{:S(2)}, u32[]{:S(2)}) collective-permute-start(bf16[1,192,768]{2,1,0:T(8,128)(2,1)} %get-tuple-element.123.refs_8_), channel_id=1, source_target_pairs={{0,4},{1,5},{2,6},{3,7},{4,0},{5,1},{6,2},{7,3},{8,12},{9,13},{10,... | collective-permute-start | bytes 884744 | tf_op jit(solution)/shard_map/ppermute | solution.py:1027
  157.2 26.0 %collective-permute-start.18 = (bf16[2,192,256]{2,1,0:T(8,128)(2,1)}, bf16[2,192,256]{2,1,0:T(8,128)(2,1)}, u32[]{:S(2)}, u32[]{:S(2)}) collective-permute-start(bf16[2,192,256]{2,1,0:T(8,128)(2,1)} %get-tuple-element.132.after_ref), channel_id=1, source_target_pairs={{0,8},{8,0},{16,24},{24,16},{1,9},{9,1},{17,25},{25,17},{2,10},{10... | collective-permute-start | bytes 589832 | tf_op jit(solution)/shard_map/ppermute | solution.py:1027
  160.1 16.5 %collective-permute-start.14 = (bf16[1,768,384]{2,1,0:T(8,128)(2,1)}, bf16[1,768,384]{2,1,0:T(8,128)(2,1)}, u32[]{:S(2)}, u32[]{:S(2)}) collective-permute-start(bf16[1,768,384]{2,1,0:T(8,128)(2,1)} %get-tuple-element.117.after_ref), channel_id=1, source_target_pairs={{0,2},{1,3},{2,0},{3,1},{4,6},{5,7},{6,4},{7,5},{8,10},{9,11},{10,... | collective-permute-start | bytes 1769480 | tf_op jit(solution)/shard_map/ppermute | solution.py:1027
  160.7 1.9 copy-start.10
  163.3 23.3 %collective-permute-start.15 = (bf16[96,768]{1,0:T(8,128)(2,1)}, bf16[96,768]{1,0:T(8,128)(2,1)}, u32[]{:S(2)}, u32[]{:S(2)}) collective-permute-start(bf16[96,768]{1,0:T(8,128)(2,1)} %get-tuple-element.130.refs_8_), channel_id=1, source_target_pairs={{0,0},{3,1},{6,2},{1,3},{4,4},{7,5},{2,6},{5,7},{8,8},{11,9},{14,1... | collective-permute-start | bytes 442376 | tf_op jit(solution)/shard_map/ppermute | solution.py:1232
  166.2 23.1 %collective-permute-start.16 = (bf16[96,768]{1,0:T(8,128)(2,1)}, bf16[96,768]{1,0:T(8,128)(2,1)}, u32[]{:S(2)}, u32[]{:S(2)}) collective-permute-start(bf16[96,768]{1,0:T(8,128)(2,1)} %get-tuple-element.129.refs_9_), channel_id=1, source_target_pairs={{1,0},{4,1},{7,2},{2,3},{5,4},{0,5},{3,6},{6,7},{9,8},{12,9},{15,1... | collective-permute-start | bytes 442376 | tf_op jit(solution)/shard_map/ppermute | solution.py:1232
  166.2 10.4 %copy-start.11 = (bf16[96,768]{1,0:T(8,128)(2,1)S(1)}, bf16[96,768]{1,0:T(8,128)(2,1)}, u32[]{:S(2)}) copy-start(bf16[96,768]{1,0:T(8,128)(2,1)} %get-tuple-element.128.refs_10_) | copy-start | bytes 442372
  176.6 12.7 %collective-permute-start.17 = (bf16[96,768]{1,0:T(8,128)(2,1)S(1)}, bf16[96,768]{1,0:T(8,128)(2,1)S(1)}, u32[]{:S(2)}, u32[]{:S(2)}) collective-permute-start(bf16[96,768]{1,0:T(8,128)(2,1)S(1)} %copy-done.11), channel_id=1, source_target_pairs={{2,0},{5,1},{0,2},{3,3},{6,4},{1,5},{4,6},{7,7},{10,8},{13,9},{8,1... | collective-permute-start | bytes 442376 | tf_op jit(solution)/shard_map/ppermute | solution.py:1232
  181.3 1.8 copy-start.4
  183.2 11.6 %collective-permute-start.19 = (bf16[2,192,384]{2,1,0:T(8,128)(2,1)S(1)}, bf16[2,192,384]{2,1,0:T(8,128)(2,1)S(1)}, u32[]{:S(2)}, u32[]{:S(2)}) collective-permute-start(bf16[2,192,384]{2,1,0:T(8,128)(2,1)S(1)} %copy-done.4), channel_id=1, source_target_pairs={{0,8},{8,0},{16,24},{24,16},{1,9},{9,1},{17,25},{25,17},{2,10},{10... | collective-permute-start | bytes 884744 | tf_op jit(solution)/shard_map/ppermute | solution.py:1027
  186.7 17.3 %collective-permute-start.23 = (bf16[1,192,256]{2,1,0:T(8,128)(2,1)}, bf16[1,192,256]{2,1,0:T(8,128)(2,1)S(1)}, u32[]{:S(2)}, u32[]{:S(2)}) collective-permute-start(bf16[1,192,256]{2,1,0:T(8,128)(2,1)} %get-tuple-element.136.after_ref), channel_id=1, source_target_pairs={{0,16},{8,24},{16,0},{24,8},{1,17},{9,25},{17,1},{25,9},{2,18},{10... | collective-permute-start | bytes 294920 | tf_op jit(solution)/shard_map/ppermute | solution.py:1027
  191.5 10.1 %collective-permute-start.21 = (bf16[2,192,384]{2,1,0:T(8,128)(2,1)S(1)}, bf16[2,192,384]{2,1,0:T(8,128)(2,1)S(1)}, u32[]{:S(2)}, u32[]{:S(2)}) collective-permute-start(bf16[2,192,384]{2,1,0:T(8,128)(2,1)S(1)} %get-tuple-element.125.after_ref), channel_id=1, source_target_pairs={{0,8},{8,0},{16,24},{24,16},{1,9},{9,1},{17,25},{25,17},{2,10},{10... | collective-permute-start | bytes 884744 | tf_op jit(solution)/shard_map/ppermute | solution.py:1027
  192.2 19.7 %all-to-all-start.4 = ((f32[32,16,96]{2,1,0:T(8,128)}), f32[32,16,96]{2,1,0:T(8,128)S(1)}, u32[]{:S(2)}, u32[]{:S(2)}) async-start(f32[32,16,96]{2,1,0:T(8,128)} %bitcast.26), calls=%async_computation.4 | async-start | bytes 524288 | tf_op jit(solution)/shard_map/all_to_all | solution.py:1127
  195.9 2.8 %copy-start.7 = (bf16[1,192,384]{2,1,0:T(8,128)(2,1)}, bf16[1,192,384]{2,1,0:T(8,128)(2,1)S(1)}, u32[]{:S(2)}) copy-start(bf16[1,192,384]{2,1,0:T(8,128)(2,1)S(1)} %constant_dynamic-slice_fusion.2.after_ref) | copy-start | bytes 442372
  195.9 23.9 %collective-permute-start.24 = (bf16[1,192,384]{2,1,0:T(8,128)(2,1)S(1)}, bf16[1,192,384]{2,1,0:T(8,128)(2,1)S(1)}, u32[]{:S(2)}, u32[]{:S(2)}) collective-permute-start(bf16[1,192,384]{2,1,0:T(8,128)(2,1)S(1)} %constant_dynamic-slice_fusion.2.after_ref), channel_id=1, source_target_pairs={{0,16},{8,24},{16,0},{24,8},{1,17},{9,25},{17,1},{25,9},{2,18},{10... | collective-permute-start | bytes 442376 | tf_op jit(solution)/shard_map/ppermute | solution.py:1027
  200.0 1.5 copy-start.2
  200.0 18.0 %collective-permute-start.25 = (bf16[2,96,768]{2,1,0:T(8,128)(2,1)S(1)}, bf16[2,96,768]{2,1,0:T(8,128)(2,1)S(1)}, u32[]{:S(2)}, u32[]{:S(2)}) collective-permute-start(bf16[2,96,768]{2,1,0:T(8,128)(2,1)S(1)} %get-tuple-element.121.after_ref), channel_id=1, source_target_pairs={{0,2},{1,3},{2,0},{3,1},{4,6},{5,7},{6,4},{7,5},{8,10},{9,11},{10,... | collective-permute-start | bytes 884744 | tf_op jit(solution)/shard_map/ppermute | solution.py:1027
  202.7 14.5 %collective-permute-start.22 = (bf16[1,192,384]{2,1,0:T(8,128)(2,1)S(1)}, bf16[1,192,384]{2,1,0:T(8,128)(2,1)S(1)}, u32[]{:S(2)}, u32[]{:S(2)}) collective-permute-start(bf16[1,192,384]{2,1,0:T(8,128)(2,1)S(1)} %constant_dynamic-slice_fusion.1.after_ref), channel_id=1, source_target_pairs={{0,16},{8,24},{16,0},{24,8},{1,17},{9,25},{17,1},{25,9},{2,18},{10... | collective-permute-start | bytes 442376 | tf_op jit(solution)/shard_map/ppermute | solution.py:1027
  212.7 15.8 %all-to-all-start.5 = ((bf16[32,24,256]{2,1,0:T(8,128)(2,1)}), bf16[32,24,256]{2,1,0:T(8,128)(2,1)S(1)}, u32[]{:S(2)}, u32[]{:S(2)}) async-start(bf16[32,24,256]{2,1,0:T(8,128)(2,1)} %bitcast.38), calls=%async_computation.5 | async-start | bytes 786432 | tf_op jit(solution)/shard_map/all_to_all | solution.py:1127
  217.2 11.3 %copy-start.9 = (f32[192,384]{1,0:T(8,128)}, f32[192,384]{1,0:T(8,128)S(1)}, u32[]{:S(2)}) copy-start(f32[192,384]{1,0:T(8,128)S(1)} %add_bitcast_fusion.2) | copy-start | bytes 884740
  218.1 7.7 %collective-permute-start.26 = (bf16[1,96,768]{2,1,0:T(8,128)(2,1)S(1)}, bf16[1,96,768]{2,1,0:T(8,128)(2,1)S(1)}, u32[]{:S(2)}, u32[]{:S(2)}) collective-permute-start(bf16[1,96,768]{2,1,0:T(8,128)(2,1)S(1)} %fusion.1), channel_id=1, source_target_pairs={{0,4},{1,5},{2,6},{3,7},{4,0},{5,1},{6,2},{7,3},{8,12},{9,13},{10,... | collective-permute-start | bytes 442376 | tf_op jit(solution)/shard_map/ppermute | solution.py:1027
  226.5 2.2 copy-start.6
  (5 other events, 4.9 us)
where the time goes:
time: 231 us; the launch traced here: 230 us
  Pallas kernels  102 us (44%)
  starting transfers between devices  54.9 us (24%)
  waiting for transfers between devices  30.2 us (13%)
  local copies, waits for them, and re-layouts  20.6 us (9%)
  other arithmetic  20.6 us (9%)
    pallas_call x13, Pallas kernels, launch(): pl.pallas_call(run, grid=grid, out_shape=tuple(outs) + tuple((shape(v.sha...  102 us
    ppermute x14, starting transfers between devices, begin(): lax.ppermute(send, axis, [(i, i ^ bit) for i in range(count)])  21.2 us
    ppermute x14, waiting for transfers between devices, begin(): lax.ppermute(send, axis, [(i, i ^ bit) for i in range(count)])  10.3 us
    all_to_all x2, waiting for transfers between devices, to_all(): lax.all_to_all(wide, ('dp', 'freq'), split_axis=0, concat_axis=0, tiled=T...  8.97 us
    convert_element_type x3, other arithmetic, step_on(): keep = finish([v[:half] for v in pending]).astype(BF16)  7.99 us
    all_to_all x1, waiting for transfers between devices, body(): lax.all_to_all(conv, 'freq', split_axis=0, concat_axis=0, tiled=True)  6.38 us
    ppermute x3, starting transfers between devices, body(): lax.ppermute(moved[-1], 'freq', [((3 * d + r) % freq, d) for d in range(f...  5.26 us
    ppermute x10, starting transfers between devices, flip(): lax.ppermute(value, 'freq', [(i, i ^ bit) for i in range(freq_parts)])  5.21 us
  transfers between devices with their start and end apart: 33, of which 8 were waited for; matrix products, arithmetic and copies ran while one was open for 16% of the time, Pallas kernels for 38%

commit v1 on v0

--- a/solution.py
+++ b/solution.py
@@ -89,13 +89,13 @@
     return high, (value - high.astype(F32)).astype(BF16)
 
 
-def spectrum_of(block, fhi, flo):
-    return mm(block, fhi) + mm(block, flo)
-
-
-def signal_of(spec, ghi, glo):
+def spectrum_of(block, fhi):
+    return mm(block, fhi)
+
+
+def signal_of(spec, ghi):
     high, low = split_value(spec)
-    return mm(high, ghi) + (mm(low, ghi) + mm(high, glo))
+    return mm(high, ghi) + mm(low, ghi)
 
 
 def each(count, step, unroll):
@@ -106,17 +106,17 @@
         lax.fori_loop(0, count, lambda i, c: (step(i), c)[1], 0)
 
 
-def blocks_to_spectra(x_ref, spec_ref, fhi, flo, batch, width):
+def blocks_to_spectra(x_ref, spec_ref, fhi, batch, width):
     count, chans = x_ref.shape[0], x_ref.shape[1]
     for b in range(batch):
         lanes = slice(b * width, (b + 1) * width)
         if chans % 16 == 0:
             rows = x_ref[:, :, lanes].reshape(count * chans, width)
-            spec_ref[b] = spectrum_of(rows, fhi[...], flo[...]).reshape(count, chans, 2 * width)
+            spec_ref[b] = spectrum_of(rows, fhi[...]).reshape(count, chans, 2 * width)
         else:
 
             def step(j, b=b, lanes=lanes):
-                spec_ref[b, j] = spectrum_of(x_ref[j, :, lanes], fhi[...], flo[...])
+                spec_ref[b, j] = spectrum_of(x_ref[j, :, lanes], fhi[...])
 
             each(count, step, False)
 
@@ -220,29 +220,29 @@
         each(count, row, False)
 
 
-def conv_body(adjoint, batch, x_ref, k_ref, skip_ref, fhi, flo, ghi, glo, out_ref, spec_ref, z_ref):
+def conv_body(adjoint, batch, x_ref, k_ref, skip_ref, fhi, ghi, out_ref, spec_ref, z_ref):
     count, chans = x_ref.shape[:2]
     width = fhi.shape[0]
-    blocks_to_spectra(x_ref, spec_ref, fhi, flo, batch, width)
+    blocks_to_spectra(x_ref, spec_ref, fhi, batch, width)
     conv_products(spec_ref, k_ref, z_ref, batch, width, adjoint)
     for b in range(batch):
         cut = slice(b * width, (b + 1) * width)
         if chans % 16 == 0:
-            y = signal_of(z_ref[b].reshape(count * chans, 2 * width), ghi[...], glo[...])
+            y = signal_of(z_ref[b].reshape(count * chans, 2 * width), ghi[...])
             y = y.reshape(count, chans, width) + skip_ref[...][None] * x_ref[:, :, cut].astype(F32)
             out_ref[:, :, cut] = y.astype(BF16)
         else:
 
             def step(j, b=b, cut=cut):
-                y = signal_of(z_ref[b, j], ghi[...], glo[...])
+                y = signal_of(z_ref[b, j], ghi[...])
                 out_ref[j, :, cut] = (y + skip_ref[...] * x_ref[j, :, cut].astype(F32)).astype(BF16)
 
             each(count, step, False)
 
 
-def forward_kernel(batch, x_ref, s_ref, len_ref, skip_ref, fhi, flo, ghi, glo, out_ref, k_ref, spec_ref, z_ref, raw_ref):
+def forward_kernel(batch, x_ref, s_ref, len_ref, skip_ref, fhi, flo, ghi, out_ref, k_ref, spec_ref, z_ref, raw_ref):
     taps_spectra(s_ref, s_ref.shape[2] - fhi.shape[0], len_ref, fhi, flo, k_ref, raw_ref)
-    conv_body(False, batch, x_ref, k_ref, skip_ref, fhi, flo, ghi, glo, out_ref, spec_ref, z_ref)
+    conv_body(False, batch, x_ref, k_ref, skip_ref, fhi, ghi, out_ref, spec_ref, z_ref)
 
 
 def forward_call(x, batch, width, taps, lens, skip, after=(), carry=()):
@@ -260,8 +260,8 @@
     return launch(
         kernel,
         (1,),
-        (*args, lens, skip, *tabs),
-        [whole(v.shape) for v in (*args, lens, skip, *tabs)],
+        (*args, lens, skip, *tabs[:3]),
+        [whole(v.shape) for v in (*args, lens, skip, *tabs[:3])],
         (shape((count, chans, batch * width), BF16), shape((span, chans, 2 * width), F32)),
         (whole((count, chans, batch * width)), whole((span, chans, 2 * width))),
         [spec, spec, pltpu.VMEM((reach, chans, 2 * width), F32)],
@@ -284,8 +284,8 @@
     return launch(
         functools.partial(adjoint_kernel, batch),
         (1,),
-        (x, k_spec, skip, *tabs),
-        [whole(v.shape) for v in (x, k_spec, skip, *tabs)],
+        (x, k_spec, skip, tabs[0], tabs[2]),
+        [whole(v.shape) for v in (x, k_spec, skip, tabs[0], tabs[2])],
         (shape(x.shape, BF16),),
         (whole(x.shape),),
         [spec, spec],
@@ -320,13 +320,13 @@
         out_ref[count] = wide_quarter(jnp.zeros((chans, 2 * width), F32), raw_ref[count - 1], width)
 
 
-def taps_grad_kernel(x_ref, g_ref, len_ref, fhi, flo, ghi, glo, out_ref, skip_ref, xs_ref, gs_ref, z_ref):
+def taps_grad_kernel(x_ref, g_ref, len_ref, fhi, ghi, out_ref, skip_ref, xs_ref, gs_ref, z_ref):
     count, chans, lanes = g_ref.shape
-    reach = out_ref.shape[0]
+    reach = z_ref.shape[0]
     width = fhi.shape[0]
     batch = lanes // width
-    blocks_to_spectra(x_ref, xs_ref, fhi, flo, batch, width)
-    blocks_to_spectra(g_ref, gs_ref, fhi, flo, batch, width)
+    blocks_to_spectra(x_ref, xs_ref, fhi, batch, width)
+    blocks_to_spectra(g_ref, gs_ref, fhi, batch, width)
     if small(count, chans, width):
 
         def step(rows, lane):
@@ -343,7 +343,7 @@
                 put_pair(z_ref, (d,), rows, lane, width, total[d])
 
         tiles(chans, width, step)
-        rows = signal_of(z_ref[...].reshape(reach * chans, 2 * width), ghi[...], glo[...])
+        rows = signal_of(z_ref[...].reshape(reach * chans, 2 * width), ghi[...])
         rows = rows.reshape(reach, chans, width)
         pieces = [rows[d] for d in range(reach)]
     else:
@@ -367,30 +367,37 @@
             z_ref[d] = total
 
         each(reach, lag, False)
-        pieces = [signal_of(z_ref[d], ghi[...], glo[...]) for d in range(reach)]
+        pieces = [signal_of(z_ref[d], ghi[...]) for d in range(reach)]
     full = jnp.concatenate(pieces, axis=1)
     place = lax.broadcasted_iota(jnp.int32, (1, reach * width), 1)
     full = pooled_rows(jnp.where(place < len_ref[...], full, 0.0))
-    for d in range(reach):
-        out_ref[d] = full[:, d * width : (d + 1) * width].astype(BF16)
+    if len(out_ref.shape) == 4:
+        per = out_ref.shape[2]
+        for q in range(out_ref.shape[0]):
+            for d in range(reach):
+                out_ref[q, d] = full[q * per : (q + 1) * per, d * width : (d + 1) * width].astype(BF16)
+    else:
+        for d in range(reach):
+            out_ref[d] = full[:, d * width : (d + 1) * width].astype(BF16)
     dot = jnp.zeros((chans, lanes), F32)
     for j in range(count):
         dot = dot + x_ref[j, :, :lanes].astype(F32) * g_ref[j].astype(F32)
     skip_ref[...] = jnp.sum(dot, axis=1, keepdims=True)
 
 
-def taps_grad_call(x, g, lens, width, reach, after=(), carry=()):
+def taps_grad_call(x, g, lens, width, reach, split, after=(), carry=()):
     count, chans, lanes = g.shape
     batch = lanes // width
     tabs = tables(width)
     spec = pltpu.VMEM((batch, count, chans, 2 * width), F32)
+    made = (split, reach, chans // split, width) if split else (reach, chans, width)
     return launch(
         taps_grad_kernel,
         (1,),
-        (x, g, lens, *tabs,),
-        [whole(v.shape) for v in (x, g, lens, *tabs)],
-        (shape((reach, chans, width), BF16), shape((chans, 1), F32)),
-        (whole((reach, chans, width)), whole((chans, 1))),
+        (x, g, lens, tabs[0], tabs[2]),
+        [whole(v.shape) for v in (x, g, lens, tabs[0], tabs[2])],
+        (shape(made, BF16), shape((chans, 1), F32)),
+        (whole(made), whole((chans, 1))),
         [spec, spec, pltpu.VMEM((reach, chans, 2 * width), F32)],
         cost(x.size * width * 20, x.size * 6),
         "taps_gradient",
@@ -416,24 +423,30 @@
     return position >= limit
 
 
-def front_kernel(batch, tok_rows, offs_ref, tok, gain, bias, wv, wg, ws, bv, bg, bs, taps, normed, mixed, value, gate, second):
+def front_kernel(batch, tok_rows, offs_ref, tok, gain, bias, wv, wg, ws, in_bias, taps, normed, mixed, value, gate, second, spread):
     rows = tok.shape[0]
+    cut = wv.shape[1]
+    per = in_bias.shape[0] // (3 * cut)
 
     @pl.when(pl.program_id(0) == 0)
     def _():
         n, _ = normalized(tok[...].astype(F32))
+        row = in_bias[...].reshape(1, -1)
+        for k in range(3 * per):
+            spread[k] = row[:, k * cut : (k + 1) * cut]
         normed[...] = (n * gain[...].reshape(1, -1) + bias[...].reshape(1, -1)).astype(BF16)
 
     x = normed[...]
-    v = mm(x, wv[...]) + bv[...]
-    g = mm(x, wg[...]) + bg[...]
+    step = pl.program_id(0)
+    v = mm(x, wv[...]) + spread[step]
+    g = mm(x, wg[...]) + spread[per + step]
     live = live_rows(offs_ref, batch, tok_rows, rows)
     mixed[:, :rows] = jnp.where(live, g * v, 0.0).T.astype(BF16)
     t = taps[...]
     mixed[:, rows:] = (t - SHRINK * jnp.tanh(t / SHRINK)).astype(BF16)
     value[...] = jnp.where(live, v, 0.0).astype(BF16)
     gate[...] = jnp.where(live, g, 0.0).astype(BF16)
-    second[...] = (mm(x, ws[...]) + bs[...]).astype(BF16)
+    second[...] = (mm(x, ws[...]) + spread[2 * per + step]).astype(BF16)
 
 
 def front_call(tok, offsets, gain, bias, weight, in_bias, taps, batch, tok_rows):
@@ -452,10 +465,10 @@
     return launch(
         functools.partial(front_kernel, batch, tok_rows),
         (per,),
-        (offsets, tok, gain, bias, weight, weight, weight, in_bias, in_bias, in_bias, taps),
+        (offsets, tok, gain, bias, weight, weight, weight, in_bias, taps),
         [smem(), pl.BlockSpec((rows, width), full), whole((width,)), whole((width,))]
         + [pl.BlockSpec((width, cut), col(k)) for k in range(3)]
-        + [pl.BlockSpec((1, cut), col(k)) for k in range(3)]
+        + [whole(in_bias.shape)]
         + [pl.BlockSpec((cut, taps.shape[1]), lambda i: (i, 0))],
         (act, shape((width, span), BF16), act, act, act),
         (
@@ -465,7 +478,7 @@
             pl.BlockSpec((rows, cut), lambda i: (0, i)),
             pl.BlockSpec((rows, cut), lambda i: (0, i)),
         ),
-        [],
+        [pltpu.VMEM((3 * per, 1, cut), F32)],
         cost(2 * rows * width * 3 * width, weight.size * 2 + rows * width * 12),
         "norm_project",
             )
@@ -509,7 +522,7 @@
 
 
 def mlp_kernel(paired, freq_parts, tok, convt, second, wo, ob, gain, bias, wup, b1, ag_ref, cot, pack, res, b1g, rgrad, convgt, sgrad, mine_t, other_t, vecs, *rest):
-    mine, (n2, gn, conv, acc) = rest[:-4], rest[-4:]
+    mine, (n2, gn, conv, acc, wide) = rest[:-5], rest[-5:]
     step = pl.program_id(0)
     cut, part = wup.shape[1], gn.shape[2]
     core = lax.rem(lax.axis_index("freq"), 2)
@@ -520,7 +533,8 @@
         conv[...] = c.astype(BF16)
         g = (second[...].astype(F32) * c).astype(BF16)
         r = tok[...].astype(F32) + (mm(g, wo[...]) + ob[...])
-        res[...] = r
+        res[...] = r.astype(BF16)
+        wide[...] = r
         n, _ = normalized(r)
         m = (n * gain[...] + bias[...]).astype(BF16)
         n2[...] = m
@@ -555,12 +569,12 @@
     @pl.when(step == pl.num_programs(0) - 1)
     def _():
         ng = acc[...]
-        n, rate = normalized(res[...])
+        n, rate = normalized(wide[...])
         e = ng * gain[...]
         pulled = e - jnp.mean(e, axis=-1, keepdims=True) - n * jnp.mean(e * n, axis=-1, keepdims=True)
         r = cot[...].astype(F32) + rate * pulled
-        rgrad[...] = r
         br = r.astype(BF16)
+        rgrad[...] = br
         brf = br.astype(F32)
         gg = mm(br, wo[...], NT)
         convgt[...] = (gg * second[...].astype(F32)).T.astype(BF16)
@@ -593,7 +607,7 @@
     act = shape((rows, width), BF16)
     mine = [shape((rows, ff // 2), BF16)] if paired else []
     turned, turned_spec = shape((width, rows), BF16), pl.BlockSpec((width, rows), full)
-    wide = shape((rows, width), F32)
+    wide = act
     return launch(
         functools.partial(mlp_kernel, paired, freq_parts),
         (steps,),
@@ -624,7 +638,7 @@
             pl.BlockSpec((8, width), full),
             *[pl.BlockSpec((rows, cut // 2), along) for _ in mine],
         ),
-        [pltpu.VMEM((rows, width), BF16), pltpu.VMEM((steps, rows, part), BF16), pltpu.VMEM((rows, width), BF16), pltpu.VMEM((rows, width), F32)],
+        [pltpu.VMEM((rows, width), BF16), pltpu.VMEM((steps, rows, part), BF16), pltpu.VMEM((rows, width), BF16), pltpu.VMEM((rows, width), F32), pltpu.VMEM((rows, width), F32)],
         cost(2 * rows * width * (2 * ff + width), wup.size * 4 + rows * ff * 4 + rows * width * 14, rows * ff),
         "mix_out_mlp",
         after,
@@ -667,7 +681,7 @@
 
     @pl.when(step == 0)
     def _():
-        acc[...] = res[...] + b2[...] + part
+        acc[...] = res[...].astype(F32) + b2[...] + part
 
     @pl.when(step > 0)
     def _():
@@ -728,7 +742,7 @@
         vecs[1:2] = jnp.sum(ng, axis=0, keepdims=True)
         e = ng * gain[...]
         pulled = e - jnp.mean(e, axis=-1, keepdims=True) - n * jnp.mean(e * n, axis=-1, keepdims=True)
-        out[...] = (rgrad[...] + rate * pulled).astype(BF16)
+        out[...] = (rgrad[...].astype(F32) + rate * pulled).astype(BF16)
 
 
 def back_call(mgt, value, gate, sgrad, weight, tok, gain, rgrad, after=(), carry=()):
@@ -1162,7 +1176,7 @@
 
     cut = 768
     normed, mixed_t, value, gate, gate_two = front_call(
-        tok, offsets, norm1_gain, norm1_bias, w_in, row(in_bias), kernel_taps, batch, tok_rows
+        tok, offsets, norm1_gain, norm1_bias, w_in, in_bias, kernel_taps, batch, tok_rows
     )
     mixed = lax.all_to_all(mixed_t.reshape(freq, chans, -1), "freq", split_axis=0, concat_axis=0, tiled=True)
     taps = mixed if tap_rows == tok_rows else reblocked(mixed[:, :, rows:], reach, tok_rows)
@@ -1214,10 +1228,12 @@
     fc2_sum, sent = step_on((keep, fc2_sum[1]), "dp", deep, 1)
     mixer_sum, sent_m = step_on((once(keep_m, sent), mixer_sum[1]), "freq", low, 1)
     (taps_g, skip_g), (keep, keep_1, keep_m) = taps_grad_call(
-        mixed, convg, lens, tok_rows, reach, after=(owned, sent_m), carry=(fc2_sum[0], fc1_sum[0], mixer_sum[0])
+        mixed, convg, lens, tok_rows, reach, dp if tap_rows == tok_rows else 0, after=(owned, sent_m), carry=(fc2_sum[0], fc1_sum[0], mixer_sum[0])
     )
     fc2_sum = (keep, fc2_sum[1])
-    taps_g = reblocked(taps_g, freq, tap_rows).reshape(freq, dp, chans // dp, tap_rows).transpose(1, 0, 2, 3).reshape(dp, width // dp, tap_rows)
+    if tap_rows != tok_rows:
+        taps_g = reblocked(taps_g, freq, tap_rows).reshape(freq, dp, chans // dp, tap_rows).transpose(1, 0, 2, 3)
+    taps_g = taps_g.reshape(dp, width // dp, tap_rows)
     taps_sum, sent_t = across_first(taps_g)
     fc1_sum, sent_1 = step_on((once(keep_1, sent_t), fc1_sum[1]), "freq", high, 1)
     mixer_sum = (once(keep_m, sent_1), mixer_sum[1])
@@ -1230,9 +1246,15 @@
         part = lax.rem((freq % 3) * (r - me + 3 * freq), 3)
         moved.append(lax.dynamic_index_in_dim(parts, part, 0, keepdims=False))
         pieces.append(lax.ppermute(moved[-1], "freq", [((3 * d + r) % freq, d) for d in range(freq)]))
+    fc2_sum = (once(keep, moved[0]), fc2_sum[1])
+    for level in range(2, len(deep)):
+        fc2_sum, _ = step_on(fc2_sum, "dp", deep, level)
+    half = chips // 2
+    sent = finish([v[0, half:] for v in fc2_sum]).astype(BF16)
+    fc2_sum = begin(finish([v[0, :half] for v in fc2_sum]).astype(BF16), sent, "freq", low[0])
     (input_grad, vec_one), (keep, keep_1, keep_t) = back_call(
         mixed_grad_t, value, gate, sgrad, w_in, tok, row(norm1_gain), rgrad,
-        after=tuple(moved), carry=(fc2_sum[0], fc1_sum[0], taps_sum[0]),
+        after=(*moved, sent), carry=(fc2_sum[0], fc1_sum[0], taps_sum[0]),
     )
     fa = ff // freq
     fc1_sum = (keep_1, fc1_sum[1])
@@ -1244,18 +1266,14 @@
     taps_sum, sent_t = across_next((keep_t, taps_sum[1]))
     second = jnp.concatenate(pieces + [once(mixer[:chans], sent_t)], axis=0).T.reshape(dp, width // dp, 4 * chans)
     second, sent = across_first(second)
-    first = (once(first[0], sent), first[1])
+    first = (once(once(first[0], sent), final), first[1])
     first, sent = across_next(first)
     fc2_sum = (once(keep, sent), fc2_sum[1])
-    for level in range(2, len(deep)):
-        fc2_sum, _ = step_on(fc2_sum, "dp", deep, level)
-    half = chips // 2
-    sent = finish([v[0, half:] for v in fc2_sum]).astype(BF16)
-    fc2_sum = begin(finish([v[0, :half] for v in fc2_sum]).astype(BF16), sent, "freq", low[0])
+    fc2_sum, sent = step_on(fc2_sum, "freq", low, 1)
     second, sent = across_next((once(second[0], sent), second[1]))
     quarter_sum = across_rest((once(taps_sum[0], sent), taps_sum[1])).astype(BF16).reshape(freq, chans // dp, tap_rows)
     spread = to_all(quarter_sum)
-    for level in range(1, len(low) + 1):
+    for level in range(2, len(low) + 1):
         fc2_sum, _ = step_on(fc2_sum, "freq", low, level)
     first, second = across_rest(first), across_rest(second)
     fc1_final, in_final, out_final = first, second[:, : 3 * chans], second[:, 3 * chans :]

time: 231 us -> 228 us (0.987)
  Pallas kernels: 102 us -> 97.7 us
    pallas_call x13, Pallas kernels: 102 us -> 97.7 us  [launch(): pl.pallas_call(run, grid=grid, out_shape=tuple(outs) + tuple((shape(v.sha...]
    ppermute x14, starting transfers between devices: 21.2 us -> 16.8 us  [begin(): lax.ppermute(send, axis, [(i, i ^ bit) for i in range(count)])]
    all_to_all x2, starting transfers between devices: 5.2 us -> 9.08 us  [to_all(): lax.all_to_all(wide, ('dp', 'freq'), split_axis=0, concat_axis=0, tiled=T...]
  transfers between devices with their start and end apart: 33 -> 33, of which waited for: 8 -> 9; matrix products, arithmetic and copies ran while one was open for 16% -> 17% of each run, Pallas kernels for 38% -> 37%
where the time goes in v1:
time: 228 us; the launch traced here: 227 us
  Pallas kernels  97.7 us (43%)
  starting transfers between devices  54.2 us (24%)
  waiting for transfers between devices  30.7 us (13%)
  other arithmetic  22.4 us (10%)
  local copies, waits for them, and re-layouts  20.8 us (9%)
    pallas_call x13, Pallas kernels, launch(): pl.pallas_call(run, grid=grid, out_shape=tuple(outs) + tuple((shape(v.sha...  97.7 us
    ppermute x14, starting transfers between devices, begin(): lax.ppermute(send, axis, [(i, i ^ bit) for i in range(count)])  16.8 us
    all_to_all x2, waiting for transfers between devices, to_all(): lax.all_to_all(wide, ('dp', 'freq'), split_axis=0, concat_axis=0, tiled=T...  10.1 us
    all_to_all x2, starting transfers between devices, to_all(): lax.all_to_all(wide, ('dp', 'freq'), split_axis=0, concat_axis=0, tiled=T...  9.08 us
    ppermute x14, waiting for transfers between devices, begin(): lax.ppermute(send, axis, [(i, i ^ bit) for i in range(count)])  8.68 us
    convert_element_type x3, other arithmetic, step_on(): keep = finish([v[:half] for v in pending]).astype(BF16)  7.98 us
    all_to_all x1, waiting for transfers between devices, body(): lax.all_to_all(conv, 'freq', split_axis=0, concat_axis=0, tiled=True)  6.37 us
    ppermute x3, starting transfers between devices, body(): lax.ppermute(moved[-1], 'freq', [((3 * d + r) % freq, d) for d in range(f...  5.41 us
  transfers between devices with their start and end apart: 33, of which 9 were waited for; matrix products, arithmetic and copies ran while one was open for 17% of the time, Pallas kernels for 37%

profile of v1, /device:TPU:0, one launch (start us, length us, event | category | flops | bytes accessed | tf_op | source)
XLA Modules:
  0.0 226.9 jit_solution(8155307972142388633)
XLA Ops:
  0.7 6.6 %norm_project.1 = (bf16[512,768]{1,0:T(8,128)(2,1)}, bf16[768,768]{1,0:T(8,128)(2,1)}, bf16[512,768]{1,0:T(8,128)(2,1)}, bf16[512,768]{1,0:T(8,128)(2,1)}, bf16[512,768]{1,0:T(8,128)(2,1)}) custom-call(s32[2]{0:T(128)} %refs_0_.3, bf16[512,768]{1,0:T(8,128)(2,1)} %bitcast.102, f32[768]{0:T(1024)} %refs_2_.1, f32[768]{0:T(1024)} %refs_3_.5, ...), custom_call_target="tpu_custom_call" | custom-call | flops 115964116992 | bytes 528482304 | tf_op jit(solution)/shard_map/norm_project/pallas_call | solution.py:51
  7.3 5.2 %all-to-all-start = ((bf16[8,96,768]{2,1,0:T(8,128)(2,1)}), bf16[8,96,768]{2,1,0:T(8,128)(2,1)}, u32[]{:S(2)}, u32[]{:S(2)}) async-start(bf16[8,96,768]{2,1,0:T(8,128)(2,1)} %bitcast.91), calls=%async_computation | async-start | bytes 2359296 | tf_op jit(solution)/shard_map/all_to_all | solution.py:1181
  13.0 6.9 %active_grad.1 = (bf16[512,3072]{1,0:T(8,128)(2,1)}, f32[1,768]{1,0:T(1,128)}, bf16[384,512]{1,0:T(8,128)(2,1)}, bf16[384,512]{1,0:T(8,128)(2,1)}) custom-call(bf16[512,768]{1,0:T(8,128)(2,1)} %bitcast.100, bf16[3072,768]{1,0:T(8,128)(2,1)} %refs_1_.3, bf16[768,768]{1,0:T(8,128)(2,1)} %get-tuple-element.65.refs_2_), custom_call_target="tpu_custom_call" | custom-call | flops 154618822656 | bytes 503316480 | tf_op jit(solution)/shard_map/active_grad/pallas_call | solution.py:51
  19.9 1.3 constant_dynamic-slice_fusion.5
  25.5 3.9 %all-to-all-done.refs_0_ = bf16[8,96,768]{2,1,0:T(8,128)(2,1)} async-done(((bf16[8,96,768]{2,1,0:T(8,128)(2,1)}), bf16[8,96,768]{2,1,0:T(8,128)(2,1)}, u32[]{:S(2)}, u32[]{:S(2)}) %all-to-all-start) | async-done | bytes 1179680 | tf_op jit(solution)/shard_map/all_to_all | solution.py:1181
  29.4 6.9 %conv_forward.1 = (bf16[8,96,512]{2,1,0:T(8,128)(2,1)}, f32[8,96,512]{2,1,0:T(8,128)}, bf16[384,512]{1,0:T(8,128)(2,1)}, bf16[512,768]{1,0:T(8,128)(2,1)}, bf16[512,768]{1,0:T(8,128)(2,1)}) custom-call(bf16[8,96,768]{2,1,0:T(8,128)(2,1)} %all-to-all-done.refs_0_, ...), custom_call_target="tpu_custom_call", output_to_operand_aliasing={{2}: (9, {}), {3}: (10, {}), {4}: (11, {})} | custom-call | flops 193273528320 | bytes 369098752 | tf_op jit(solution)/shard_map/conv_forward/pallas_call | solution.py:51
  36.4 3.9 %all-to-all-start.1 = ((bf16[8,96,512]{2,1,0:T(8,128)(2,1)}), bf16[8,96,512]{2,1,0:T(8,128)(2,1)S(1)}, u32[]{:S(2)}, u32[]{:S(2)}) async-start(bf16[8,96,512]{2,1,0:T(8,128)(2,1)} %get-tuple-element.69), calls=%async_computation.1 | async-start | bytes 1572864 | tf_op jit(solution)/shard_map/all_to_all | solution.py:1187
  43.3 1.7 collective-permute-start.3
  45.0 1.5 collective-permute-start.4
  46.8 6.4 %all-to-all-done.1 = bf16[8,96,512]{2,1,0:T(8,128)(2,1)S(1)} async-done(((bf16[8,96,512]{2,1,0:T(8,128)(2,1)}), bf16[8,96,512]{2,1,0:T(8,128)(2,1)S(1)}, u32[]{:S(2)}, u32[]{:S(2)}) %all-to-all-start.1) | async-done | bytes 786464 | tf_op jit(solution)/shard_map/all_to_all | solution.py:1187
  54.0 19.4 %mix_out_mlp.1 = (bf16[512,6144]{1,0:T(8,128)(2,1)}, bf16[512,768]{1,0:T(8,128)(2,1)}, f32[1,3072]{1,0:T(1,128)}, bf16[512,768]{1,0:T(8,128)(2,1)}, bf16[768,512...) custom-call(bf16[512,768]{1,0:T(8,128)(2,1)} %bitcast.103, ...), custom_call_target="tpu_custom_call" | custom-call | flops 347892350976 | bytes 1358954496 | tf_op jit(solution)/shard_map/mix_out_mlp/pallas_call | solution.py:51
  73.4 4.2 %all-to-all-start.2 = ((bf16[8,96,512]{2,1,0:T(8,128)(2,1)}), bf16[8,96,512]{2,1,0:T(8,128)(2,1)}, u32[]{:S(2)}, u32[]{:S(2)}) async-start(bf16[8,96,512]{2,1,0:T(8,128)(2,1)} %bitcast.93), calls=%async_computation.2 | async-start | bytes 1572864 | tf_op jit(solution)/shard_map/all_to_all | solution.py:1197
  78.2 7.2 %block_out.1.refs_4_ = bf16[512,768]{1,0:T(8,128)(2,1)} custom-call(bf16[512,6144]{1,0:T(8,128)(2,1)} %get-tuple-element.71.refs_0_.refs_1_.refs_2_, bf16[3072,768]{1,0:T(8,128)(2,1)} %refs_1_.3, bf16[512,768]{1,0:T(8,128)(2,1)} %get-tuple-element.72.refs_2_, f32[1,768]{1,0:T(1,128)} %reshape.154.refs_3_), custom_call_target="tpu_custom_call" | custom-call | flops 154618822656 | bytes 704643072 | tf_op jit(solution)/shard_map/block_out/pallas_call | solution.py:51
  85.4 1.6 collective-permute-done.5.refs_7_
  87.0 7.1 %fc2_gradient.1 = (bf16[2,4,96,768]{3,2,1,0:T(8,128)(2,1)}, bf16[2,4,96,768]{3,2,1,0:T(8,128)(2,1)}, bf16[512,768]{1,0:T(8,128)(2,1)}, bf16[512,768]{1,0:T(8,128)(2,1)}, bf16[512,768]{1,0:T(8,128)(2,1)}) custom-call(bf16[384,512]{1,0:T(8,128)(2,1)} %get-tuple-element.76.refs_0_, ...), custom_call_target="tpu_custom_call", output_to_operand_aliasing={{2}: (5, {}), {3}: (6, {}), {4}: (7, {})} | custom-call | flops 154618822656 | bytes 402653184 | tf_op jit(solution)/shard_map/fc2_gradient/pallas_call | solution.py:51
  94.6 2.0 collective-permute-start.10
  96.6 7.8 %fc1_gradient.1 = (bf16[2,768,384]{2,1,0:T(8,128)(2,1)}, bf16[2,768,384]{2,1,0:T(8,128)(2,1)}) custom-call(bf16[512,6144]{1,0:T(8,128)(2,1)} %get-tuple-element.71.refs_0_.refs_1_.refs_2_, bf16[512,6144]{1,0:T(8,128)(2,1)} %get-tuple-element.71.refs_0_.refs_1_.refs_2_, bf16[512,1536]{1,0:T(8,128)(2,1)} %get-tuple-element.75.refs_2_, ...), custom_call_target="tpu_custom_call" | custom-call | flops 154618822656 | bytes 503316480 | tf_op jit(solution)/shard_map/fc1_gradient/pallas_call | solution.py:51
  105.0 6.0 %conv_adjoint.1.refs_8_.refs_3_ = bf16[8,96,512]{2,1,0:T(8,128)(2,1)} custom-call(bf16[8,96,512]{2,1,0:T(8,128)(2,1)} %all-to-all-done.2.refs_0_.refs_1_, f32[8,96,512]{2,1,0:T(8,128)} %get-tuple-element.74.refs_1_, f32[96,1]{1,0:T(8,128)} %copy.91.refs_2_, bf16[256,512]{1,0:T(8,128)(2,1)} %constant.125.clone.refs_3_, ...), custom_call_target="tpu_custom_call" | custom-call | flops 128849018880 | bytes 268435456 | tf_op jit(solution)/shard_map/conv_adjoint/pallas_call | solution.py:51
  111.0 4.4 %all-to-all-start.3 = ((bf16[8,96,512]{2,1,0:T(8,128)(2,1)}), bf16[8,96,512]{2,1,0:T(8,128)(2,1)}, u32[]{:S(2)}, u32[]{:S(2)}) async-start(bf16[8,96,512]{2,1,0:T(8,128)(2,1)} %conv_adjoint.1.refs_8_.refs_3_), calls=%async_computation.3 | async-start | bytes 1572864 | tf_op jit(solution)/shard_map/all_to_all | solution.py:1221
  115.6 5.1 %mixer_gradient.1 = (bf16[2,192,768]{2,1,0:T(8,128)(2,1)}, bf16[2,192,768]{2,1,0:T(8,128)(2,1)}) custom-call(bf16[768,512]{1,0:T(8,128)(2,1)} %get-tuple-element.89.refs_0_, bf16[512,6144]{1,0:T(8,128)(2,1)} %get-tuple-element.71.refs_0_.refs_1_.refs_2_, bf16[512,6144]{1,0:T(8,128)(2,1)} %get-tuple-element.71.refs_0_.refs_1_.refs_2_, ...), custom_call_target="tpu_custom_call" | custom-call | flops 77309411328 | bytes 402653184 | tf_op jit(solution)/shard_map/mixer_gradient/pallas_call | solution.py:51
  120.7 1.7 collective-permute-start.11
  123.4 8.3 %owner_gradients.1 = (bf16[192,768]{1,0:T(8,128)(2,1)}, bf16[2,4,96,768]{3,2,1,0:T(8,128)(2,1)}, bf16[2,192,768]{2,1,0:T(8,128)(2,1)}) custom-call(s32[2]{0:T(128)} %refs_0_.3, bf16[192,768]{1,0:T(8,128)(2,1)} %maximum_bitcast_fusion.1.refs_7_.refs_1_, f32[192,1]{1,0:T(8,128)} %copy.92.refs_8_.refs_2_, ...), custom_call_target="tpu_custom_call", output_to_operand_aliasing={{1}: (13, {}), {2}: (14, {})} | custom-call | flops 154618822656 | bytes 402653184 | tf_op jit(solution)/shard_map/owner_gradients/pallas_call | solution.py:51
  131.7 2.9 %add_convert_fusion.3 = (bf16[1,4,96,768]{3,2,1,0:T(8,128)(2,1)}, bf16[1,4,96,768]{3,2,1,0:T(8,128)(2,1)}) fusion(bf16[2,4,96,768]{3,2,1,0:T(8,128)(2,1)} %collective-permute-done.10, bf16[2,4,96,768]{3,2,1,0:T(8,128)(2,1)} %get-tuple-element.95), kind=kLoop, calls=%fused_computation.3 | loop fusion | flops 2359296 | bytes 3538944 | tf_op jit(solution)/shard_map/convert_element_type | solution.py:1053
  134.6 2.6 %collective-permute-start.14 = (bf16[1,4,96,768]{3,2,1,0:T(8,128)(2,1)}, bf16[1,4,96,768]{3,2,1,0:T(8,128)(2,1)}, u32[]{:S(2)}, u32[]{:S(2)}) collective-permute-start(bf16[1,4,96,768]{3,2,1,0:T(8,128)(2,1)} %get-tuple-element.119.after_ref), channel_id=1, source_target_pairs={{0,16},{8,24},{16,0},{24,8},{1,17},{9,25},{17,1},{25,9},{2,18},{10... | collective-permute-start | bytes 1769480 | tf_op jit(solution)/shard_map/ppermute | solution.py:1041
  137.2 2.4 %collective-permute-done.11 = bf16[2,192,768]{2,1,0:T(8,128)(2,1)} collective-permute-done((bf16[2,192,768]{2,1,0:T(8,128)(2,1)}, bf16[2,192,768]{2,1,0:T(8,128)(2,1)}, u32[]{:S(2)}, u32[]{:S(2)}) %collective-permute-start.11) | collective-permute-done | bytes 589856 | tf_op jit(solution)/shard_map/ppermute | solution.py:1041
  139.6 2.2 add_convert_fusion.10
  141.7 1.5 collective-permute-start.13
  143.2 7.1 %taps_gradient.1 = (bf16[4,8,24,256]{3,2,1,0:T(8,128)(2,1)}, f32[96,1]{1,0:T(8,128)}, bf16[1,4,96,768]{3,2,1,0:T(8,128)(2,1)}, bf16[2,768,384]{2,1,0:T(8,128)(2,1)}, bf16[1,192,768]{2,1,0:T(8,128)(2,1)}) custom-call(bf16[8,96,768]{2,1,0:T(8,128)(2,1)} %all-to-all-done.refs_0_, ...), custom_call_target="tpu_custom_call", output_to_operand_aliasing={{2}: (7, {}), {3}: (8, {}), {4}: (9, {})} | custom-call | flops 193273528320 | bytes 226492416 | tf_op jit(solution)/shard_map/taps_gradient/pallas_call | solution.py:51
  150.3 1.8 dynamic-slice_bitcast_fusion.4
  152.2 2.9 %add_convert_fusion.1 = (bf16[1,768,384]{2,1,0:T(8,128)(2,1)}, bf16[1,768,384]{2,1,0:T(8,128)(2,1)}) fusion(bf16[2,768,384]{2,1,0:T(8,128)(2,1)} %collective-permute-done.12, bf16[2,768,384]{2,1,0:T(8,128)(2,1)} %gate.11), kind=kLoop, calls=%fused_computation.1 | loop fusion | flops 2359296 | bytes 3538944 | tf_op jit(solution)/shard_map/convert_element_type | solution.py:1053
  155.6 1.2 add_convert_fusion.9
  158.3 2.8 %collective-permute-start.16 = (bf16[96,768]{1,0:T(8,128)(2,1)}, bf16[96,768]{1,0:T(8,128)(2,1)}, u32[]{:S(2)}, u32[]{:S(2)}) collective-permute-start(bf16[96,768]{1,0:T(8,128)(2,1)} %get-tuple-element.130.after_ref.refs_8_), channel_id=1, source_target_pairs={{0,0},{3,1},{6,2},{1,3},{4,4},{7,5},{2,6},{5,7},{8,8},{11,9},{14,1... | collective-permute-start | bytes 442376 | tf_op jit(solution)/shard_map/ppermute | solution.py:1248
  161.1 2.6 %collective-permute-done.14 = bf16[1,4,96,768]{3,2,1,0:T(8,128)(2,1)} collective-permute-done((bf16[1,4,96,768]{3,2,1,0:T(8,128)(2,1)}, bf16[1,4,96,768]{3,2,1,0:T(8,128)(2,1)}, u32[]{:S(2)}, u32[]{:S(2)}) %collective-permute-start.14) | collective-permute-done | bytes 589856 | tf_op jit(solution)/shard_map/ppermute | solution.py:1041
  163.7 2.6 %collective-permute-start.18 = (bf16[96,768]{1,0:T(8,128)(2,1)}, bf16[96,768]{1,0:T(8,128)(2,1)}, u32[]{:S(2)}, u32[]{:S(2)}) collective-permute-start(bf16[96,768]{1,0:T(8,128)(2,1)} %get-tuple-element.128.refs_10_), channel_id=1, source_target_pairs={{2,0},{5,1},{0,2},{3,3},{6,4},{1,5},{4,6},{7,7},{10,8},{13,9},{8,1... | collective-permute-start | bytes 442376 | tf_op jit(solution)/shard_map/ppermute | solution.py:1248
  166.3 2.2 fusion.1
  168.5 7.4 %project_back.1 = (bf16[512,768]{1,0:T(8,128)(2,1)}, f32[8,768]{1,0:T(8,128)}, bf16[2,96,768]{2,1,0:T(8,128)(2,1)}, bf16[1,768,384]{2,1,0:T(8,128)(2,1)}, bf16[2,192,256]{2,1,0:T(8,128)(2,1)}) custom-call(bf16[768,512]{1,0:T(8,128)(2,1)} %bitcast.11.refs_0_, ...), custom_call_target="tpu_custom_call", output_to_operand_aliasing={{2}: (12, {}), {3}: (13, {}), {4}: (14, {})} | custom-call | flops 237494511599616 | bytes 1288490188800 | tf_op jit(solution)/shard_map/project_back/pallas_call | solution.py:51
  175.9 1.4 add_convert_fusion
  178.8 1.8 pack_vectors.1
  180.6 5.0 %all-to-all-start.4 = ((f32[32,16,96]{2,1,0:T(8,128)}), f32[32,16,96]{2,1,0:T(8,128)S(1)}, u32[]{:S(2)}, u32[]{:S(2)}) async-start(f32[32,16,96]{2,1,0:T(8,128)} %bitcast.97), calls=%async_computation.4 | async-start | bytes 524288 | tf_op jit(solution)/shard_map/all_to_all | solution.py:1141
  185.6 1.8 collective-permute-start.21
  189.2 2.4 %collective-permute-start.24 = (bf16[1,192,256]{2,1,0:T(8,128)(2,1)}, bf16[1,192,256]{2,1,0:T(8,128)(2,1)S(1)}, u32[]{:S(2)}, u32[]{:S(2)}) collective-permute-start(bf16[1,192,256]{2,1,0:T(8,128)(2,1)} %get-tuple-element.136.after_ref), channel_id=1, source_target_pairs={{0,16},{8,24},{16,0},{24,8},{1,17},{9,25},{17,1},{25,9},{2,18},{10... | collective-permute-start | bytes 294920 | tf_op jit(solution)/shard_map/ppermute | solution.py:1041
  193.8 1.5 collective-permute-start.22
  195.4 2.7 %all-to-all-done.4.after_ref = f32[32,16,96]{2,1,0:T(8,128)S(1)} async-done(((f32[32,16,96]{2,1,0:T(8,128)}), f32[32,16,96]{2,1,0:T(8,128)S(1)}, u32[]{:S(2)}, u32[]{:S(2)}) %all-to-all-start.4) | async-done | bytes 196640 | tf_op jit(solution)/shard_map/all_to_all | solution.py:1141
  201.5 1.3 collective-permute-start.26
  202.8 2.2 collective-permute-done.22
  208.4 4.1 %all-to-all-start.5 = ((bf16[32,24,256]{2,1,0:T(8,128)(2,1)}), bf16[32,24,256]{2,1,0:T(8,128)(2,1)S(1)}, u32[]{:S(2)}, u32[]{:S(2)}) async-start(bf16[32,24,256]{2,1,0:T(8,128)(2,1)} %bitcast.36), calls=%async_computation.5 | async-start | bytes 786432 | tf_op jit(solution)/shard_map/all_to_all | solution.py:1141
  214.5 1.5 collective-permute-done.23
  218.3 7.4 %all-to-all-done.5 = bf16[32,24,256]{2,1,0:T(8,128)(2,1)S(1)} async-done(((bf16[32,24,256]{2,1,0:T(8,128)(2,1)}), bf16[32,24,256]{2,1,0:T(8,128)(2,1)S(1)}, u32[]{:S(2)}, u32[]{:S(2)}) %all-to-all-start.5) | async-done | bytes 393248 | tf_op jit(solution)/shard_map/all_to_all | solution.py:1141
  (138 shorter events, 31.4 us)
Async XLA Ops:
  0.6 22.6 %copy-start = (s32[768]{0:T(1024)S(1)}, s32[768]{0:T(1024)}, u32[]{:S(2)}) copy-start(s32[768]{0:T(1024)} %param.23) | copy-start | bytes 9220
  7.3 22.1 %all-to-all-start = ((bf16[8,96,768]{2,1,0:T(8,128)(2,1)}), bf16[8,96,768]{2,1,0:T(8,128)(2,1)}, u32[]{:S(2)}, u32[]{:S(2)}) async-start(bf16[8,96,768]{2,1,0:T(8,128)(2,1)} %bitcast.91), calls=%async_computation | async-start | bytes 2359296 | tf_op jit(solution)/shard_map/all_to_all | solution.py:1181
  12.5 13.0 %collective-permute-start.1 = (bf16[512,768]{1,0:T(8,128)(2,1)}, bf16[512,768]{1,0:T(8,128)(2,1)}, u32[]{:S(2)}, u32[]{:S(2)}) collective-permute-start(bf16[512,768]{1,0:T(8,128)(2,1)} %get-tuple-element.68.refs_11_), channel_id=1, source_target_pairs={{0,1},{1,0},{2,3},{3,2},{4,5},{5,4},{6,7},{7,6},{8,9},{9,8},{10,11... | collective-permute-start | bytes 2359304 | tf_op jit(solution)/shard_map/ppermute | solution.py:1036
  19.9 4.1 %copy-start.20 = (f32[96]{0:T(128)S(1)}, f32[96]{0:T(128)}, u32[]{:S(2)}) copy-start(f32[96]{0:T(128)} %param.29) | copy-start | bytes 1156
  19.9 5.6 %collective-permute-start = (bf16[384,512]{1,0:T(8,128)(2,1)}, bf16[384,512]{1,0:T(8,128)(2,1)S(1)}, u32[]{:S(2)}, u32[]{:S(2)}) collective-permute-start(bf16[384,512]{1,0:T(8,128)(2,1)} %get-tuple-element.67), channel_id=1, source_target_pairs={{0,1},{1,0},{2,3},{3,2},{4,5},{5,4},{6,7},{7,6},{8,9},{9,8},{10,11... | collective-permute-start | bytes 1179656 | tf_op jit(solution)/shard_map/ppermute | solution.py:1036
  25.5 3.9 %copy-start.22 = (bf16[384,512]{1,0:T(8,128)(2,1)}, bf16[384,512]{1,0:T(8,128)(2,1)S(1)}, u32[]{:S(2)}) copy-start(bf16[384,512]{1,0:T(8,128)(2,1)S(1)} %collective-permute-done.refs_9_) | copy-start | bytes 1179652
  36.3 4.0 %copy-start.15 = (f32[768]{0:T(1024)S(1)}, f32[768]{0:T(1024)}, u32[]{:S(2)}) copy-start(f32[768]{0:T(1024)} %refs_2_.1) | copy-start | bytes 9220
  36.3 4.6 %copy-start.16 = (f32[768]{0:T(1024)S(1)}, f32[768]{0:T(1024)}, u32[]{:S(2)}) copy-start(f32[768]{0:T(1024)} %param.31) | copy-start | bytes 9220
  36.3 5.1 %copy-start.17 = (f32[768]{0:T(1024)S(1)}, f32[768]{0:T(1024)}, u32[]{:S(2)}) copy-start(f32[768]{0:T(1024)} %param.32) | copy-start | bytes 9220
  36.4 5.7 %copy-start.18 = (f32[768]{0:T(1024)S(1)}, f32[768]{0:T(1024)}, u32[]{:S(2)}) copy-start(f32[768]{0:T(1024)} %param.33) | copy-start | bytes 9220
  36.4 6.3 %copy-start.19 = (f32[768]{0:T(1024)S(1)}, f32[768]{0:T(1024)}, u32[]{:S(2)}) copy-start(f32[768]{0:T(1024)} %param.37) | copy-start | bytes 9220
  36.4 16.7 %all-to-all-start.1 = ((bf16[8,96,512]{2,1,0:T(8,128)(2,1)}), bf16[8,96,512]{2,1,0:T(8,128)(2,1)S(1)}, u32[]{:S(2)}, u32[]{:S(2)}) async-start(bf16[8,96,512]{2,1,0:T(8,128)(2,1)} %get-tuple-element.69), calls=%async_computation.1 | async-start | bytes 1572864 | tf_op jit(solution)/shard_map/all_to_all | solution.py:1187
  43.3 42.1 %collective-permute-start.3 = (bf16[512,768]{1,0:T(8,128)(2,1)}, bf16[512,768]{1,0:T(8,128)(2,1)}, u32[]{:S(2)}, u32[]{:S(2)}) collective-permute-start(bf16[512,768]{1,0:T(8,128)(2,1)} %get-tuple-element.78.refs_3_.refs_4_), channel_id=1, source_target_pairs={{0,2},{1,3},{2,0},{3,1},{4,6},{5,7},{6,4},{7,5},{8,10},{9,11},{10,... | collective-permute-start | bytes 2359304 | tf_op jit(solution)/shard_map/ppermute | solution.py:1036
  45.0 40.4 %collective-permute-start.4 = (bf16[512,768]{1,0:T(8,128)(2,1)}, bf16[512,768]{1,0:T(8,128)(2,1)}, u32[]{:S(2)}, u32[]{:S(2)}) collective-permute-start(bf16[512,768]{1,0:T(8,128)(2,1)} %get-tuple-element.78.refs_3_.refs_4_), channel_id=1, source_target_pairs={{0,4},{1,5},{2,6},{3,7},{4,0},{5,1},{6,2},{7,3},{8,12},{9,13},{10,... | collective-permute-start | bytes 2359304 | tf_op jit(solution)/shard_map/ppermute | solution.py:1036
  46.5 40.5 %collective-permute-start.5 = (bf16[512,768]{1,0:T(8,128)(2,1)}, bf16[512,768]{1,0:T(8,128)(2,1)}, u32[]{:S(2)}, u32[]{:S(2)}) collective-permute-start(bf16[512,768]{1,0:T(8,128)(2,1)} %get-tuple-element.78.refs_3_.refs_4_), channel_id=1, source_target_pairs={{0,6},{1,7},{2,4},{3,5},{4,2},{5,3},{6,0},{7,1},{8,14},{9,15},{10,... | collective-permute-start | bytes 2359304 | tf_op jit(solution)/shard_map/ppermute | solution.py:1036
  73.4 13.6 %collective-permute-start.2 = (bf16[512,6144]{1,0:T(8,128)(2,1)}, bf16[512,6144]{1,0:T(8,128)(2,1)}, u32[]{:S(2)}, u32[]{:S(2)}) collective-permute-start(bf16[512,6144]{1,0:T(8,128)(2,1)} %get-tuple-element.71.refs_0_.refs_1_.refs_2_), channel_id=1, source_target_pairs={{0,1},{1,0},{2,3},{3,2},{4,5},{5,4},{6,7},{7,6},{8,9},{9,8},{10,11... | collective-permute-start | bytes 18874376 | tf_op jit(solution)/shard_map/ppermute | solution.py:1036
  73.4 31.5 %all-to-all-start.2 = ((bf16[8,96,512]{2,1,0:T(8,128)(2,1)}), bf16[8,96,512]{2,1,0:T(8,128)(2,1)}, u32[]{:S(2)}, u32[]{:S(2)}) async-start(bf16[8,96,512]{2,1,0:T(8,128)(2,1)} %bitcast.93), calls=%async_computation.2 | async-start | bytes 1572864 | tf_op jit(solution)/shard_map/all_to_all | solution.py:1197
  77.7 37.8 %collective-permute-start.9 = (bf16[768,512]{1,0:T(8,128)(2,1)}, bf16[768,512]{1,0:T(8,128)(2,1)}, u32[]{:S(2)}, u32[]{:S(2)}) collective-permute-start(bf16[768,512]{1,0:T(8,128)(2,1)} %get-tuple-element.90), channel_id=1, source_target_pairs={{0,1},{1,0},{2,3},{3,2},{4,5},{5,4},{6,7},{7,6},{8,9},{9,8},{10,11... | collective-permute-start | bytes 2359304 | tf_op jit(solution)/shard_map/ppermute | solution.py:1036
  94.1 26.7 %collective-permute-start.6 = (bf16[512,768]{1,0:T(8,128)(2,1)}, bf16[512,768]{1,0:T(8,128)(2,1)}, u32[]{:S(2)}, u32[]{:S(2)}) collective-permute-start(bf16[512,768]{1,0:T(8,128)(2,1)} %get-tuple-element.86.refs_6_), channel_id=1, source_target_pairs={{0,1},{1,0},{2,3},{3,2},{4,5},{5,4},{6,7},{7,6},{8,9},{9,8},{10,11... | collective-permute-start | bytes 2359304 | tf_op jit(solution)/shard_map/ppermute | solution.py:1036
  94.1 28.4 %collective-permute-start.7 = (bf16[512,768]{1,0:T(8,128)(2,1)}, bf16[512,768]{1,0:T(8,128)(2,1)}, u32[]{:S(2)}, u32[]{:S(2)}) collective-permute-start(bf16[512,768]{1,0:T(8,128)(2,1)} %get-tuple-element.87.refs_8_), channel_id=1, source_target_pairs={{0,1},{1,0},{2,3},{3,2},{4,5},{5,4},{6,7},{7,6},{8,9},{9,8},{10,11... | collective-permute-start | bytes 2359304 | tf_op jit(solution)/shard_map/ppermute | solution.py:1036
  94.6 37.1 %collective-permute-start.10 = (bf16[2,4,96,768]{3,2,1,0:T(8,128)(2,1)}, bf16[2,4,96,768]{3,2,1,0:T(8,128)(2,1)}, u32[]{:S(2)}, u32[]{:S(2)}) collective-permute-start(bf16[2,4,96,768]{3,2,1,0:T(8,128)(2,1)} %get-tuple-element.79.refs_6_), channel_id=1, source_target_pairs={{0,8},{8,0},{16,24},{24,16},{1,9},{9,1},{17,25},{25,17},{2,10},{10... | collective-permute-start | bytes 3538952 | tf_op jit(solution)/shard_map/ppermute | solution.py:1041
  104.4 47.7 %collective-permute-start.12 = (bf16[2,768,384]{2,1,0:T(8,128)(2,1)}, bf16[2,768,384]{2,1,0:T(8,128)(2,1)}, u32[]{:S(2)}, u32[]{:S(2)}) collective-permute-start(bf16[2,768,384]{2,1,0:T(8,128)(2,1)} %get-tuple-element.80.refs_5_), channel_id=1, source_target_pairs={{0,4},{1,5},{2,6},{3,7},{4,0},{5,1},{6,2},{7,3},{8,12},{9,13},{10,... | collective-permute-start | bytes 3538952 | tf_op jit(solution)/shard_map/ppermute | solution.py:1041
  111.0 57.5 %all-to-all-start.3 = ((bf16[8,96,512]{2,1,0:T(8,128)(2,1)}), bf16[8,96,512]{2,1,0:T(8,128)(2,1)}, u32[]{:S(2)}, u32[]{:S(2)}) async-start(bf16[8,96,512]{2,1,0:T(8,128)(2,1)} %conv_adjoint.1.refs_8_.refs_3_), calls=%async_computation.3 | async-start | bytes 1572864 | tf_op jit(solution)/shard_map/all_to_all | solution.py:1221
  115.4 7.1 %collective-permute-start.8 = (bf16[512,768]{1,0:T(8,128)(2,1)}, bf16[512,768]{1,0:T(8,128)(2,1)S(1)}, u32[]{:S(2)}, u32[]{:S(2)}) collective-permute-start(bf16[512,768]{1,0:T(8,128)(2,1)} %get-tuple-element.88.refs_10_), channel_id=1, source_target_pairs={{0,1},{1,0},{2,3},{3,2},{4,5},{5,4},{6,7},{7,6},{8,9},{9,8},{10,11... | collective-permute-start | bytes 2359304 | tf_op jit(solution)/shard_map/ppermute | solution.py:1036
  120.7 18.8 %collective-permute-start.11 = (bf16[2,192,768]{2,1,0:T(8,128)(2,1)}, bf16[2,192,768]{2,1,0:T(8,128)(2,1)}, u32[]{:S(2)}, u32[]{:S(2)}) collective-permute-start(bf16[2,192,768]{2,1,0:T(8,128)(2,1)} %get-tuple-element.91.refs_12_), channel_id=1, source_target_pairs={{0,2},{1,3},{2,0},{3,1},{4,6},{5,7},{6,4},{7,5},{8,10},{9,11},{10,... | collective-permute-start | bytes 1769480 | tf_op jit(solution)/shard_map/ppermute | solution.py:1041
  134.6 29.1 %collective-permute-start.14 = (bf16[1,4,96,768]{3,2,1,0:T(8,128)(2,1)}, bf16[1,4,96,768]{3,2,1,0:T(8,128)(2,1)}, u32[]{:S(2)}, u32[]{:S(2)}) collective-permute-start(bf16[1,4,96,768]{3,2,1,0:T(8,128)(2,1)} %get-tuple-element.119.after_ref), channel_id=1, source_target_pairs={{0,16},{8,24},{16,0},{24,8},{1,17},{9,25},{17,1},{25,9},{2,18},{10... | collective-permute-start | bytes 1769480 | tf_op jit(solution)/shard_map/ppermute | solution.py:1041
  141.7 13.9 %collective-permute-start.13 = (bf16[1,192,768]{2,1,0:T(8,128)(2,1)}, bf16[1,192,768]{2,1,0:T(8,128)(2,1)}, u32[]{:S(2)}, u32[]{:S(2)}) collective-permute-start(bf16[1,192,768]{2,1,0:T(8,128)(2,1)} %get-tuple-element.123.refs_6_), channel_id=1, source_target_pairs={{0,4},{1,5},{2,6},{3,7},{4,0},{5,1},{6,2},{7,3},{8,12},{9,13},{10,... | collective-permute-start | bytes 884744 | tf_op jit(solution)/shard_map/ppermute | solution.py:1041
  152.1 33.4 %collective-permute-start.19 = (bf16[2,192,256]{2,1,0:T(8,128)(2,1)}, bf16[2,192,256]{2,1,0:T(8,128)(2,1)}, u32[]{:S(2)}, u32[]{:S(2)}) collective-permute-start(bf16[2,192,256]{2,1,0:T(8,128)(2,1)} %get-tuple-element.132.after_ref), channel_id=1, source_target_pairs={{0,8},{8,0},{16,24},{24,16},{1,9},{9,1},{17,25},{25,17},{2,10},{10... | collective-permute-start | bytes 589832 | tf_op jit(solution)/shard_map/ppermute | solution.py:1041
  155.1 20.8 %collective-permute-start.15 = (bf16[1,768,384]{2,1,0:T(8,128)(2,1)}, bf16[1,768,384]{2,1,0:T(8,128)(2,1)}, u32[]{:S(2)}, u32[]{:S(2)}) collective-permute-start(bf16[1,768,384]{2,1,0:T(8,128)(2,1)} %get-tuple-element.117.after_ref), channel_id=1, source_target_pairs={{0,2},{1,3},{2,0},{3,1},{4,6},{5,7},{6,4},{7,5},{8,10},{9,11},{10,... | collective-permute-start | bytes 1769480 | tf_op jit(solution)/shard_map/ppermute | solution.py:1041
  155.6 1.9 copy-start.14
  158.3 30.9 %collective-permute-start.16 = (bf16[96,768]{1,0:T(8,128)(2,1)}, bf16[96,768]{1,0:T(8,128)(2,1)}, u32[]{:S(2)}, u32[]{:S(2)}) collective-permute-start(bf16[96,768]{1,0:T(8,128)(2,1)} %get-tuple-element.130.after_ref.refs_8_), channel_id=1, source_target_pairs={{0,0},{3,1},{6,2},{1,3},{4,4},{7,5},{2,6},{5,7},{8,8},{11,9},{14,1... | collective-permute-start | bytes 442376 | tf_op jit(solution)/shard_map/ppermute | solution.py:1248
  161.1 30.4 %collective-permute-start.17 = (bf16[96,768]{1,0:T(8,128)(2,1)}, bf16[96,768]{1,0:T(8,128)(2,1)}, u32[]{:S(2)}, u32[]{:S(2)}) collective-permute-start(bf16[96,768]{1,0:T(8,128)(2,1)} %get-tuple-element.129.refs_9_), channel_id=1, source_target_pairs={{1,0},{4,1},{7,2},{2,3},{5,4},{0,5},{3,6},{6,7},{9,8},{12,9},{15,1... | collective-permute-start | bytes 442376 | tf_op jit(solution)/shard_map/ppermute | solution.py:1248
  163.7 27.9 %collective-permute-start.18 = (bf16[96,768]{1,0:T(8,128)(2,1)}, bf16[96,768]{1,0:T(8,128)(2,1)}, u32[]{:S(2)}, u32[]{:S(2)}) collective-permute-start(bf16[96,768]{1,0:T(8,128)(2,1)} %get-tuple-element.128.refs_10_), channel_id=1, source_target_pairs={{2,0},{5,1},{0,2},{3,3},{6,4},{1,5},{4,6},{7,7},{10,8},{13,9},{8,1... | collective-permute-start | bytes 442376 | tf_op jit(solution)/shard_map/ppermute | solution.py:1248
  177.3 8.3 %copy-start.13 = (bf16[2,96,768]{2,1,0:T(8,128)(2,1)S(1)}, bf16[2,96,768]{2,1,0:T(8,128)(2,1)}, u32[]{:S(2)}) copy-start(bf16[2,96,768]{2,1,0:T(8,128)(2,1)} %get-tuple-element.121.refs_11_) | copy-start | bytes 884740
  178.1 20.7 %collective-permute-start.20 = (bf16[2,192,384]{2,1,0:T(8,128)(2,1)S(1)}, bf16[2,192,384]{2,1,0:T(8,128)(2,1)S(1)}, u32[]{:S(2)}, u32[]{:S(2)}) collective-permute-start(bf16[2,192,384]{2,1,0:T(8,128)(2,1)S(1)} %get-tuple-element.127.refs_5_), channel_id=1, source_target_pairs={{0,8},{8,0},{16,24},{24,16},{1,9},{9,1},{17,25},{25,17},{2,10},{10... | collective-permute-start | bytes 884744 | tf_op jit(solution)/shard_map/ppermute | solution.py:1041
  180.6 17.4 %all-to-all-start.4 = ((f32[32,16,96]{2,1,0:T(8,128)}), f32[32,16,96]{2,1,0:T(8,128)S(1)}, u32[]{:S(2)}, u32[]{:S(2)}) async-start(f32[32,16,96]{2,1,0:T(8,128)} %bitcast.97), calls=%async_computation.4 | async-start | bytes 524288 | tf_op jit(solution)/shard_map/all_to_all | solution.py:1141
  185.6 14.9 %collective-permute-start.21 = (bf16[2,96,768]{2,1,0:T(8,128)(2,1)S(1)}, bf16[2,96,768]{2,1,0:T(8,128)(2,1)S(1)}, u32[]{:S(2)}, u32[]{:S(2)}) collective-permute-start(bf16[2,96,768]{2,1,0:T(8,128)(2,1)S(1)} %copy-done.13), channel_id=1, source_target_pairs={{0,2},{1,3},{2,0},{3,1},{4,6},{5,7},{6,4},{7,5},{8,10},{9,11},{10,... | collective-permute-start | bytes 884744 | tf_op jit(solution)/shard_map/ppermute | solution.py:1041
  189.2 17.6 %collective-permute-start.24 = (bf16[1,192,256]{2,1,0:T(8,128)(2,1)}, bf16[1,192,256]{2,1,0:T(8,128)(2,1)S(1)}, u32[]{:S(2)}, u32[]{:S(2)}) collective-permute-start(bf16[1,192,256]{2,1,0:T(8,128)(2,1)} %get-tuple-element.136.after_ref), channel_id=1, source_target_pairs={{0,16},{8,24},{16,0},{24,8},{1,17},{9,25},{17,1},{25,9},{2,18},{10... | collective-permute-start | bytes 294920 | tf_op jit(solution)/shard_map/ppermute | solution.py:1041
  193.8 1.5 copy-start.5
  193.8 11.1 %collective-permute-start.22 = (bf16[2,192,384]{2,1,0:T(8,128)(2,1)S(1)}, bf16[2,192,384]{2,1,0:T(8,128)(2,1)S(1)}, u32[]{:S(2)}, u32[]{:S(2)}) collective-permute-start(bf16[2,192,384]{2,1,0:T(8,128)(2,1)S(1)} %get-tuple-element.125.after_ref), channel_id=1, source_target_pairs={{0,8},{8,0},{16,24},{24,16},{1,9},{9,1},{17,25},{25,17},{2,10},{10... | collective-permute-start | bytes 884744 | tf_op jit(solution)/shard_map/ppermute | solution.py:1041
  199.8 17.0 %collective-permute-start.25 = (bf16[1,192,384]{2,1,0:T(8,128)(2,1)S(1)}, bf16[1,192,384]{2,1,0:T(8,128)(2,1)S(1)}, u32[]{:S(2)}, u32[]{:S(2)}) collective-permute-start(bf16[1,192,384]{2,1,0:T(8,128)(2,1)S(1)} %constant_dynamic-slice_fusion.2.after_ref), channel_id=1, source_target_pairs={{0,16},{8,24},{16,0},{24,8},{1,17},{9,25},{17,1},{25,9},{2,18},{10... | collective-permute-start | bytes 442376 | tf_op jit(solution)/shard_map/ppermute | solution.py:1041
  201.5 16.1 %collective-permute-start.26 = (bf16[1,96,768]{2,1,0:T(8,128)(2,1)S(1)}, bf16[1,96,768]{2,1,0:T(8,128)(2,1)S(1)}, u32[]{:S(2)}, u32[]{:S(2)}) collective-permute-start(bf16[1,96,768]{2,1,0:T(8,128)(2,1)S(1)} %add_convert_fusion.14.after_ref), channel_id=1, source_target_pairs={{0,4},{1,5},{2,6},{3,7},{4,0},{5,1},{6,2},{7,3},{8,12},{9,13},{10,... | collective-permute-start | bytes 442376 | tf_op jit(solution)/shard_map/ppermute | solution.py:1041
  206.0 6.5 %copy-start.4 = (f32[32,16,96]{2,1,0:T(8,128)S(1)}, f32[32,16,96]{2,1,0:T(8,128)}, u32[]{:S(2)}) copy-start(f32[32,16,96]{2,1,0:T(8,128)} %copy-done.3) | copy-start | bytes 589828
  206.1 9.9 %collective-permute-start.23 = (bf16[1,192,384]{2,1,0:T(8,128)(2,1)S(1)}, bf16[1,192,384]{2,1,0:T(8,128)(2,1)S(1)}, u32[]{:S(2)}, u32[]{:S(2)}) collective-permute-start(bf16[1,192,384]{2,1,0:T(8,128)(2,1)S(1)} %constant_dynamic-slice_fusion.1.after_ref), channel_id=1, source_target_pairs={{0,16},{8,24},{16,0},{24,8},{1,17},{9,25},{17,1},{25,9},{2,18},{10... | collective-permute-start | bytes 442376 | tf_op jit(solution)/shard_map/ppermute | solution.py:1041
  208.4 9.1 %copy-start.2 = (bf16[2,96,768]{2,1,0:T(8,128)(2,1)S(1)}, bf16[2,96,768]{2,1,0:T(8,128)(2,1)}, u32[]{:S(2)}) copy-start(bf16[2,96,768]{2,1,0:T(8,128)(2,1)} %gate.17) | copy-start | bytes 884740
  208.4 17.3 %all-to-all-start.5 = ((bf16[32,24,256]{2,1,0:T(8,128)(2,1)}), bf16[32,24,256]{2,1,0:T(8,128)(2,1)S(1)}, u32[]{:S(2)}, u32[]{:S(2)}) async-start(bf16[32,24,256]{2,1,0:T(8,128)(2,1)} %bitcast.36), calls=%async_computation.5 | async-start | bytes 786432 | tf_op jit(solution)/shard_map/all_to_all | solution.py:1141
  216.0 9.8 %copy-start.12 = (f32[192,384]{1,0:T(8,128)}, f32[192,384]{1,0:T(8,128)S(1)}, u32[]{:S(2)}) copy-start(f32[192,384]{1,0:T(8,128)S(1)} %add_bitcast_fusion.2) | copy-start | bytes 884740
  218.3 7.6 %copy-start.8 = (f32[768,256]{1,0:T(8,128)S(1)}, f32[768,256]{1,0:T(8,128)}, u32[]{:S(2)}) copy-start(f32[768,256]{1,0:T(8,128)} %refs_8_.1) | copy-start | bytes 2359300
  (8 other events, 6.9 us)

commit v2 on v1

--- a/solution.py
+++ b/solution.py
@@ -94,8 +94,7 @@
 
 
 def signal_of(spec, ghi):
-    high, low = split_value(spec)
-    return mm(high, ghi) + mm(low, ghi)
+    return mm(spec.astype(BF16), ghi)
 
 
 def each(count, step, unroll):
@@ -452,7 +451,7 @@
 def front_call(tok, offsets, gain, bias, weight, in_bias, taps, batch, tok_rows):
     rows, width = tok.shape
     span = rows + taps.shape[1]
-    cut = 256
+    cut = 384
     per = width // cut
 
     def full(i):

time: 228 us -> 227 us (level)
  no operation moved by 1% of the time
where the time goes in v2:
time: 227 us; the launch traced here: 226 us
  Pallas kernels  96.2 us (42%)
  starting transfers between devices  53.8 us (24%)
  waiting for transfers between devices  31.2 us (14%)
  other arithmetic  22.4 us (10%)
  local copies, waits for them, and re-layouts  21 us (9%)
    pallas_call x13, Pallas kernels, launch(): pl.pallas_call(run, grid=grid, out_shape=tuple(outs) + tuple((shape(v.sha...  96.2 us
    ppermute x14, starting transfers between devices, begin(): lax.ppermute(send, axis, [(i, i ^ bit) for i in range(count)])  16.6 us
    all_to_all x2, waiting for transfers between devices, to_all(): lax.all_to_all(wide, ('dp', 'freq'), split_axis=0, concat_axis=0, tiled=T...  10.1 us
    ppermute x14, waiting for transfers between devices, begin(): lax.ppermute(send, axis, [(i, i ^ bit) for i in range(count)])  9.26 us
    all_to_all x2, starting transfers between devices, to_all(): lax.all_to_all(wide, ('dp', 'freq'), split_axis=0, concat_axis=0, tiled=T...  9.07 us
    convert_element_type x3, other arithmetic, step_on(): keep = finish([v[:half] for v in pending]).astype(BF16)  7.98 us
    all_to_all x1, waiting for transfers between devices, body(): lax.all_to_all(conv, 'freq', split_axis=0, concat_axis=0, tiled=True)  6.37 us
    ppermute x10, starting transfers between devices, flip(): lax.ppermute(value, 'freq', [(i, i ^ bit) for i in range(freq_parts)])  5.25 us
  transfers between devices with their start and end apart: 33, of which 9 were waited for; matrix products, arithmetic and copies ran while one was open for 17% of the time, Pallas kernels for 37%

profile of v2, /device:TPU:0, one launch (start us, length us, event | category | flops | bytes accessed | tf_op | source)
XLA Modules:
  0.0 225.7 jit_solution(4862566536444712054)
XLA Ops:
  0.7 6.5 %norm_project.1 = (bf16[512,768]{1,0:T(8,128)(2,1)}, bf16[768,768]{1,0:T(8,128)(2,1)}, bf16[512,768]{1,0:T(8,128)(2,1)}, bf16[512,768]{1,0:T(8,128)(2,1)}, bf16[512,768]{1,0:T(8,128)(2,1)}) custom-call(s32[2]{0:T(128)} %refs_0_.3, bf16[512,768]{1,0:T(8,128)(2,1)} %bitcast.102, f32[768]{0:T(1024)} %refs_2_.1, f32[768]{0:T(1024)} %refs_3_.5, ...), custom_call_target="tpu_custom_call" | custom-call | flops 115964116992 | bytes 528482304 | tf_op jit(solution)/shard_map/norm_project/pallas_call | solution.py:51
  7.2 5.2 %all-to-all-start = ((bf16[8,96,768]{2,1,0:T(8,128)(2,1)}), bf16[8,96,768]{2,1,0:T(8,128)(2,1)}, u32[]{:S(2)}, u32[]{:S(2)}) async-start(bf16[8,96,768]{2,1,0:T(8,128)(2,1)} %bitcast.91), calls=%async_computation | async-start | bytes 2359296 | tf_op jit(solution)/shard_map/all_to_all | solution.py:1180
  12.9 6.9 %active_grad.1 = (bf16[512,3072]{1,0:T(8,128)(2,1)}, f32[1,768]{1,0:T(1,128)}, bf16[384,512]{1,0:T(8,128)(2,1)}, bf16[384,512]{1,0:T(8,128)(2,1)}) custom-call(bf16[512,768]{1,0:T(8,128)(2,1)} %bitcast.100, bf16[3072,768]{1,0:T(8,128)(2,1)} %refs_1_.3, bf16[768,768]{1,0:T(8,128)(2,1)} %get-tuple-element.65.refs_2_), custom_call_target="tpu_custom_call" | custom-call | flops 154618822656 | bytes 503316480 | tf_op jit(solution)/shard_map/active_grad/pallas_call | solution.py:51
  19.8 1.3 constant_dynamic-slice_fusion.5
  25.4 3.9 %all-to-all-done.refs_0_ = bf16[8,96,768]{2,1,0:T(8,128)(2,1)} async-done(((bf16[8,96,768]{2,1,0:T(8,128)(2,1)}), bf16[8,96,768]{2,1,0:T(8,128)(2,1)}, u32[]{:S(2)}, u32[]{:S(2)}) %all-to-all-start) | async-done | bytes 1179680 | tf_op jit(solution)/shard_map/all_to_all | solution.py:1180
  29.3 6.5 %conv_forward.1 = (bf16[8,96,512]{2,1,0:T(8,128)(2,1)}, f32[8,96,512]{2,1,0:T(8,128)}, bf16[384,512]{1,0:T(8,128)(2,1)}, bf16[512,768]{1,0:T(8,128)(2,1)}, bf16[512,768]{1,0:T(8,128)(2,1)}) custom-call(bf16[8,96,768]{2,1,0:T(8,128)(2,1)} %all-to-all-done.refs_0_, ...), custom_call_target="tpu_custom_call", output_to_operand_aliasing={{2}: (9, {}), {3}: (10, {}), {4}: (11, {})} | custom-call | flops 193273528320 | bytes 369098752 | tf_op jit(solution)/shard_map/conv_forward/pallas_call | solution.py:51
  35.8 3.9 %all-to-all-start.1 = ((bf16[8,96,512]{2,1,0:T(8,128)(2,1)}), bf16[8,96,512]{2,1,0:T(8,128)(2,1)S(1)}, u32[]{:S(2)}, u32[]{:S(2)}) async-start(bf16[8,96,512]{2,1,0:T(8,128)(2,1)} %get-tuple-element.69), calls=%async_computation.1 | async-start | bytes 1572864 | tf_op jit(solution)/shard_map/all_to_all | solution.py:1186
  42.7 1.7 collective-permute-start.3
  44.4 1.5 collective-permute-start.4
  46.2 6.4 %all-to-all-done.1 = bf16[8,96,512]{2,1,0:T(8,128)(2,1)S(1)} async-done(((bf16[8,96,512]{2,1,0:T(8,128)(2,1)}), bf16[8,96,512]{2,1,0:T(8,128)(2,1)S(1)}, u32[]{:S(2)}, u32[]{:S(2)}) %all-to-all-start.1) | async-done | bytes 786464 | tf_op jit(solution)/shard_map/all_to_all | solution.py:1186
  53.5 19.4 %mix_out_mlp.1 = (bf16[512,6144]{1,0:T(8,128)(2,1)}, bf16[512,768]{1,0:T(8,128)(2,1)}, f32[1,3072]{1,0:T(1,128)}, bf16[512,768]{1,0:T(8,128)(2,1)}, bf16[768,512...) custom-call(bf16[512,768]{1,0:T(8,128)(2,1)} %bitcast.103, ...), custom_call_target="tpu_custom_call" | custom-call | flops 347892350976 | bytes 1358954496 | tf_op jit(solution)/shard_map/mix_out_mlp/pallas_call | solution.py:51
  72.9 4.2 %all-to-all-start.2 = ((bf16[8,96,512]{2,1,0:T(8,128)(2,1)}), bf16[8,96,512]{2,1,0:T(8,128)(2,1)}, u32[]{:S(2)}, u32[]{:S(2)}) async-start(bf16[8,96,512]{2,1,0:T(8,128)(2,1)} %bitcast.93), calls=%async_computation.2 | async-start | bytes 1572864 | tf_op jit(solution)/shard_map/all_to_all | solution.py:1196
  77.6 7.2 %block_out.1.refs_4_ = bf16[512,768]{1,0:T(8,128)(2,1)} custom-call(bf16[512,6144]{1,0:T(8,128)(2,1)} %get-tuple-element.71.refs_0_.refs_1_.refs_2_, bf16[3072,768]{1,0:T(8,128)(2,1)} %refs_1_.3, bf16[512,768]{1,0:T(8,128)(2,1)} %get-tuple-element.72.refs_2_, f32[1,768]{1,0:T(1,128)} %reshape.154.refs_3_), custom_call_target="tpu_custom_call" | custom-call | flops 154618822656 | bytes 704643072 | tf_op jit(solution)/shard_map/block_out/pallas_call | solution.py:51
  84.8 1.6 collective-permute-done.5.refs_7_
  86.4 7.1 %fc2_gradient.1 = (bf16[2,4,96,768]{3,2,1,0:T(8,128)(2,1)}, bf16[2,4,96,768]{3,2,1,0:T(8,128)(2,1)}, bf16[512,768]{1,0:T(8,128)(2,1)}, bf16[512,768]{1,0:T(8,128)(2,1)}, bf16[512,768]{1,0:T(8,128)(2,1)}) custom-call(bf16[384,512]{1,0:T(8,128)(2,1)} %get-tuple-element.76.refs_0_, ...), custom_call_target="tpu_custom_call", output_to_operand_aliasing={{2}: (5, {}), {3}: (6, {}), {4}: (7, {})} | custom-call | flops 154618822656 | bytes 402653184 | tf_op jit(solution)/shard_map/fc2_gradient/pallas_call | solution.py:51
  94.0 2.0 collective-permute-start.10
  96.0 7.8 %fc1_gradient.1 = (bf16[2,768,384]{2,1,0:T(8,128)(2,1)}, bf16[2,768,384]{2,1,0:T(8,128)(2,1)}) custom-call(bf16[512,6144]{1,0:T(8,128)(2,1)} %get-tuple-element.71.refs_0_.refs_1_.refs_2_, bf16[512,6144]{1,0:T(8,128)(2,1)} %get-tuple-element.71.refs_0_.refs_1_.refs_2_, bf16[512,1536]{1,0:T(8,128)(2,1)} %get-tuple-element.75.refs_2_, ...), custom_call_target="tpu_custom_call" | custom-call | flops 154618822656 | bytes 503316480 | tf_op jit(solution)/shard_map/fc1_gradient/pallas_call | solution.py:51
  104.4 5.6 %conv_adjoint.1.refs_8_.refs_3_ = bf16[8,96,512]{2,1,0:T(8,128)(2,1)} custom-call(bf16[8,96,512]{2,1,0:T(8,128)(2,1)} %all-to-all-done.2.refs_0_.refs_1_, f32[8,96,512]{2,1,0:T(8,128)} %get-tuple-element.74.refs_1_, f32[96,1]{1,0:T(8,128)} %copy.91.refs_2_, bf16[256,512]{1,0:T(8,128)(2,1)} %constant.125.clone.refs_3_, ...), custom_call_target="tpu_custom_call" | custom-call | flops 128849018880 | bytes 268435456 | tf_op jit(solution)/shard_map/conv_adjoint/pallas_call | solution.py:51
  110.0 4.4 %all-to-all-start.3 = ((bf16[8,96,512]{2,1,0:T(8,128)(2,1)}), bf16[8,96,512]{2,1,0:T(8,128)(2,1)}, u32[]{:S(2)}, u32[]{:S(2)}) async-start(bf16[8,96,512]{2,1,0:T(8,128)(2,1)} %conv_adjoint.1.refs_8_.refs_3_), calls=%async_computation.3 | async-start | bytes 1572864 | tf_op jit(solution)/shard_map/all_to_all | solution.py:1220
  114.6 5.1 %mixer_gradient.1 = (bf16[2,192,768]{2,1,0:T(8,128)(2,1)}, bf16[2,192,768]{2,1,0:T(8,128)(2,1)}) custom-call(bf16[768,512]{1,0:T(8,128)(2,1)} %get-tuple-element.89.refs_0_, bf16[512,6144]{1,0:T(8,128)(2,1)} %get-tuple-element.71.refs_0_.refs_1_.refs_2_, bf16[512,6144]{1,0:T(8,128)(2,1)} %get-tuple-element.71.refs_0_.refs_1_.refs_2_, ...), custom_call_target="tpu_custom_call" | custom-call | flops 77309411328 | bytes 402653184 | tf_op jit(solution)/shard_map/mixer_gradient/pallas_call | solution.py:51
  119.8 1.7 collective-permute-start.11
  122.4 8.3 %owner_gradients.1 = (bf16[192,768]{1,0:T(8,128)(2,1)}, bf16[2,4,96,768]{3,2,1,0:T(8,128)(2,1)}, bf16[2,192,768]{2,1,0:T(8,128)(2,1)}) custom-call(s32[2]{0:T(128)} %refs_0_.3, bf16[192,768]{1,0:T(8,128)(2,1)} %maximum_bitcast_fusion.1.refs_7_.refs_1_, f32[192,1]{1,0:T(8,128)} %copy.92.refs_8_.refs_2_, ...), custom_call_target="tpu_custom_call", output_to_operand_aliasing={{1}: (13, {}), {2}: (14, {})} | custom-call | flops 154618822656 | bytes 402653184 | tf_op jit(solution)/shard_map/owner_gradients/pallas_call | solution.py:51
  130.7 2.9 %add_convert_fusion.3 = (bf16[1,4,96,768]{3,2,1,0:T(8,128)(2,1)}, bf16[1,4,96,768]{3,2,1,0:T(8,128)(2,1)}) fusion(bf16[2,4,96,768]{3,2,1,0:T(8,128)(2,1)} %collective-permute-done.10, bf16[2,4,96,768]{3,2,1,0:T(8,128)(2,1)} %get-tuple-element.95), kind=kLoop, calls=%fused_computation.3 | loop fusion | flops 2359296 | bytes 3538944 | tf_op jit(solution)/shard_map/convert_element_type | solution.py:1052
  133.6 2.6 %collective-permute-start.14 = (bf16[1,4,96,768]{3,2,1,0:T(8,128)(2,1)}, bf16[1,4,96,768]{3,2,1,0:T(8,128)(2,1)}, u32[]{:S(2)}, u32[]{:S(2)}) collective-permute-start(bf16[1,4,96,768]{3,2,1,0:T(8,128)(2,1)} %get-tuple-element.119.after_ref), channel_id=1, source_target_pairs={{0,16},{8,24},{16,0},{24,8},{1,17},{9,25},{17,1},{25,9},{2,18},{10... | collective-permute-start | bytes 1769480 | tf_op jit(solution)/shard_map/ppermute | solution.py:1040
  136.2 2.4 %collective-permute-done.11 = bf16[2,192,768]{2,1,0:T(8,128)(2,1)} collective-permute-done((bf16[2,192,768]{2,1,0:T(8,128)(2,1)}, bf16[2,192,768]{2,1,0:T(8,128)(2,1)}, u32[]{:S(2)}, u32[]{:S(2)}) %collective-permute-start.11) | collective-permute-done | bytes 589856 | tf_op jit(solution)/shard_map/ppermute | solution.py:1040
  138.6 2.2 add_convert_fusion.10
  140.8 1.5 collective-permute-start.13
  142.3 6.5 %taps_gradient.1 = (bf16[4,8,24,256]{3,2,1,0:T(8,128)(2,1)}, f32[96,1]{1,0:T(8,128)}, bf16[1,4,96,768]{3,2,1,0:T(8,128)(2,1)}, bf16[2,768,384]{2,1,0:T(8,128)(2,1)}, bf16[1,192,768]{2,1,0:T(8,128)(2,1)}) custom-call(bf16[8,96,768]{2,1,0:T(8,128)(2,1)} %all-to-all-done.refs_0_, ...), custom_call_target="tpu_custom_call", output_to_operand_aliasing={{2}: (7, {}), {3}: (8, {}), {4}: (9, {})} | custom-call | flops 193273528320 | bytes 226492416 | tf_op jit(solution)/shard_map/taps_gradient/pallas_call | solution.py:51
  148.8 1.8 dynamic-slice_bitcast_fusion.4
  150.6 2.9 %add_convert_fusion.1 = (bf16[1,768,384]{2,1,0:T(8,128)(2,1)}, bf16[1,768,384]{2,1,0:T(8,128)(2,1)}) fusion(bf16[2,768,384]{2,1,0:T(8,128)(2,1)} %collective-permute-done.12, bf16[2,768,384]{2,1,0:T(8,128)(2,1)} %gate.11), kind=kLoop, calls=%fused_computation.1 | loop fusion | flops 2359296 | bytes 3538944 | tf_op jit(solution)/shard_map/convert_element_type | solution.py:1052
  154.1 1.2 add_convert_fusion.9
  156.7 2.8 %collective-permute-start.16 = (bf16[96,768]{1,0:T(8,128)(2,1)}, bf16[96,768]{1,0:T(8,128)(2,1)}, u32[]{:S(2)}, u32[]{:S(2)}) collective-permute-start(bf16[96,768]{1,0:T(8,128)(2,1)} %get-tuple-element.130.after_ref.refs_8_), channel_id=1, source_target_pairs={{0,0},{3,1},{6,2},{1,3},{4,4},{7,5},{2,6},{5,7},{8,8},{11,9},{14,1... | collective-permute-start | bytes 442376 | tf_op jit(solution)/shard_map/ppermute | solution.py:1247
  159.5 3.2 %collective-permute-done.14 = bf16[1,4,96,768]{3,2,1,0:T(8,128)(2,1)} collective-permute-done((bf16[1,4,96,768]{3,2,1,0:T(8,128)(2,1)}, bf16[1,4,96,768]{3,2,1,0:T(8,128)(2,1)}, u32[]{:S(2)}, u32[]{:S(2)}) %collective-permute-start.14) | collective-permute-done | bytes 589856 | tf_op jit(solution)/shard_map/ppermute | solution.py:1040
  162.7 2.3 %collective-permute-start.18 = (bf16[96,768]{1,0:T(8,128)(2,1)}, bf16[96,768]{1,0:T(8,128)(2,1)}, u32[]{:S(2)}, u32[]{:S(2)}) collective-permute-start(bf16[96,768]{1,0:T(8,128)(2,1)} %get-tuple-element.128.refs_10_), channel_id=1, source_target_pairs={{2,0},{5,1},{0,2},{3,3},{6,4},{1,5},{4,6},{7,7},{10,8},{13,9},{8,1... | collective-permute-start | bytes 442376 | tf_op jit(solution)/shard_map/ppermute | solution.py:1247
  165.1 2.2 fusion.1
  167.2 7.4 %project_back.1 = (bf16[512,768]{1,0:T(8,128)(2,1)}, f32[8,768]{1,0:T(8,128)}, bf16[2,96,768]{2,1,0:T(8,128)(2,1)}, bf16[1,768,384]{2,1,0:T(8,128)(2,1)}, bf16[2,192,256]{2,1,0:T(8,128)(2,1)}) custom-call(bf16[768,512]{1,0:T(8,128)(2,1)} %bitcast.11.refs_0_, ...), custom_call_target="tpu_custom_call", output_to_operand_aliasing={{2}: (12, {}), {3}: (13, {}), {4}: (14, {})} | custom-call | flops 237494511599616 | bytes 1288490188800 | tf_op jit(solution)/shard_map/project_back/pallas_call | solution.py:51
  174.6 1.4 add_convert_fusion
  177.6 1.8 pack_vectors.1
  179.4 5.0 %all-to-all-start.4 = ((f32[32,16,96]{2,1,0:T(8,128)}), f32[32,16,96]{2,1,0:T(8,128)S(1)}, u32[]{:S(2)}, u32[]{:S(2)}) async-start(f32[32,16,96]{2,1,0:T(8,128)} %bitcast.97), calls=%async_computation.4 | async-start | bytes 524288 | tf_op jit(solution)/shard_map/all_to_all | solution.py:1140
  184.3 1.8 collective-permute-start.21
  187.9 2.4 %collective-permute-start.24 = (bf16[1,192,256]{2,1,0:T(8,128)(2,1)}, bf16[1,192,256]{2,1,0:T(8,128)(2,1)S(1)}, u32[]{:S(2)}, u32[]{:S(2)}) collective-permute-start(bf16[1,192,256]{2,1,0:T(8,128)(2,1)} %get-tuple-element.136.after_ref), channel_id=1, source_target_pairs={{0,16},{8,24},{16,0},{24,8},{1,17},{9,25},{17,1},{25,9},{2,18},{10... | collective-permute-start | bytes 294920 | tf_op jit(solution)/shard_map/ppermute | solution.py:1040
  192.6 1.5 collective-permute-start.22
  194.1 2.7 %all-to-all-done.4.after_ref = f32[32,16,96]{2,1,0:T(8,128)S(1)} async-done(((f32[32,16,96]{2,1,0:T(8,128)}), f32[32,16,96]{2,1,0:T(8,128)S(1)}, u32[]{:S(2)}, u32[]{:S(2)}) %all-to-all-start.4) | async-done | bytes 196640 | tf_op jit(solution)/shard_map/all_to_all | solution.py:1140
  200.2 1.3 collective-permute-start.26
  201.6 2.2 collective-permute-done.22
  207.2 4.1 %all-to-all-start.5 = ((bf16[32,24,256]{2,1,0:T(8,128)(2,1)}), bf16[32,24,256]{2,1,0:T(8,128)(2,1)S(1)}, u32[]{:S(2)}, u32[]{:S(2)}) async-start(bf16[32,24,256]{2,1,0:T(8,128)(2,1)} %bitcast.36), calls=%async_computation.5 | async-start | bytes 786432 | tf_op jit(solution)/shard_map/all_to_all | solution.py:1140
  213.2 1.5 collective-permute-done.23
  217.1 7.4 %all-to-all-done.5 = bf16[32,24,256]{2,1,0:T(8,128)(2,1)S(1)} async-done(((bf16[32,24,256]{2,1,0:T(8,128)(2,1)}), bf16[32,24,256]{2,1,0:T(8,128)(2,1)S(1)}, u32[]{:S(2)}, u32[]{:S(2)}) %all-to-all-start.5) | async-done | bytes 393248 | tf_op jit(solution)/shard_map/all_to_all | solution.py:1140
  (138 shorter events, 31.4 us)
Async XLA Ops:
  0.6 22.5 %copy-start = (s32[768]{0:T(1024)S(1)}, s32[768]{0:T(1024)}, u32[]{:S(2)}) copy-start(s32[768]{0:T(1024)} %param.23) | copy-start | bytes 9220
  7.2 22.1 %all-to-all-start = ((bf16[8,96,768]{2,1,0:T(8,128)(2,1)}), bf16[8,96,768]{2,1,0:T(8,128)(2,1)}, u32[]{:S(2)}, u32[]{:S(2)}) async-start(bf16[8,96,768]{2,1,0:T(8,128)(2,1)} %bitcast.91), calls=%async_computation | async-start | bytes 2359296 | tf_op jit(solution)/shard_map/all_to_all | solution.py:1180
  12.4 13.0 %collective-permute-start.1 = (bf16[512,768]{1,0:T(8,128)(2,1)}, bf16[512,768]{1,0:T(8,128)(2,1)}, u32[]{:S(2)}, u32[]{:S(2)}) collective-permute-start(bf16[512,768]{1,0:T(8,128)(2,1)} %get-tuple-element.68.refs_11_), channel_id=1, source_target_pairs={{0,1},{1,0},{2,3},{3,2},{4,5},{5,4},{6,7},{7,6},{8,9},{9,8},{10,11... | collective-permute-start | bytes 2359304 | tf_op jit(solution)/shard_map/ppermute | solution.py:1035
  19.8 4.1 %copy-start.20 = (f32[96]{0:T(128)S(1)}, f32[96]{0:T(128)}, u32[]{:S(2)}) copy-start(f32[96]{0:T(128)} %param.29) | copy-start | bytes 1156
  19.8 5.6 %collective-permute-start = (bf16[384,512]{1,0:T(8,128)(2,1)}, bf16[384,512]{1,0:T(8,128)(2,1)S(1)}, u32[]{:S(2)}, u32[]{:S(2)}) collective-permute-start(bf16[384,512]{1,0:T(8,128)(2,1)} %get-tuple-element.67), channel_id=1, source_target_pairs={{0,1},{1,0},{2,3},{3,2},{4,5},{5,4},{6,7},{7,6},{8,9},{9,8},{10,11... | collective-permute-start | bytes 1179656 | tf_op jit(solution)/shard_map/ppermute | solution.py:1035
  25.4 3.9 %copy-start.22 = (bf16[384,512]{1,0:T(8,128)(2,1)}, bf16[384,512]{1,0:T(8,128)(2,1)S(1)}, u32[]{:S(2)}) copy-start(bf16[384,512]{1,0:T(8,128)(2,1)S(1)} %collective-permute-done.refs_9_) | copy-start | bytes 1179652
  35.8 4.0 %copy-start.15 = (f32[768]{0:T(1024)S(1)}, f32[768]{0:T(1024)}, u32[]{:S(2)}) copy-start(f32[768]{0:T(1024)} %refs_2_.1) | copy-start | bytes 9220
  35.8 4.6 %copy-start.16 = (f32[768]{0:T(1024)S(1)}, f32[768]{0:T(1024)}, u32[]{:S(2)}) copy-start(f32[768]{0:T(1024)} %param.31) | copy-start | bytes 9220
  35.8 5.1 %copy-start.17 = (f32[768]{0:T(1024)S(1)}, f32[768]{0:T(1024)}, u32[]{:S(2)}) copy-start(f32[768]{0:T(1024)} %param.32) | copy-start | bytes 9220
  35.8 5.7 %copy-start.18 = (f32[768]{0:T(1024)S(1)}, f32[768]{0:T(1024)}, u32[]{:S(2)}) copy-start(f32[768]{0:T(1024)} %param.33) | copy-start | bytes 9220
  35.8 6.3 %copy-start.19 = (f32[768]{0:T(1024)S(1)}, f32[768]{0:T(1024)}, u32[]{:S(2)}) copy-start(f32[768]{0:T(1024)} %param.37) | copy-start | bytes 9220
  35.8 16.7 %all-to-all-start.1 = ((bf16[8,96,512]{2,1,0:T(8,128)(2,1)}), bf16[8,96,512]{2,1,0:T(8,128)(2,1)S(1)}, u32[]{:S(2)}, u32[]{:S(2)}) async-start(bf16[8,96,512]{2,1,0:T(8,128)(2,1)} %get-tuple-element.69), calls=%async_computation.1 | async-start | bytes 1572864 | tf_op jit(solution)/shard_map/all_to_all | solution.py:1186
  42.7 42.1 %collective-permute-start.3 = (bf16[512,768]{1,0:T(8,128)(2,1)}, bf16[512,768]{1,0:T(8,128)(2,1)}, u32[]{:S(2)}, u32[]{:S(2)}) collective-permute-start(bf16[512,768]{1,0:T(8,128)(2,1)} %get-tuple-element.78.refs_3_.refs_4_), channel_id=1, source_target_pairs={{0,2},{1,3},{2,0},{3,1},{4,6},{5,7},{6,4},{7,5},{8,10},{9,11},{10,... | collective-permute-start | bytes 2359304 | tf_op jit(solution)/shard_map/ppermute | solution.py:1035
  44.4 40.4 %collective-permute-start.4 = (bf16[512,768]{1,0:T(8,128)(2,1)}, bf16[512,768]{1,0:T(8,128)(2,1)}, u32[]{:S(2)}, u32[]{:S(2)}) collective-permute-start(bf16[512,768]{1,0:T(8,128)(2,1)} %get-tuple-element.78.refs_3_.refs_4_), channel_id=1, source_target_pairs={{0,4},{1,5},{2,6},{3,7},{4,0},{5,1},{6,2},{7,3},{8,12},{9,13},{10,... | collective-permute-start | bytes 2359304 | tf_op jit(solution)/shard_map/ppermute | solution.py:1035
  45.9 40.5 %collective-permute-start.5 = (bf16[512,768]{1,0:T(8,128)(2,1)}, bf16[512,768]{1,0:T(8,128)(2,1)}, u32[]{:S(2)}, u32[]{:S(2)}) collective-permute-start(bf16[512,768]{1,0:T(8,128)(2,1)} %get-tuple-element.78.refs_3_.refs_4_), channel_id=1, source_target_pairs={{0,6},{1,7},{2,4},{3,5},{4,2},{5,3},{6,0},{7,1},{8,14},{9,15},{10,... | collective-permute-start | bytes 2359304 | tf_op jit(solution)/shard_map/ppermute | solution.py:1035
  72.8 13.6 %collective-permute-start.2 = (bf16[512,6144]{1,0:T(8,128)(2,1)}, bf16[512,6144]{1,0:T(8,128)(2,1)}, u32[]{:S(2)}, u32[]{:S(2)}) collective-permute-start(bf16[512,6144]{1,0:T(8,128)(2,1)} %get-tuple-element.71.refs_0_.refs_1_.refs_2_), channel_id=1, source_target_pairs={{0,1},{1,0},{2,3},{3,2},{4,5},{5,4},{6,7},{7,6},{8,9},{9,8},{10,11... | collective-permute-start | bytes 18874376 | tf_op jit(solution)/shard_map/ppermute | solution.py:1035
  72.9 31.5 %all-to-all-start.2 = ((bf16[8,96,512]{2,1,0:T(8,128)(2,1)}), bf16[8,96,512]{2,1,0:T(8,128)(2,1)}, u32[]{:S(2)}, u32[]{:S(2)}) async-start(bf16[8,96,512]{2,1,0:T(8,128)(2,1)} %bitcast.93), calls=%async_computation.2 | async-start | bytes 1572864 | tf_op jit(solution)/shard_map/all_to_all | solution.py:1196
  77.1 37.3 %collective-permute-start.9 = (bf16[768,512]{1,0:T(8,128)(2,1)}, bf16[768,512]{1,0:T(8,128)(2,1)}, u32[]{:S(2)}, u32[]{:S(2)}) collective-permute-start(bf16[768,512]{1,0:T(8,128)(2,1)} %get-tuple-element.90), channel_id=1, source_target_pairs={{0,1},{1,0},{2,3},{3,2},{4,5},{5,4},{6,7},{7,6},{8,9},{9,8},{10,11... | collective-permute-start | bytes 2359304 | tf_op jit(solution)/shard_map/ppermute | solution.py:1035
  93.5 26.2 %collective-permute-start.6 = (bf16[512,768]{1,0:T(8,128)(2,1)}, bf16[512,768]{1,0:T(8,128)(2,1)}, u32[]{:S(2)}, u32[]{:S(2)}) collective-permute-start(bf16[512,768]{1,0:T(8,128)(2,1)} %get-tuple-element.86.refs_6_), channel_id=1, source_target_pairs={{0,1},{1,0},{2,3},{3,2},{4,5},{5,4},{6,7},{7,6},{8,9},{9,8},{10,11... | collective-permute-start | bytes 2359304 | tf_op jit(solution)/shard_map/ppermute | solution.py:1035
  93.5 28.0 %collective-permute-start.7 = (bf16[512,768]{1,0:T(8,128)(2,1)}, bf16[512,768]{1,0:T(8,128)(2,1)}, u32[]{:S(2)}, u32[]{:S(2)}) collective-permute-start(bf16[512,768]{1,0:T(8,128)(2,1)} %get-tuple-element.87.refs_8_), channel_id=1, source_target_pairs={{0,1},{1,0},{2,3},{3,2},{4,5},{5,4},{6,7},{7,6},{8,9},{9,8},{10,11... | collective-permute-start | bytes 2359304 | tf_op jit(solution)/shard_map/ppermute | solution.py:1035
  94.0 36.7 %collective-permute-start.10 = (bf16[2,4,96,768]{3,2,1,0:T(8,128)(2,1)}, bf16[2,4,96,768]{3,2,1,0:T(8,128)(2,1)}, u32[]{:S(2)}, u32[]{:S(2)}) collective-permute-start(bf16[2,4,96,768]{3,2,1,0:T(8,128)(2,1)} %get-tuple-element.79.refs_6_), channel_id=1, source_target_pairs={{0,8},{8,0},{16,24},{24,16},{1,9},{9,1},{17,25},{25,17},{2,10},{10... | collective-permute-start | bytes 3538952 | tf_op jit(solution)/shard_map/ppermute | solution.py:1040
  103.9 46.7 %collective-permute-start.12 = (bf16[2,768,384]{2,1,0:T(8,128)(2,1)}, bf16[2,768,384]{2,1,0:T(8,128)(2,1)}, u32[]{:S(2)}, u32[]{:S(2)}) collective-permute-start(bf16[2,768,384]{2,1,0:T(8,128)(2,1)} %get-tuple-element.80.refs_5_), channel_id=1, source_target_pairs={{0,4},{1,5},{2,6},{3,7},{4,0},{5,1},{6,2},{7,3},{8,12},{9,13},{10,... | collective-permute-start | bytes 3538952 | tf_op jit(solution)/shard_map/ppermute | solution.py:1040
  110.0 57.2 %all-to-all-start.3 = ((bf16[8,96,512]{2,1,0:T(8,128)(2,1)}), bf16[8,96,512]{2,1,0:T(8,128)(2,1)}, u32[]{:S(2)}, u32[]{:S(2)}) async-start(bf16[8,96,512]{2,1,0:T(8,128)(2,1)} %conv_adjoint.1.refs_8_.refs_3_), calls=%async_computation.3 | async-start | bytes 1572864 | tf_op jit(solution)/shard_map/all_to_all | solution.py:1220
  114.5 7.0 %collective-permute-start.8 = (bf16[512,768]{1,0:T(8,128)(2,1)}, bf16[512,768]{1,0:T(8,128)(2,1)S(1)}, u32[]{:S(2)}, u32[]{:S(2)}) collective-permute-start(bf16[512,768]{1,0:T(8,128)(2,1)} %get-tuple-element.88.refs_10_), channel_id=1, source_target_pairs={{0,1},{1,0},{2,3},{3,2},{4,5},{5,4},{6,7},{7,6},{8,9},{9,8},{10,11... | collective-permute-start | bytes 2359304 | tf_op jit(solution)/shard_map/ppermute | solution.py:1035
  119.8 18.8 %collective-permute-start.11 = (bf16[2,192,768]{2,1,0:T(8,128)(2,1)}, bf16[2,192,768]{2,1,0:T(8,128)(2,1)}, u32[]{:S(2)}, u32[]{:S(2)}) collective-permute-start(bf16[2,192,768]{2,1,0:T(8,128)(2,1)} %get-tuple-element.91.refs_12_), channel_id=1, source_target_pairs={{0,2},{1,3},{2,0},{3,1},{4,6},{5,7},{6,4},{7,5},{8,10},{9,11},{10,... | collective-permute-start | bytes 1769480 | tf_op jit(solution)/shard_map/ppermute | solution.py:1040
  133.6 29.1 %collective-permute-start.14 = (bf16[1,4,96,768]{3,2,1,0:T(8,128)(2,1)}, bf16[1,4,96,768]{3,2,1,0:T(8,128)(2,1)}, u32[]{:S(2)}, u32[]{:S(2)}) collective-permute-start(bf16[1,4,96,768]{3,2,1,0:T(8,128)(2,1)} %get-tuple-element.119.after_ref), channel_id=1, source_target_pairs={{0,16},{8,24},{16,0},{24,8},{1,17},{9,25},{17,1},{25,9},{2,18},{10... | collective-permute-start | bytes 1769480 | tf_op jit(solution)/shard_map/ppermute | solution.py:1040
  140.8 13.3 %collective-permute-start.13 = (bf16[1,192,768]{2,1,0:T(8,128)(2,1)}, bf16[1,192,768]{2,1,0:T(8,128)(2,1)}, u32[]{:S(2)}, u32[]{:S(2)}) collective-permute-start(bf16[1,192,768]{2,1,0:T(8,128)(2,1)} %get-tuple-element.123.refs_6_), channel_id=1, source_target_pairs={{0,4},{1,5},{2,6},{3,7},{4,0},{5,1},{6,2},{7,3},{8,12},{9,13},{10,... | collective-permute-start | bytes 884744 | tf_op jit(solution)/shard_map/ppermute | solution.py:1040
  150.6 33.8 %collective-permute-start.19 = (bf16[2,192,256]{2,1,0:T(8,128)(2,1)}, bf16[2,192,256]{2,1,0:T(8,128)(2,1)}, u32[]{:S(2)}, u32[]{:S(2)}) collective-permute-start(bf16[2,192,256]{2,1,0:T(8,128)(2,1)} %get-tuple-element.132.after_ref), channel_id=1, source_target_pairs={{0,8},{8,0},{16,24},{24,16},{1,9},{9,1},{17,25},{25,17},{2,10},{10... | collective-permute-start | bytes 589832 | tf_op jit(solution)/shard_map/ppermute | solution.py:1040
  153.5 21.1 %collective-permute-start.15 = (bf16[1,768,384]{2,1,0:T(8,128)(2,1)}, bf16[1,768,384]{2,1,0:T(8,128)(2,1)}, u32[]{:S(2)}, u32[]{:S(2)}) collective-permute-start(bf16[1,768,384]{2,1,0:T(8,128)(2,1)} %get-tuple-element.117.after_ref), channel_id=1, source_target_pairs={{0,2},{1,3},{2,0},{3,1},{4,6},{5,7},{6,4},{7,5},{8,10},{9,11},{10,... | collective-permute-start | bytes 1769480 | tf_op jit(solution)/shard_map/ppermute | solution.py:1040
  154.0 1.9 copy-start.14
  156.7 31.2 %collective-permute-start.16 = (bf16[96,768]{1,0:T(8,128)(2,1)}, bf16[96,768]{1,0:T(8,128)(2,1)}, u32[]{:S(2)}, u32[]{:S(2)}) collective-permute-start(bf16[96,768]{1,0:T(8,128)(2,1)} %get-tuple-element.130.after_ref.refs_8_), channel_id=1, source_target_pairs={{0,0},{3,1},{6,2},{1,3},{4,4},{7,5},{2,6},{5,7},{8,8},{11,9},{14,1... | collective-permute-start | bytes 442376 | tf_op jit(solution)/shard_map/ppermute | solution.py:1247
  159.5 30.8 %collective-permute-start.17 = (bf16[96,768]{1,0:T(8,128)(2,1)}, bf16[96,768]{1,0:T(8,128)(2,1)}, u32[]{:S(2)}, u32[]{:S(2)}) collective-permute-start(bf16[96,768]{1,0:T(8,128)(2,1)} %get-tuple-element.129.refs_9_), channel_id=1, source_target_pairs={{1,0},{4,1},{7,2},{2,3},{5,4},{0,5},{3,6},{6,7},{9,8},{12,9},{15,1... | collective-permute-start | bytes 442376 | tf_op jit(solution)/shard_map/ppermute | solution.py:1247
  162.7 27.6 %collective-permute-start.18 = (bf16[96,768]{1,0:T(8,128)(2,1)}, bf16[96,768]{1,0:T(8,128)(2,1)}, u32[]{:S(2)}, u32[]{:S(2)}) collective-permute-start(bf16[96,768]{1,0:T(8,128)(2,1)} %get-tuple-element.128.refs_10_), channel_id=1, source_target_pairs={{2,0},{5,1},{0,2},{3,3},{6,4},{1,5},{4,6},{7,7},{10,8},{13,9},{8,1... | collective-permute-start | bytes 442376 | tf_op jit(solution)/shard_map/ppermute | solution.py:1247
  176.0 8.3 %copy-start.13 = (bf16[2,96,768]{2,1,0:T(8,128)(2,1)S(1)}, bf16[2,96,768]{2,1,0:T(8,128)(2,1)}, u32[]{:S(2)}) copy-start(bf16[2,96,768]{2,1,0:T(8,128)(2,1)} %get-tuple-element.121.refs_11_) | copy-start | bytes 884740
  176.8 20.7 %collective-permute-start.20 = (bf16[2,192,384]{2,1,0:T(8,128)(2,1)S(1)}, bf16[2,192,384]{2,1,0:T(8,128)(2,1)S(1)}, u32[]{:S(2)}, u32[]{:S(2)}) collective-permute-start(bf16[2,192,384]{2,1,0:T(8,128)(2,1)S(1)} %get-tuple-element.127.refs_5_), channel_id=1, source_target_pairs={{0,8},{8,0},{16,24},{24,16},{1,9},{9,1},{17,25},{25,17},{2,10},{10... | collective-permute-start | bytes 884744 | tf_op jit(solution)/shard_map/ppermute | solution.py:1040
  179.4 17.4 %all-to-all-start.4 = ((f32[32,16,96]{2,1,0:T(8,128)}), f32[32,16,96]{2,1,0:T(8,128)S(1)}, u32[]{:S(2)}, u32[]{:S(2)}) async-start(f32[32,16,96]{2,1,0:T(8,128)} %bitcast.97), calls=%async_computation.4 | async-start | bytes 524288 | tf_op jit(solution)/shard_map/all_to_all | solution.py:1140
  184.3 14.9 %collective-permute-start.21 = (bf16[2,96,768]{2,1,0:T(8,128)(2,1)S(1)}, bf16[2,96,768]{2,1,0:T(8,128)(2,1)S(1)}, u32[]{:S(2)}, u32[]{:S(2)}) collective-permute-start(bf16[2,96,768]{2,1,0:T(8,128)(2,1)S(1)} %copy-done.13), channel_id=1, source_target_pairs={{0,2},{1,3},{2,0},{3,1},{4,6},{5,7},{6,4},{7,5},{8,10},{9,11},{10,... | collective-permute-start | bytes 884744 | tf_op jit(solution)/shard_map/ppermute | solution.py:1040
  187.9 17.6 %collective-permute-start.24 = (bf16[1,192,256]{2,1,0:T(8,128)(2,1)}, bf16[1,192,256]{2,1,0:T(8,128)(2,1)S(1)}, u32[]{:S(2)}, u32[]{:S(2)}) collective-permute-start(bf16[1,192,256]{2,1,0:T(8,128)(2,1)} %get-tuple-element.136.after_ref), channel_id=1, source_target_pairs={{0,16},{8,24},{16,0},{24,8},{1,17},{9,25},{17,1},{25,9},{2,18},{10... | collective-permute-start | bytes 294920 | tf_op jit(solution)/shard_map/ppermute | solution.py:1040
  192.6 1.5 copy-start.5
  192.6 11.1 %collective-permute-start.22 = (bf16[2,192,384]{2,1,0:T(8,128)(2,1)S(1)}, bf16[2,192,384]{2,1,0:T(8,128)(2,1)S(1)}, u32[]{:S(2)}, u32[]{:S(2)}) collective-permute-start(bf16[2,192,384]{2,1,0:T(8,128)(2,1)S(1)} %get-tuple-element.125.after_ref), channel_id=1, source_target_pairs={{0,8},{8,0},{16,24},{24,16},{1,9},{9,1},{17,25},{25,17},{2,10},{10... | collective-permute-start | bytes 884744 | tf_op jit(solution)/shard_map/ppermute | solution.py:1040
  198.6 17.0 %collective-permute-start.25 = (bf16[1,192,384]{2,1,0:T(8,128)(2,1)S(1)}, bf16[1,192,384]{2,1,0:T(8,128)(2,1)S(1)}, u32[]{:S(2)}, u32[]{:S(2)}) collective-permute-start(bf16[1,192,384]{2,1,0:T(8,128)(2,1)S(1)} %constant_dynamic-slice_fusion.2.after_ref), channel_id=1, source_target_pairs={{0,16},{8,24},{16,0},{24,8},{1,17},{9,25},{17,1},{25,9},{2,18},{10... | collective-permute-start | bytes 442376 | tf_op jit(solution)/shard_map/ppermute | solution.py:1040
  200.2 16.1 %collective-permute-start.26 = (bf16[1,96,768]{2,1,0:T(8,128)(2,1)S(1)}, bf16[1,96,768]{2,1,0:T(8,128)(2,1)S(1)}, u32[]{:S(2)}, u32[]{:S(2)}) collective-permute-start(bf16[1,96,768]{2,1,0:T(8,128)(2,1)S(1)} %add_convert_fusion.14.after_ref), channel_id=1, source_target_pairs={{0,4},{1,5},{2,6},{3,7},{4,0},{5,1},{6,2},{7,3},{8,12},{9,13},{10,... | collective-permute-start | bytes 442376 | tf_op jit(solution)/shard_map/ppermute | solution.py:1040
  204.8 6.5 %copy-start.4 = (f32[32,16,96]{2,1,0:T(8,128)S(1)}, f32[32,16,96]{2,1,0:T(8,128)}, u32[]{:S(2)}) copy-start(f32[32,16,96]{2,1,0:T(8,128)} %copy-done.3) | copy-start | bytes 589828
  204.8 9.9 %collective-permute-start.23 = (bf16[1,192,384]{2,1,0:T(8,128)(2,1)S(1)}, bf16[1,192,384]{2,1,0:T(8,128)(2,1)S(1)}, u32[]{:S(2)}, u32[]{:S(2)}) collective-permute-start(bf16[1,192,384]{2,1,0:T(8,128)(2,1)S(1)} %constant_dynamic-slice_fusion.1.after_ref), channel_id=1, source_target_pairs={{0,16},{8,24},{16,0},{24,8},{1,17},{9,25},{17,1},{25,9},{2,18},{10... | collective-permute-start | bytes 442376 | tf_op jit(solution)/shard_map/ppermute | solution.py:1040
  207.2 9.1 %copy-start.2 = (bf16[2,96,768]{2,1,0:T(8,128)(2,1)S(1)}, bf16[2,96,768]{2,1,0:T(8,128)(2,1)}, u32[]{:S(2)}) copy-start(bf16[2,96,768]{2,1,0:T(8,128)(2,1)} %gate.17) | copy-start | bytes 884740
  207.2 17.3 %all-to-all-start.5 = ((bf16[32,24,256]{2,1,0:T(8,128)(2,1)}), bf16[32,24,256]{2,1,0:T(8,128)(2,1)S(1)}, u32[]{:S(2)}, u32[]{:S(2)}) async-start(bf16[32,24,256]{2,1,0:T(8,128)(2,1)} %bitcast.36), calls=%async_computation.5 | async-start | bytes 786432 | tf_op jit(solution)/shard_map/all_to_all | solution.py:1140
  214.8 9.8 %copy-start.12 = (f32[192,384]{1,0:T(8,128)}, f32[192,384]{1,0:T(8,128)S(1)}, u32[]{:S(2)}) copy-start(f32[192,384]{1,0:T(8,128)S(1)} %add_bitcast_fusion.2) | copy-start | bytes 884740
  217.1 7.6 %copy-start.8 = (f32[768,256]{1,0:T(8,128)S(1)}, f32[768,256]{1,0:T(8,128)}, u32[]{:S(2)}) copy-start(f32[768,256]{1,0:T(8,128)} %refs_8_.1) | copy-start | bytes 2359300
  (8 other events, 6.9 us)
